TPU v7x, 256 devices: a whole 4x4x8 slice. The times are simulated.
256 devices in a mesh: tm: 8 (over y, core), seq: 32 (over x, z).
Axes of the slice: x: 4, y: 4, z: 8, core: 2. Of those that a mesh axis runs over, the one named last changes fastest.
Arguments:
- queries: bfloat16 [65536, 4096], P(('tm', 'seq')), may hold values from -9 to 9
- keys_values: bfloat16 [2, 65536, 4096], P(None, ('tm', 'seq')), may hold values from -6 to 6
- extents: int32 [3, 32], replicated, may hold values from 0 to 2
- tile_lists: int32 [512, 16], P('tm'), may hold values from 0 to 511, as said below
Outputs:
- attended: bfloat16 [65536, 4096], P(('tm', 'seq'))
Inputs may be any that keep to these rules, and one draw needn't show every extreme that they name: `tile_lists`: slot 0 of row g is g itself; the other 15 entries of a row are different tiles of g's window, 3 tiles along each of time, height and width, centred on g and moved inward at the grid's edges.
All inputs are finite; a program needn't handle non-finite values.
Results may differ from a plain program's by a relative error of at most 0.0065.
Values may be sent and summed in bfloat16 or wider, within the bound.
No kernel may reach another device: no remote copies, remote signals or barrier semaphores. Data moves between devices by JAX's collectives and lax.ppermute only.
A program may use at most 128 MiB of HBM per device.

v0:
```python
import jax
import jax.numpy as jnp
from jax import lax
from jax.sharding import PartitionSpec as P

HEAD_DIM = 128
TILE = 128
GH = 4
GW = 8


def with_halo(cells, sides, width):
    for axis, dim in sides:
        count = lax.axis_size(axis)
        ends = count - 1
        head = lax.slice_in_dim(cells, 0, width, axis=dim)
        tail = lax.slice_in_dim(cells, cells.shape[dim] - width, cells.shape[dim], axis=dim)
        cells = jnp.concatenate(
            [
                lax.ppermute(tail, axis, [(i, (i + 1) % count) for i in range(ends)]),
                cells,
                lax.ppermute(head, axis, [((i + 1) % count, i) for i in range(ends)]),
            ],
            axis=dim,
        )
    return cells


def tile_place(tile_ids):
    return (tile_ids // (GH * GW), tile_ids // GW % GH, tile_ids % GW)


def divisor_below(amount, limit_size):
    best_size = 1
    for candidate in range(1, min(amount, limit_size) + 1):
        if amount % candidate == 0:
            best_size = candidate
    return best_size


def listed_attention(query_tiles, key_tiles, value_tiles, local_lists, live_slots):
    tile_count, tile_size, head_dim = query_tiles.shape
    score_scale = head_dim ** (-0.5)
    group_size = divisor_below(tile_count, max(1, 512 // tile_size))
    groups = tile_count // group_size

    def one_group(inputs):
        queries_block, lists_block, live_block = inputs
        gathered_keys = jnp.take(key_tiles, lists_block, axis=0)
        gathered_values = jnp.take(value_tiles, lists_block, axis=0)
        scores = (
            jnp.einsum(
                "bid,bkjd->bikj", queries_block, gathered_keys, preferred_element_type=jnp.float32
            )
            * score_scale
        )
        alive_grid = live_block[:, None, :, None]
        block_top = jnp.max(jnp.where(alive_grid, scores, -jnp.inf), axis=(2, 3), keepdims=True)
        weights = jnp.where(alive_grid, jnp.exp(scores - block_top), 0.0)
        totals = jnp.sum(weights, axis=(2, 3))
        mixed = jnp.einsum(
            "bikj,bkjd->bid",
            weights.astype(jnp.bfloat16),
            gathered_values,
            preferred_element_type=jnp.float32,
        )
        return (mixed / totals[..., None]).astype(jnp.bfloat16)

    outputs = lax.map(
        one_group,
        (
            query_tiles.reshape(groups, group_size, tile_size, head_dim),
            local_lists.reshape(groups, group_size, -1),
            live_slots.reshape(groups, group_size, -1),
        ),
    )
    return outputs.reshape(tile_count * tile_size, head_dim)


def per_device(queries, keys_values, extents, tile_lists):
    seq_size = lax.axis_size("seq")
    tok_dev, width_all = queries.shape
    slab_tok = tok_dev * seq_size
    frame_tok = GH * GW * TILE
    widened = with_halo(keys_values, (("tm", 1),), tok_dev)
    stacked = widened.reshape(2, 3, tok_dev, width_all)
    head_queries, head_pairs = (
        lax.all_to_all(
            queries.reshape(1, 1, tok_dev, width_all),
            "seq",
            split_axis=3,
            concat_axis=2,
            tiled=True,
        ),
        lax.all_to_all(stacked, "seq", split_axis=3, concat_axis=2, tiled=True),
    )
    head_queries = head_queries[0, 0]
    extended = jnp.concatenate(
        [head_pairs[:, 0, slab_tok - frame_tok :], head_pairs[:, 1], head_pairs[:, 2, :frame_tok]],
        axis=1,
    )
    slab_tiles = slab_tok // TILE
    first_tile = lax.axis_index("tm") * slab_tiles
    query_ids = first_tile + jnp.arange(slab_tiles, dtype=jnp.int32)
    local_lists = tile_lists - (first_tile - GH * GW)
    query_time, query_row, query_column = tile_place(query_ids)
    listed_time, listed_row, listed_column = tile_place(tile_lists)
    heads_here = head_queries.shape[1] // HEAD_DIM
    head_ids = jnp.arange(extents.shape[1], dtype=jnp.int32)
    head_index = lax.axis_index("seq") * heads_here + 0
    select = (head_ids == head_index).astype(jnp.int32)
    reaches = jnp.sum(extents * select[None, :], axis=1)
    live_slots = (
        (jnp.abs(listed_time - query_time[:, None]) <= reaches[0])
        & (jnp.abs(listed_row - query_row[:, None]) <= reaches[1])
        & (jnp.abs(listed_column - query_column[:, None]) <= reaches[2])
    )
    query_tiles = head_queries.reshape(slab_tiles, TILE, HEAD_DIM)
    key_tiles = extended[0, :, 0:HEAD_DIM].reshape(-1, TILE, HEAD_DIM)
    value_tiles = extended[1, :, 0:HEAD_DIM].reshape(-1, TILE, HEAD_DIM)
    head_output = listed_attention(query_tiles, key_tiles, value_tiles, local_lists, live_slots)
    return lax.all_to_all(head_output, "seq", split_axis=0, concat_axis=1, tiled=True)


def solution(mesh):
    placed = (P(("tm", "seq"), None), P(None, ("tm", "seq"), None), P(), P("tm", None))
    return jax.shard_map(
        per_device, mesh=mesh, in_specs=placed, out_specs=P(("tm", "seq"), None), check_vma=False
    )
```

profile of v0, /device:TPU:8, one launch (start us, length us, event | category | flops | bytes accessed | tf_op | source)
XLA Modules:
  0.0 821.8 jit_solution(10980937386050734659)
XLA Ops:
  5.6 10.0 %copy.38 = bf16[1,1,256,4096]{2,1,0,3:T(2,128)(2,1)} copy(bf16[1,1,256,4096]{3,2,1,0:T(8,128)(2,1)} %bitcast.86) | data formatting | bytes 4194304 | tf_op jit(solution)/shard_map/reshape | solution.py:89
  16.1 21.6 %reduce = bf16[4096,256]{1,0:T(8,128)(2,1)S(1)} reduce(bf16[4096,1,1,256]{3,2,1,0:T(2,128)(2,1)} %bitcast.82, bf16[]{:T(256)} %broadcast.193), dimensions={1,2}, to_apply=%bitcast.55.reduce_sub_computation | reduce | bytes 4194306
  39.7 11.3 %all-to-all-start = ((bf16[32,2,16384]{2,1,0:T(2,128)(2,1)}), bf16[32,2,16384]{2,1,0:T(2,128)(2,1)S(1)}, u32[]{:S(2)}, u32[]{:S(2)}) async-start(bf16[32,2,16384]{2,1,0:T(2,128)(2,1)} %reshape.121), calls=%async_computation | async-start | bytes 4194304 | tf_op jit(solution)/shard_map/all_to_all | solution.py:88
  51.9 10.5 %pad_maximum_fusion = bf16[2,768,4096]{2,1,0:T(8,128)(2,1)} fusion(bf16[2,256,4096]{2,1,0:T(8,128)(2,1)} %collective-permute-done.1, bf16[2,256,4096]{2,1,0:T(8,128)(2,1)} %param.9, bf16[2,256,4096]{2,1,0:T(8,128)(2,1)} %collective-permute-done), kind=kLoop, calls=%fused_computation.34 | loop fusion | flops 37748736 | bytes 25165824 | tf_op jit(solution)/shard_map/concatenate | solution.py:18
  62.4 31.4 %copy.41 = bf16[2,3,256,4096]{2,0,1,3:T(2,128)(2,1)} copy(bf16[2,3,256,4096]{3,2,1,0:T(8,128)(2,1)} %bitcast.78) | data formatting | bytes 25165824 | tf_op jit(solution)/shard_map/reshape | solution.py:86
  93.7 7.5 all-to-all-done
  101.2 6.2 all-to-all-start.1
  110.3 6.8 reshape.122
  122.6 265.7 %all-to-all-done.1 = bf16[2,3,256,4096]{2,0,1,3:T(2,128)(2,1)} async-done(((bf16[2,3,256,4096]{2,0,1,3:T(2,128)(2,1)}), bf16[2,3,256,4096]{2,0,1,3:T(2,128)(2,1)}, u32[]{:S(2)}, u32[]{:S(2)}) %all-to-all-start.1) | async-done | bytes 12582944 | tf_op jit(solution)/shard_map/all_to_all | solution.py:95
  388.2 11.7 %copy.42 = bf16[2,3,256,4096]{2,3,1,0:T(8,128)(2,1)} copy(bf16[2,3,256,4096]{2,0,1,3:T(2,128)(2,1)} %all-to-all-done.1) | data formatting | bytes 25165824 | tf_op jit(solution)/shard_map/all_to_all | solution.py:95
  400.0 16.7 %copy.43 = bf16[2,3,32,256,128]{4,3,2,1,0:T(8,128)(2,1)} copy(bf16[2,3,32,256,128]{3,4,2,1,0:T(8,128)(2,1)} %bitcast.72) | data formatting | bytes 25165824 | tf_op jit(solution)/shard_map/all_to_all | solution.py:95
  416.6 4.4 slice_bitcast_fusion
  422.8 16.7 %copy.50 = bf16[2,3,32,256,128]{4,3,2,0,1:T(8,128)(2,1)} copy(bf16[2,3,32,256,128]{3,4,2,1,0:T(8,128)(2,1)} %bitcast.73) | data formatting | bytes 25165824 | tf_op jit(solution)/shard_map/all_to_all | solution.py:95
  442.3 38.4 %pad_maximum_fusion.1 = bf16[2,16384,128]{2,1,0:T(8,128)(2,1)S(1)} fusion(bf16[2,4096,128]{2,1,0:T(8,128)(2,1)S(1)} %slice_bitcast_fusion.1, bf16[2,8192,128]{2,1,0:T(8,128)(2,1)S(1)} %copy-done.1, bf16[2,4096,128]{2,1,0:T(8,128)(2,1)S(1)} %slice_bitcast_fusion.2), kind=kLoop, calls=%fused_computation.35 | loop fusion | flops 25165824 | bytes 16777216 | tf_op jit(solution)/shard_map/concatenate | solution.py:98
  484.2 249.2 %while.10 = (s32[]{:T(128)}, bf16[16,4,128,128]{3,2,1,0:T(8,128)(2,1)}, pred[16,4,16]{2,1,0:T(4,128)(4,1)S(1)}, bf16[16,4,128,128]{3,2,1,0:T(8,128)(2,1)}, s32[1...) while((s32[]{:T(128)}, ...), condition=%wide.region_4.6_spmd, body=%wide.region_1.5_spmd.sunk | while | flops 550633856 | bytes 42222968 | solution.py:69
  495.4 4.4 fusion.74
  510.9 4.4 fusion.74
  526.5 4.4 fusion.74
  542.1 4.4 fusion.74
  557.7 4.4 fusion.74
  573.2 4.4 fusion.74
  588.8 4.4 fusion.74
  604.4 4.4 fusion.74
  620.0 4.4 fusion.74
  635.5 4.4 fusion.74
  651.1 4.4 fusion.74
  666.7 4.4 fusion.74
  682.3 4.4 fusion.74
  697.8 4.4 fusion.74
  713.4 4.4 fusion.74
  729.0 4.4 fusion.74
  733.3 81.5 %all_to_all.52 = bf16[32,256,128]{2,1,0:T(8,128)(2,1)S(1)} all-to-all(bf16[32,256,128]{2,1,0:T(8,128)(2,1)} %bitcast.87), channel_id=1, replica_groups=mesh['tm'=8,'seq'=32] {'seq'}, dimensions={0} | all-to-all | bytes 4194304 | tf_op jit(solution)/shard_map/all_to_all | solution.py:122
  (189 shorter events, 211.1 us)
Async XLA Ops:
  0.0 51.0 %collective-permute-start = (bf16[2,256,4096]{2,1,0:T(8,128)(2,1)}, bf16[2,256,4096]{2,1,0:T(8,128)(2,1)}, u32[]{:S(2)}, u32[]{:S(2)}) collective-permute-start(bf16[2,256,4096]{2,1,0:T(8,128)(2,1)} %param.9), channel_id=1, source_target_pairs={{0,32},{32,64},{64,96},{96,128},{128,160},{160,192},{192,224},{1,3... | collective-permute-start | bytes 12582920 | tf_op jit(solution)/shard_map/ppermute | solution.py:20
  1.9 50.0 %collective-permute-start.1 = (bf16[2,256,4096]{2,1,0:T(8,128)(2,1)}, bf16[2,256,4096]{2,1,0:T(8,128)(2,1)}, u32[]{:S(2)}, u32[]{:S(2)}) collective-permute-start(bf16[2,256,4096]{2,1,0:T(8,128)(2,1)} %param.9), channel_id=1, source_target_pairs={{32,0},{64,32},{96,64},{128,96},{160,128},{192,160},{224,192},{33,... | collective-permute-start | bytes 12582920 | tf_op jit(solution)/shard_map/ppermute | solution.py:22
  39.7 61.5 %all-to-all-start = ((bf16[32,2,16384]{2,1,0:T(2,128)(2,1)}), bf16[32,2,16384]{2,1,0:T(2,128)(2,1)S(1)}, u32[]{:S(2)}, u32[]{:S(2)}) async-start(bf16[32,2,16384]{2,1,0:T(2,128)(2,1)} %reshape.121), calls=%async_computation | async-start | bytes 4194304 | tf_op jit(solution)/shard_map/all_to_all | solution.py:88
  93.7 13.8 %copy-start.3 = (s32[3,32]{1,0:T(4,128)S(1)}, s32[3,32]{1,0:T(4,128)}, u32[]{:S(2)}) copy-start(s32[3,32]{1,0:T(4,128)} %param.10) | copy-start | bytes 1156
  93.7 14.6 %copy-start.2 = (s32[64,16]{0,1:T(8,128)S(1)}, s32[64,16]{0,1:T(8,128)}, u32[]{:S(2)}) copy-start(s32[64,16]{0,1:T(8,128)} %param.11) | copy-start | bytes 12292
  101.2 287.0 %all-to-all-start.1 = ((bf16[2,3,256,4096]{2,0,1,3:T(2,128)(2,1)}), bf16[2,3,256,4096]{2,0,1,3:T(2,128)(2,1)}, u32[]{:S(2)}, u32[]{:S(2)}) async-start(bf16[2,3,256,4096]{2,0,1,3:T(2,128)(2,1)} %copy.41), calls=%async_computation.1 | async-start | bytes 25165824 | tf_op jit(solution)/shard_map/all_to_all | solution.py:95
  439.5 2.8 copy-start.1
  489.3 1.9 copy-start
  504.8 1.9 copy-start
  520.4 1.9 copy-start
  536.0 1.9 copy-start
  551.5 1.9 copy-start
  567.1 1.9 copy-start
  582.7 1.9 copy-start
  598.3 1.9 copy-start
  613.8 1.9 copy-start
  629.4 1.9 copy-start
  645.0 1.9 copy-start
  660.6 1.9 copy-start
  676.1 1.9 copy-start
  691.7 1.9 copy-start
  707.3 1.9 copy-start
  722.9 1.9 copy-start
where the time goes:
time: 831 us; the launch traced here: 822 us
  waiting for transfers between devices  274 us (33%)
  local copies, waits for them, and re-layouts  254 us (31%)
  matrix products  99 us (12%)
  other arithmetic  89.2 us (11%)
  blocking collectives  81.5 us (10%)
  starting transfers between devices  23.1 us (3%)
    all_to_all x1, waiting for transfers between devices, per_device(): lax.all_to_all(stacked, 'seq', split_axis=3, concat_axis=2, tiled=True)  266 us
    all_to_all x1, blocking collectives, per_device(): lax.all_to_all(head_output, 'seq', split_axis=0, concat_axis=1, tiled=True)  81.5 us
    dot_general x16, matrix products, one_group(): jnp.einsum('bikj,bkjd->bid', weights.astype(jnp.bfloat16), gathered_value...  69.7 us
    gather x16, local copies, waits for them, and re-layouts, one_group(): gathered_keys = jnp.take(key_tiles, lists_block, axis=0)  50.2 us
    gather x16, local copies, waits for them, and re-layouts, one_group(): gathered_values = jnp.take(value_tiles, lists_block, axis=0)  50.2 us
    all_to_all x3, local copies, waits for them, and re-layouts, per_device(): lax.all_to_all(stacked, 'seq', split_axis=3, concat_axis=2, tiled=True)  45.1 us
    concatenate x1, other arithmetic, per_device(): jnp.concatenate([head_pairs[:, 0, slab_tok - frame_tok:], head_pairs[:, 1...  38.4 us
    reshape x1, local copies, waits for them, and re-layouts, per_device(): stacked = widened.reshape(2, 3, tok_dev, width_all)  31.4 us
  transfers between devices with their start and end apart: 4, of which 3 were waited for; matrix products, arithmetic and copies ran while one was open for 11% of the time, Pallas kernels for 0%

commit v1 on v0

v1 whole, which is shorter than its diff:
```python
import functools

import jax
import jax.numpy as jnp
from jax import lax
from jax.experimental import pallas as pl
from jax.experimental.pallas import tpu as pltpu
from jax.sharding import PartitionSpec as P

HEAD_DIM = 128
TILE = 128
GH = 4
GW = 8
FRAME = GH * GW
KSEL = 16
CHUNKS = 2
EXP2_SCALE = HEAD_DIM ** (-0.5) * 1.4426950408889634
DEAD = -1e30


def attend_kernel(chunk, slots_ref, query_ref, left_ref, own_ref, right_ref, out_ref, held, sems):
    step = pl.program_id(0)
    pairs = own_ref.shape[0]
    rim = left_ref.shape[0]

    @pl.when(step == 0)
    def _():
        copies = [
            pltpu.make_async_copy(own_ref, held.at[pl.ds(rim, pairs)], sems.at[0]),
            pltpu.make_async_copy(left_ref, held.at[pl.ds(0, rim)], sems.at[1]),
            pltpu.make_async_copy(right_ref, held.at[pl.ds(rim + pairs, rim)], sems.at[2]),
        ]
        for copy in copies:
            copy.start()
        for copy in copies:
            copy.wait()

    tiles_step = query_ref.shape[0]
    ones = jnp.ones((2 * TILE, HEAD_DIM), jnp.bfloat16)
    for tile in range(tiles_step):
        row = (step * tiles_step + tile) * CHUNKS + chunk
        query = query_ref[tile]
        scores = []
        places = []
        top = None
        for slot in range(0, KSEL, 2):
            codes = [slots_ref[row, slot + i] for i in range(2)]
            tiles = [code & 127 for code in codes]
            bias = [jnp.where(code >= 128, DEAD, 0.0) for code in codes]
            places.append((tiles, bias))
            keys = jnp.concatenate([held[k >> 1, 0, k & 1] for k in tiles], axis=0)
            score = lax.dot_general(
                query, keys, (((1,), (1,)), ((), ())), preferred_element_type=jnp.float32
            )
            score = [score[:, i * TILE : (i + 1) * TILE] + bias[i] for i in range(2)]
            scores.append(score)
            best = jnp.maximum(score[0], score[1])
            top = best if top is None else jnp.maximum(top, best)
        top = jnp.max(top, axis=1, keepdims=True)
        mixed = None
        for score, (tiles, bias) in zip(scores, places):
            weights = jnp.concatenate(
                [jnp.exp2((part - top) * EXP2_SCALE).astype(jnp.bfloat16) for part in score], axis=1
            )
            values = jnp.concatenate([held[k >> 1, 1, k & 1] for k in tiles], axis=0)
            part = jnp.dot(
                weights,
                jnp.concatenate([values, ones], axis=1),
                preferred_element_type=jnp.float32,
            )
            mixed = part if mixed is None else mixed + part
        out_ref[tile] = (mixed[:, :HEAD_DIM] / mixed[:, HEAD_DIM:]).astype(jnp.bfloat16)


def attend(chunk, slots, query_tiles, left, own, right):
    count = query_tiles.shape[0]
    tiles_step = 2
    pairs = own.shape[0]
    whole = pl.BlockSpec(memory_space=pl.ANY)
    return pl.pallas_call(
        functools.partial(attend_kernel, chunk),
        grid=(count // tiles_step,),
        in_specs=[
            pl.BlockSpec(memory_space=pltpu.SMEM),
            pl.BlockSpec((tiles_step, TILE, HEAD_DIM), lambda i: (i, 0, 0)),
            whole,
            whole,
            whole,
        ],
        out_specs=pl.BlockSpec((tiles_step, TILE, HEAD_DIM), lambda i: (i, 0, 0)),
        out_shape=jax.ShapeDtypeStruct((count, TILE, HEAD_DIM), jnp.bfloat16),
        scratch_shapes=[
            pltpu.VMEM((pairs + 2 * left.shape[0],) + own.shape[1:], jnp.bfloat16),
            pltpu.SemaphoreType.DMA((3,)),
        ],
        compiler_params=pltpu.CompilerParams(vmem_limit_bytes=40 * 1024 * 1024),
        cost_estimate=pl.CostEstimate(
            flops=count * KSEL * TILE * TILE * HEAD_DIM * 4,
            bytes_accessed=12 * 1024 * 1024,
            transcendentals=count * KSEL * TILE * TILE,
        ),
    )(slots, query_tiles, left, own, right)


def tile_place(tile_ids):
    return (tile_ids // FRAME, tile_ids // GW % GH, tile_ids % GW)


def slot_codes(extents, tile_lists, head, first_tile):
    reaches = lax.dynamic_slice_in_dim(extents, head, 1, axis=1)[:, 0]
    query_ids = first_tile + jnp.arange(tile_lists.shape[0], dtype=jnp.int32)
    query_time, query_row, query_column = tile_place(query_ids)
    listed_time, listed_row, listed_column = tile_place(tile_lists)
    live = (
        (jnp.abs(listed_time - query_time[:, None]) <= reaches[0])
        & (jnp.abs(listed_row - query_row[:, None]) <= reaches[1])
        & (jnp.abs(listed_column - query_column[:, None]) <= reaches[2])
    )
    local = tile_lists - (first_tile - FRAME)
    return jnp.where(live, local, local + 128)


def exchange(blocks):
    return lax.all_to_all(blocks, "seq", split_axis=0, concat_axis=0, tiled=True)


def per_device(queries, keys_values, extents, tile_lists):
    seq_size = lax.axis_size("seq")
    tm_size = lax.axis_size("tm")
    tok_dev, width_all = queries.shape
    heads = width_all // HEAD_DIM
    slab_tiles = tok_dev * seq_size // TILE
    first_tile = lax.axis_index("tm") * slab_tiles
    head = lax.axis_index("seq")

    pairs_by_head = keys_values.reshape(2, tok_dev, heads, HEAD_DIM).transpose(2, 0, 1, 3)
    own = exchange(pairs_by_head).reshape(seq_size, 2, CHUNKS, TILE, HEAD_DIM)
    half = seq_size // 2
    ends = tm_size - 1
    left = lax.ppermute(own[half:], "tm", [(i, i + 1) for i in range(ends)])
    right = lax.ppermute(own[:half], "tm", [(i + 1, i) for i in range(ends)])

    queries_by_head = queries.reshape(CHUNKS, TILE, heads, HEAD_DIM).transpose(0, 2, 1, 3)
    slots = slot_codes(extents, tile_lists, head, first_tile)
    outputs = []
    for chunk in range(CHUNKS):
        query_tiles = exchange(queries_by_head[chunk])
        attended = attend(chunk, slots, query_tiles, left, own, right)
        outputs.append(exchange(attended))
    stacked = jnp.stack(outputs)
    return stacked.transpose(0, 2, 1, 3).reshape(tok_dev, width_all)


def solution(mesh):
    placed = (P(("tm", "seq"), None), P(None, ("tm", "seq"), None), P(), P("tm", None))
    return jax.shard_map(
        per_device, mesh=mesh, in_specs=placed, out_specs=P(("tm", "seq"), None), check_vma=False
    )
```

time: 831 us -> 257 us (0.31)
  local copies, waits for them, and re-layouts: 254 us -> 17.3 us
  waiting for transfers between devices: 274 us -> 118 us
  matrix products: 99 us -> 0 us
  other arithmetic: 89.2 us -> 2.15 us
  Pallas kernels: 0 us -> 49 us
  blocking collectives: 81.5 us -> 33.3 us
  starting transfers between devices: 23.1 us -> 36.3 us
    all_to_all x2 -> x4, waiting for transfers between devices: 273 us -> 118 us  [exchange(): lax.all_to_all(blocks, 'seq', split_axis=0, concat_axis=0, tiled=True)]
    gather x32 -> x0, local copies, waits for them, and re-layouts: 100 us -> none  [the longest x16 50.2 us: one_group(): gathered_keys = jnp.take(key_tiles, lists_block, axis=0)]
    dot_general x32 -> x0, matrix products: 99 us -> none  [the longest x16 69.7 us: one_group(): jnp.einsum('bikj,bkjd->bid', weights.astype(jnp.bfloat16), gathered_value...]
    all_to_all x6 -> x0, local copies, waits for them, and re-layouts: 54.9 us -> none  [the longest x3 45.1 us: per_device(): lax.all_to_all(stacked, 'seq', split_axis=3, concat_axis=2, tiled=True)]
    pallas_call x0 -> x2, Pallas kernels: none -> 49 us  [attend(): pl.pallas_call(functools.partial(attend_kernel, chunk), grid=(count // ti...]
    concatenate x2 -> x0, other arithmetic: 48.8 us -> none  [the longest x1 38.4 us: per_device(): jnp.concatenate([head_pairs[:, 0, slab_tok - frame_tok:], head_pairs[:, 1...]
    all_to_all x1, blocking collectives: 81.5 us -> 33.3 us  [exchange(): lax.all_to_all(blocks, 'seq', split_axis=0, concat_axis=0, tiled=True)]
    reshape x2 -> x1, local copies, waits for them, and re-layouts: 41.4 us -> 0.81 us  [per_device(): queries.reshape(CHUNKS, TILE, heads, HEAD_DIM).transpose(0, 2, 1, 3)]
  transfers between devices with their start and end apart: 4 -> 6, of which waited for: 3 -> 4; matrix products, arithmetic and copies ran while one was open for 11% -> 4% of each run, Pallas kernels for 0% -> 19%
where the time goes in v1:
time: 257 us; the launch traced here: 256 us
  waiting for transfers between devices  118 us (46%)
  Pallas kernels  49 us (19%)
  starting transfers between devices  36.3 us (14%)
  blocking collectives  33.3 us (13%)
  local copies, waits for them, and re-layouts  17.3 us (7%)
    all_to_all x4, waiting for transfers between devices, exchange(): lax.all_to_all(blocks, 'seq', split_axis=0, concat_axis=0, tiled=True)  118 us
    pallas_call x2, Pallas kernels, attend(): pl.pallas_call(functools.partial(attend_kernel, chunk), grid=(count // ti...  49 us
    all_to_all x1, blocking collectives, exchange(): lax.all_to_all(blocks, 'seq', split_axis=0, concat_axis=0, tiled=True)  33.3 us
    all_to_all x4, starting transfers between devices, exchange(): lax.all_to_all(blocks, 'seq', split_axis=0, concat_axis=0, tiled=True)  30.6 us
    transpose x1, local copies, waits for them, and re-layouts, per_device(): keys_values.reshape(2, tok_dev, heads, HEAD_DIM).transpose(2, 0, 1, 3)  5.37 us
  transfers between devices with their start and end apart: 6, of which 4 were waited for; matrix products, arithmetic and copies ran while one was open for 4% of the time, Pallas kernels for 19%

profile of v1, /device:TPU:8, one launch (start us, length us, event | category | flops | bytes accessed | tf_op | source)
XLA Modules:
  0.0 256.1 jit_solution(14662420074543545107)
XLA Ops:
  0.0 0.0 copy-start
  0.0 5.4 %bitcast_bitcast_fusion = bf16[32,2,256,128]{3,2,1,0:T(8,128)(2,1)} fusion(bf16[2,256,4096]{2,1,0:T(8,128)(2,1)} %param.5), kind=kLoop, calls=%fused_computation | loop fusion | bytes 8388608 | tf_op jit(solution)/shard_map/transpose | solution.py:136
  5.4 0.0 copy-start.1
  5.4 11.6 %all-to-all-start.1 = ((bf16[32,2,256,128]{3,2,1,0:T(8,128)(2,1)}), bf16[32,2,256,128]{3,2,1,0:T(8,128)(2,1)}, u32[]{:S(2)}, u32[]{:S(2)}) async-start(bf16[32,2,256,128]{3,2,1,0:T(8,128)(2,1)} %bitcast_bitcast_fusion), calls=%async_computation.1 | async-start | bytes 8388608 | tf_op jit(solution)/shard_map/all_to_all | solution.py:124
  17.0 0.0 copy-done.1
  17.0 0.5 copy.20
  17.5 0.8 copy.26
  18.3 1.4 slice_bitcast_fusion.1
  19.7 94.4 %all-to-all-done.1 = bf16[32,2,256,128]{3,2,1,0:T(8,128)(2,1)} async-done(((bf16[32,2,256,128]{3,2,1,0:T(8,128)(2,1)}), bf16[32,2,256,128]{3,2,1,0:T(8,128)(2,1)}, u32[]{:S(2)}, u32[]{:S(2)}) %all-to-all-start.1) | async-done | bytes 4194336 | tf_op jit(solution)/shard_map/all_to_all | solution.py:124
  114.2 4.9 %all-to-all-start = ((bf16[32,128,128]{2,1,0:T(8,128)(2,1)}), bf16[32,128,128]{2,1,0:T(8,128)(2,1)S(1)}, u32[]{:S(2)}, u32[]{:S(2)}) async-start(bf16[32,128,128]{2,1,0:T(8,128)(2,1)} %get-tuple-element.7), calls=%async_computation | async-start | bytes 2097152 | tf_op jit(solution)/shard_map/all_to_all | solution.py:124
  119.1 4.8 %fusion.18 = (bf16[16,2,256,128]{3,2,1,0:T(8,128)(2,1)}, bf16[16,2,256,128]{3,2,1,0:T(8,128)(2,1)}) fusion(bf16[32,2,256,128]{3,2,1,0:T(8,128)(2,1)} %all-to-all-done.1), kind=kLoop, calls=%fused_computation.50 | loop fusion | bytes 8388608 | tf_op jit(solution)/shard_map/slice | solution.py:141
  123.9 2.0 collective-permute-start
  125.9 3.6 %collective-permute-start.1 = (bf16[16,2,2,128,128]{4,3,2,1,0:T(8,128)(2,1)}, bf16[16,2,2,128,128]{4,3,2,1,0:T(8,128)(2,1)}, u32[]{:S(2)}, u32[]{:S(2)}) collective-permute-start(bf16[16,2,2,128,128]{4,3,2,1,0:T(8,128)(2,1)} %bitcast.8), channel_id=1, source_target_pairs={{32,0},{64,32},{96,64},{128,96},{160,128},{192,160},{224,192},{33,... | collective-permute-start | bytes 6291464 | tf_op jit(solution)/shard_map/ppermute | solution.py:141
  129.6 18.1 %all-to-all-done.query_ref = bf16[32,128,128]{2,1,0:T(8,128)(2,1)S(1)} async-done(((bf16[32,128,128]{2,1,0:T(8,128)(2,1)}), bf16[32,128,128]{2,1,0:T(8,128)(2,1)S(1)}, u32[]{:S(2)}, u32[]{:S(2)}) %all-to-all-start) | async-done | bytes 1048608 | tf_op jit(solution)/shard_map/all_to_all | solution.py:124
  147.7 5.0 %all-to-all-start.3 = ((bf16[32,128,128]{2,1,0:T(8,128)(2,1)}), bf16[32,128,128]{2,1,0:T(8,128)(2,1)S(1)}, u32[]{:S(2)}, u32[]{:S(2)}) async-start(bf16[32,128,128]{2,1,0:T(8,128)(2,1)} %get-tuple-element.8), calls=%async_computation.3 | async-start | bytes 2097152 | tf_op jit(solution)/shard_map/all_to_all | solution.py:124
  152.7 0.0 copy-done.2
  152.7 0.1 copy.11
  152.8 0.0 copy-done
  152.8 0.1 constant_dynamic-slice_fusion
  152.9 0.5 fusion.19
  153.5 1.9 add_select_fusion.slots_ref
  155.4 0.0 collective-permute-done.left_ref
  155.4 0.0 collective-permute-done.1.right_ref
  155.4 24.9 %shard_map.46 = bf16[32,128,128]{2,1,0:T(8,128)(2,1)} custom-call(s32[64,16]{1,0:T(8,128)S(1)} %add_select_fusion.slots_ref, bf16[32,128,128]{2,1,0:T(8,128)(2,1)S(1)} %all-to-all-done.query_ref, bf16[16,2,2,128,128]{4,3,2,1,0:T(8,128)(2,1)} %collective-permute-done.left_ref, bf16[32,2,2,128,128]{4,3,2,1,0:T(8,128)(2,1)} %bitcast.7.own_ref, ...), custom_call_target="tpu_custom_call" | custom-call | flops 4294967296 | bytes 12582912 | tf_op jit(solution)/shard_map/pallas_call | solution.py:80
  180.3 0.7 all-to-all-done.3.query_ref
  181.0 9.1 %all-to-all-start.2 = ((bf16[32,128,128]{2,1,0:T(8,128)(2,1)}), bf16[32,128,128]{2,1,0:T(8,128)(2,1)S(1)}, u32[]{:S(2)}, u32[]{:S(2)}) async-start(bf16[32,128,128]{2,1,0:T(8,128)(2,1)} %shard_map.46), calls=%async_computation.2 | async-start | bytes 2097152 | tf_op jit(solution)/shard_map/all_to_all | solution.py:124
  190.1 24.1 %shard_map.47 = bf16[32,128,128]{2,1,0:T(8,128)(2,1)S(1)} custom-call(s32[64,16]{1,0:T(8,128)S(1)} %add_select_fusion.slots_ref, bf16[32,128,128]{2,1,0:T(8,128)(2,1)S(1)} %all-to-all-done.3.query_ref, bf16[16,2,2,128,128]{4,3,2,1,0:T(8,128)(2,1)} %collective-permute-done.left_ref, bf16[32,2,2,128,128]{4,3,2,1,0:T(8,128)(2,1)} %bitcast.7.own_ref, ...), custom_call_target="tpu_custom_call" | custom-call | flops 4294967296 | bytes 12582912 | tf_op jit(solution)/shard_map/pallas_call | solution.py:80
  214.2 4.7 %all-to-all-done.2 = bf16[32,128,128]{2,1,0:T(8,128)(2,1)S(1)} async-done(((bf16[32,128,128]{2,1,0:T(8,128)(2,1)}), bf16[32,128,128]{2,1,0:T(8,128)(2,1)S(1)}, u32[]{:S(2)}, u32[]{:S(2)}) %all-to-all-start.2) | async-done | bytes 1048608 | tf_op jit(solution)/shard_map/all_to_all | solution.py:124
  218.9 33.3 %all_to_all.25 = bf16[32,128,128]{2,1,0:T(8,128)(2,1)S(1)} all-to-all(bf16[32,128,128]{2,1,0:T(8,128)(2,1)S(1)} %shard_map.47), channel_id=1, replica_groups=mesh['tm'=8,'seq'=32] {'seq'}, dimensions={0} | all-to-all | bytes 2097152 | tf_op jit(solution)/shard_map/all_to_all | solution.py:124
  252.3 0.2 maximum_bitcast_fusion
  252.4 1.4 copy.18
  253.8 2.3 copy.25
  (3 shorter events, 0.0 us)
Async XLA Ops:
  0.0 152.8 %copy-start = (s32[3,32]{1,0:T(4,128)S(1)}, s32[3,32]{1,0:T(4,128)}, u32[]{:S(2)}) copy-start(s32[3,32]{1,0:T(4,128)} %param.6) | copy-start | bytes 1156
  5.4 11.6 %copy-start.1 = (bf16[256,4096]{1,0:T(8,128)(2,1)S(1)}, bf16[256,4096]{1,0:T(8,128)(2,1)}, u32[]{:S(2)}) copy-start(bf16[256,4096]{1,0:T(8,128)(2,1)} %param.4) | copy-start | bytes 6291460
  5.4 108.8 %all-to-all-start.1 = ((bf16[32,2,256,128]{3,2,1,0:T(8,128)(2,1)}), bf16[32,2,256,128]{3,2,1,0:T(8,128)(2,1)}, u32[]{:S(2)}, u32[]{:S(2)}) async-start(bf16[32,2,256,128]{3,2,1,0:T(8,128)(2,1)} %bitcast_bitcast_fusion), calls=%async_computation.1 | async-start | bytes 8388608 | tf_op jit(solution)/shard_map/all_to_all | solution.py:124
  114.2 33.5 %all-to-all-start = ((bf16[32,128,128]{2,1,0:T(8,128)(2,1)}), bf16[32,128,128]{2,1,0:T(8,128)(2,1)S(1)}, u32[]{:S(2)}, u32[]{:S(2)}) async-start(bf16[32,128,128]{2,1,0:T(8,128)(2,1)} %get-tuple-element.7), calls=%async_computation | async-start | bytes 2097152 | tf_op jit(solution)/shard_map/all_to_all | solution.py:124
  123.9 28.8 %copy-start.2 = (s32[64,16]{0,1:T(8,128)S(1)}, s32[64,16]{0,1:T(8,128)}, u32[]{:S(2)}) copy-start(s32[64,16]{0,1:T(8,128)} %param.7) | copy-start | bytes 12292
  123.9 31.5 %collective-permute-start = (bf16[16,2,2,128,128]{4,3,2,1,0:T(8,128)(2,1)}, bf16[16,2,2,128,128]{4,3,2,1,0:T(8,128)(2,1)}, u32[]{:S(2)}, u32[]{:S(2)}) collective-permute-start(bf16[16,2,2,128,128]{4,3,2,1,0:T(8,128)(2,1)} %bitcast.6), channel_id=1, source_target_pairs={{0,32},{32,64},{64,96},{96,128},{128,160},{160,192},{192,224},{1,3... | collective-permute-start | bytes 6291464 | tf_op jit(solution)/shard_map/ppermute | solution.py:140
  125.9 29.5 %collective-permute-start.1 = (bf16[16,2,2,128,128]{4,3,2,1,0:T(8,128)(2,1)}, bf16[16,2,2,128,128]{4,3,2,1,0:T(8,128)(2,1)}, u32[]{:S(2)}, u32[]{:S(2)}) collective-permute-start(bf16[16,2,2,128,128]{4,3,2,1,0:T(8,128)(2,1)} %bitcast.8), channel_id=1, source_target_pairs={{32,0},{64,32},{96,64},{128,96},{160,128},{192,160},{224,192},{33,... | collective-permute-start | bytes 6291464 | tf_op jit(solution)/shard_map/ppermute | solution.py:141
  147.7 33.3 %all-to-all-start.3 = ((bf16[32,128,128]{2,1,0:T(8,128)(2,1)}), bf16[32,128,128]{2,1,0:T(8,128)(2,1)S(1)}, u32[]{:S(2)}, u32[]{:S(2)}) async-start(bf16[32,128,128]{2,1,0:T(8,128)(2,1)} %get-tuple-element.8), calls=%async_computation.3 | async-start | bytes 2097152 | tf_op jit(solution)/shard_map/all_to_all | solution.py:124
  181.0 37.9 %all-to-all-start.2 = ((bf16[32,128,128]{2,1,0:T(8,128)(2,1)}), bf16[32,128,128]{2,1,0:T(8,128)(2,1)S(1)}, u32[]{:S(2)}, u32[]{:S(2)}) async-start(bf16[32,128,128]{2,1,0:T(8,128)(2,1)} %shard_map.46), calls=%async_computation.2 | async-start | bytes 2097152 | tf_op jit(solution)/shard_map/all_to_all | solution.py:124

commit v2 on v1

v2 whole, which is shorter than its diff:
```python
import functools

import jax
import jax.numpy as jnp
from jax import lax
from jax.experimental import pallas as pl
from jax.experimental.pallas import tpu as pltpu
from jax.sharding import PartitionSpec as P

HEAD_DIM = 128
TILE = 128
FRAME = 32
KSEL = 16
CHUNKS = 2
HEADS_STEP = 4
NO_TILE = 128
EXP2_SCALE = HEAD_DIM ** (-0.5) * 1.4426950408889634
MIB = 1024 * 1024


def split_kernel(extents, list_ref, query_ref, pair_ref, block_ref, second_ref, id_ref):
    for head in range(block_ref.shape[0]):
        columns = slice(head * HEAD_DIM, (head + 1) * HEAD_DIM)
        for part in range(2):
            for half in range(CHUNKS):
                rows = slice(half * TILE, (half + 1) * TILE)
                block_ref[head, part * CHUNKS + half] = pair_ref[part, rows, columns]
        block_ref[head, 2 * CHUNKS] = query_ref[0:TILE, columns]
        second_ref[head] = query_ref[TILE : 2 * TILE, columns]

    @pl.when(pl.program_id(0) == 0)
    def _():
        head = lax.axis_index("seq")
        listed = list_ref[...]
        first = lax.axis_index("tm") * listed.shape[1]
        tiles = first + lax.broadcasted_iota(jnp.int32, listed.shape, 1)
        live = None
        for axis, (low, mask) in enumerate(((5, 15), (3, 3), (0, 7))):
            gap = jnp.abs(((listed >> low) & mask) - ((tiles >> low) & mask))
            near = gap <= extents[axis, head]
            live = near if live is None else live & near
        shift = first - FRAME
        id_ref[0] = jnp.where(live, listed, tiles) - shift
        id_ref[1] = jnp.where(live, listed - shift, NO_TILE)


def split_heads(queries, keys_values, extents, tile_lists):
    tok_dev, width_all = queries.shape
    heads = width_all // HEAD_DIM
    width = HEADS_STEP * HEAD_DIM
    parts = 2 * CHUNKS + 1
    slots, rows = tile_lists.shape[1], tile_lists.shape[0]
    return pl.pallas_call(
        split_kernel,
        grid=(heads // HEADS_STEP,),
        in_specs=[
            pl.BlockSpec(memory_space=pltpu.SMEM),
            pl.BlockSpec((slots, rows), lambda i: (0, 0)),
            pl.BlockSpec((tok_dev, width), lambda i: (0, i)),
            pl.BlockSpec((2, tok_dev, width), lambda i: (0, 0, i)),
        ],
        out_specs=[
            pl.BlockSpec((HEADS_STEP, parts, TILE, HEAD_DIM), lambda i: (i, 0, 0, 0)),
            pl.BlockSpec((HEADS_STEP, TILE, HEAD_DIM), lambda i: (i, 0, 0)),
            pl.BlockSpec((2, slots, rows), lambda i: (0, 0, 0)),
        ],
        out_shape=[
            jax.ShapeDtypeStruct((heads, parts, TILE, HEAD_DIM), jnp.bfloat16),
            jax.ShapeDtypeStruct((heads, TILE, HEAD_DIM), jnp.bfloat16),
            jax.ShapeDtypeStruct((2, slots, rows), jnp.int32),
        ],
        compiler_params=pltpu.CompilerParams(vmem_limit_bytes=60 * MIB),
    )(extents, tile_lists.T, queries, keys_values)


def join_kernel(first_ref, second_ref, out_ref):
    for head in range(first_ref.shape[0]):
        columns = slice(head * HEAD_DIM, (head + 1) * HEAD_DIM)
        out_ref[0:TILE, columns] = first_ref[head]
        out_ref[TILE : 2 * TILE, columns] = second_ref[head]


def join_heads(first, second):
    heads = first.shape[0]
    width = HEADS_STEP * HEAD_DIM
    block = pl.BlockSpec((HEADS_STEP, TILE, HEAD_DIM), lambda i: (i, 0, 0))
    return pl.pallas_call(
        join_kernel,
        grid=(heads // HEADS_STEP,),
        in_specs=[block, block],
        out_specs=pl.BlockSpec((2 * TILE, width), lambda i: (0, i)),
        out_shape=jax.ShapeDtypeStruct((2 * TILE, heads * HEAD_DIM), jnp.bfloat16),
        compiler_params=pltpu.CompilerParams(vmem_limit_bytes=60 * MIB),
    )(first, second)


def attend_kernel(
    chunk,
    query_part,
    slot_ids,
    query_hbm,
    left_hbm,
    own_hbm,
    right_hbm,
    out_ref,
    keys,
    values,
    query,
    marks,
    scores,
    tops,
    sems,
):
    pairs = own_hbm.shape[0]
    rim = left_hbm.shape[0]
    places = ((own_hbm, rim), (left_hbm, 0), (right_hbm, rim + pairs))
    copies = [pltpu.make_async_copy(query_hbm.at[:, query_part], query, sems.at[0])]
    for part, held in enumerate((keys, values)):
        for source, start in places:
            copies.append(
                pltpu.make_async_copy(
                    source.at[:, pl.ds(part * CHUNKS, CHUNKS)],
                    held.at[pl.ds(start, source.shape[0])],
                    sems.at[len(copies)],
                )
            )
    for copy in copies:
        copy.start()
    marks[0] = jnp.ones((TILE, HEAD_DIM), jnp.bfloat16)
    marks[1] = jnp.zeros((TILE, HEAD_DIM), jnp.bfloat16)
    values[NO_TILE // CHUNKS] = jnp.zeros((CHUNKS, TILE, HEAD_DIM), jnp.bfloat16)
    for copy in copies[:4]:
        copy.wait()
    count = query.shape[0]

    def score_pair(row, tile_query, slot):
        ids = [slot_ids[0, slot + i, row] for i in range(2)]
        both = jnp.concatenate([keys[k >> 1, k & 1] for k in ids], axis=0)
        return lax.dot_general(
            tile_query, both, (((1,), (1,)), ((), ())), preferred_element_type=jnp.float32
        )

    def value_pair(row, slot):
        ids = [slot_ids[1, slot + i, row] for i in range(2)]
        return jnp.concatenate(
            [jnp.concatenate([values[k >> 1, k & 1], marks[k >> 7]], axis=1) for k in ids], axis=0
        )

    def fold(best, score):
        score = jnp.maximum(score[:, :TILE], score[:, TILE:])
        return score if best is None else jnp.maximum(best, score)

    def put_top(place, best):
        tops[place] = jnp.broadcast_to(jnp.max(best, axis=1, keepdims=True), (TILE, TILE))

    best = None
    for slot in range(0, KSEL, 2):
        score = score_pair(chunk, query[0], slot)
        scores[0, slot // 2] = score
        best = fold(best, score)
    put_top(0, best)
    for copy in copies[4:]:
        copy.wait()

    def step(turn, carry):
        for now in range(2):
            tile = turn * 2 + now
            later = jnp.minimum(tile + 1, count - 1)
            row, later_row = tile * CHUNKS + chunk, later * CHUNKS + chunk
            top = tops[now]
            top = jnp.concatenate([top, top], axis=1)
            later_query = query[later]
            best = None
            mixed = None
            for slot in range(0, KSEL, 2):
                score = score_pair(later_row, later_query, slot)
                scores[1 - now, slot // 2] = score
                best = fold(best, score)
                weights = jnp.exp2((scores[now, slot // 2] - top) * EXP2_SCALE)
                part = jnp.dot(
                    weights.astype(jnp.bfloat16),
                    value_pair(row, slot),
                    preferred_element_type=jnp.float32,
                )
                mixed = part if mixed is None else mixed + part
            put_top(1 - now, best)
            out_ref[tile] = (mixed[:, :HEAD_DIM] / mixed[:, HEAD_DIM:]).astype(jnp.bfloat16)
        return carry

    lax.fori_loop(0, count // 2, step, 0)


def attend(chunk, ids, query_tiles, query_part, left, own, right):
    count = query_tiles.shape[0]
    held = own.shape[0] + 2 * left.shape[0]
    whole = pl.BlockSpec(memory_space=pl.ANY)
    scalar = pl.BlockSpec(memory_space=pltpu.SMEM)
    return pl.pallas_call(
        functools.partial(attend_kernel, chunk, query_part),
        in_specs=[scalar, whole, whole, whole, whole],
        out_specs=pl.BlockSpec(memory_space=pltpu.VMEM),
        out_shape=jax.ShapeDtypeStruct((count, TILE, HEAD_DIM), jnp.bfloat16),
        scratch_shapes=[
            pltpu.VMEM((held, CHUNKS, TILE, HEAD_DIM), jnp.bfloat16),
            pltpu.VMEM((held + 1, CHUNKS, TILE, HEAD_DIM), jnp.bfloat16),
            pltpu.VMEM((count, TILE, HEAD_DIM), jnp.bfloat16),
            pltpu.VMEM((2, TILE, HEAD_DIM), jnp.bfloat16),
            pltpu.VMEM((2, KSEL // 2, TILE, 2 * TILE), jnp.float32),
            pltpu.VMEM((2, TILE, TILE), jnp.float32),
            pltpu.SemaphoreType.DMA((7,)),
        ],
        compiler_params=pltpu.CompilerParams(vmem_limit_bytes=60 * MIB),
        cost_estimate=pl.CostEstimate(
            flops=count * KSEL * TILE * TILE * HEAD_DIM * 4,
            bytes_accessed=12 * MIB,
            transcendentals=count * KSEL * TILE * TILE,
        ),
    )(ids, query_tiles, left, own, right)


def exchange(blocks):
    return lax.all_to_all(blocks, "seq", split_axis=0, concat_axis=0, tiled=True)


def per_device(queries, keys_values, extents, tile_lists):
    seq_size = lax.axis_size("seq")
    tm_size = lax.axis_size("tm")
    blocks, second, ids = split_heads(queries, keys_values, extents, tile_lists)
    own = exchange(blocks)
    half = seq_size // 2
    ends = tm_size - 1
    rims = 2 * CHUNKS
    left = lax.ppermute(own[half:, :rims], "tm", [(i, i + 1) for i in range(ends)])
    right = lax.ppermute(own[:half, :rims], "tm", [(i + 1, i) for i in range(ends)])

    second = exchange(second)[:, None]
    first_out = exchange(attend(0, ids, own, rims, left, own, right))
    second_out = exchange(attend(1, ids, second, 0, left, own, right))
    return join_heads(first_out, second_out)


def solution(mesh):
    placed = (P(("tm", "seq"), None), P(None, ("tm", "seq"), None), P(), P("tm", None))
    return jax.shard_map(
        per_device, mesh=mesh, in_specs=placed, out_specs=P(("tm", "seq"), None), check_vma=False
    )
```

time: 257 us -> 264 us (1.027)
  blocking collectives: 33.3 us -> 163 us
  waiting for transfers between devices: 118 us -> 27.8 us
  starting transfers between devices: 36.3 us -> 14.5 us
  local copies, waits for them, and re-layouts: 17.3 us -> 2.93 us
  Pallas kernels: 49 us -> 54.6 us
    all_to_all x1 -> x2, blocking collectives: 33.3 us -> 163 us  [exchange(): lax.all_to_all(blocks, 'seq', split_axis=0, concat_axis=0, tiled=True)]
    all_to_all x4 -> x2, waiting for transfers between devices: 118 us -> 7.81 us  [exchange(): lax.all_to_all(blocks, 'seq', split_axis=0, concat_axis=0, tiled=True)]
    all_to_all x4 -> x2, starting transfers between devices: 30.6 us -> 10.2 us  [exchange(): lax.all_to_all(blocks, 'seq', split_axis=0, concat_axis=0, tiled=True)]
    ppermute x2, waiting for transfers between devices: 0.01 us -> 20 us  [the longest x1 16.3 us: per_device(): lax.ppermute(own[:half, :rims], 'tm', [(i + 1, i) for i in range(ends)])]
    transpose x2 -> x0, local copies, waits for them, and re-layouts: 6.72 us -> none  [the longest x1 5.37 us: per_device(): keys_values.reshape(2, tok_dev, heads, HEAD_DIM).transpose(2, 0, 1, 3)]
    pallas_call x2 -> x4, Pallas kernels: 49 us -> 54.6 us  [the longest x2 40.6 us: attend(): pl.pallas_call(functools.partial(attend_kernel, chunk, query_part), in_sp...]
    slice x2 -> x1, local copies, waits for them, and re-layouts: 5.33 us -> 2.01 us  [per_device(): own[:half, :rims]]
  transfers between devices with their start and end apart: 6 -> 4, of which waited for: 4 -> 3; matrix products, arithmetic and copies ran while one was open for 4% -> 0% of each run, Pallas kernels for 19% -> 15%
where the time goes in v2:
time: 264 us; the launch traced here: 263 us
  blocking collectives  163 us (62%)
  Pallas kernels  54.6 us (21%)
  waiting for transfers between devices  27.8 us (11%)
  starting transfers between devices  14.5 us (5%)
  local copies, waits for them, and re-layouts  2.93 us (1%)
    all_to_all x2, blocking collectives, exchange(): lax.all_to_all(blocks, 'seq', split_axis=0, concat_axis=0, tiled=True)  163 us
    pallas_call x2, Pallas kernels, attend(): pl.pallas_call(functools.partial(attend_kernel, chunk, query_part), in_sp...  40.6 us
    ppermute x1, waiting for transfers between devices, per_device(): lax.ppermute(own[:half, :rims], 'tm', [(i + 1, i) for i in range(ends)])  16.3 us
    all_to_all x2, starting transfers between devices, exchange(): lax.all_to_all(blocks, 'seq', split_axis=0, concat_axis=0, tiled=True)  10.2 us
    pallas_call x1, Pallas kernels, split_heads(): pl.pallas_call(split_kernel, grid=(heads // HEADS_STEP,), in_specs=[pl.Bl...  8.18 us
    all_to_all x2, waiting for transfers between devices, exchange(): lax.all_to_all(blocks, 'seq', split_axis=0, concat_axis=0, tiled=True)  7.81 us
    pallas_call x1, Pallas kernels, join_heads(): pl.pallas_call(join_kernel, grid=(heads // HEADS_STEP,), in_specs=[block,...  5.84 us
  transfers between devices with their start and end apart: 4, of which 3 were waited for; matrix products, arithmetic and copies ran while one was open for 0% of the time, Pallas kernels for 15%

profile of v2, /device:TPU:8, one launch (start us, length us, event | category | flops | bytes accessed | tf_op | source)
XLA Modules:
  0.0 263.0 jit_solution(18029493028857850695)
XLA Ops:
  0.0 8.2 %shard_map.46 = (bf16[32,5,128,128]{3,2,1,0:T(8,128)(2,1)}, bf16[32,128,128]{2,1,0:T(8,128)(2,1)}, s32[2,16,64]{2,1,0:T(8,128)}) custom-call(s32[3,32]{1,0:T(4,128)} %extents.1, s32[16,64]{1,0:T(8,128)} %bitcast.3, bf16[256,4096]{1,0:T(8,128)(2,1)} %query_ref.1, bf16[2,256,4096]{2,1,0:T(8,128)(2,1)} %pair_ref.1), custom_call_target="tpu_custom_call" | custom-call | tf_op jit(solution)/shard_map/pallas_call | solution.py:53
  8.2 129.8 %all_to_all.20.query_hbm.own_hbm = bf16[32,5,128,128]{3,2,1,0:T(8,128)(2,1)S(1)} all-to-all(bf16[32,5,128,128]{3,2,1,0:T(8,128)(2,1)} %get-tuple-element.9), channel_id=1, replica_groups=mesh['tm'=8,'seq'=32] {'seq'}, dimensions={0} | all-to-all | bytes 10485760 | tf_op jit(solution)/shard_map/all_to_all | solution.py:222
  138.0 0.0 copy-start
  138.0 2.0 fusion
  140.0 0.9 copy-done
  140.9 1.9 collective-permute-start.1
  142.9 2.4 collective-permute-start
  145.3 5.1 %all-to-all-start.2 = ((bf16[32,128,128]{2,1,0:T(8,128)(2,1)}), bf16[32,128,128]{2,1,0:T(8,128)(2,1)S(1)}, u32[]{:S(2)}, u32[]{:S(2)}) async-start(bf16[32,128,128]{2,1,0:T(8,128)(2,1)} %get-tuple-element.10), calls=%async_computation.2 | async-start | bytes 2097152 | tf_op jit(solution)/shard_map/all_to_all | solution.py:222
  150.4 16.3 %collective-permute-done.1.right_hbm = bf16[16,4,128,128]{3,2,1,0:T(8,128)(2,1)} collective-permute-done((bf16[16,4,128,128]{3,2,1,0:T(8,128)(2,1)}, bf16[16,4,128,128]{3,2,1,0:T(8,128)(2,1)}, u32[]{:S(2)}, u32[]{:S(2)}) %collective-permute-start.1) | collective-permute-done | bytes 2097184 | tf_op jit(solution)/shard_map/ppermute | solution.py:234
  166.7 3.6 %collective-permute-done.left_hbm = bf16[16,4,128,128]{3,2,1,0:T(8,128)(2,1)} collective-permute-done((bf16[16,4,128,128]{3,2,1,0:T(8,128)(2,1)S(1)}, bf16[16,4,128,128]{3,2,1,0:T(8,128)(2,1)}, u32[]{:S(2)}, u32[]{:S(2)}) %collective-permute-start) | collective-permute-done | bytes 2097184 | tf_op jit(solution)/shard_map/ppermute | solution.py:233
  170.3 20.3 %shard_map.47 = bf16[32,128,128]{2,1,0:T(8,128)(2,1)} custom-call(s32[2,16,64]{2,1,0:T(8,128)} %get-tuple-element.8.slot_ids, bf16[32,5,128,128]{3,2,1,0:T(8,128)(2,1)} %copy-done, bf16[16,4,128,128]{3,2,1,0:T(8,128)(2,1)} %collective-permute-done.left_hbm, bf16[32,5,128,128]{3,2,1,0:T(8,128)(2,1)} %copy-done, ...), custom_call_target="tpu_custom_call" | custom-call | flops 4294967296 | bytes 12582912 | tf_op jit(solution)/shard_map/pallas_call | solution.py:198
  190.6 0.0 all-to-all-done.2
  190.7 0.0 copy-start.2
  190.7 5.1 %all-to-all-start.1 = ((bf16[32,128,128]{2,1,0:T(8,128)(2,1)}), bf16[32,128,128]{2,1,0:T(8,128)(2,1)S(1)}, u32[]{:S(2)}, u32[]{:S(2)}) async-start(bf16[32,128,128]{2,1,0:T(8,128)(2,1)} %shard_map.47), calls=%async_computation.1 | async-start | bytes 2097152 | tf_op jit(solution)/shard_map/all_to_all | solution.py:222
  195.8 0.0 copy-done.2
  195.8 20.3 %shard_map.48 = bf16[32,128,128]{2,1,0:T(8,128)(2,1)} custom-call(s32[2,16,64]{2,1,0:T(8,128)} %get-tuple-element.8.slot_ids, bf16[32,1,128,128]{3,2,1,0:T(8,128)(2,1)} %bitcast.2, bf16[16,4,128,128]{3,2,1,0:T(8,128)(2,1)} %collective-permute-done.left_hbm, bf16[32,5,128,128]{3,2,1,0:T(8,128)(2,1)} %copy-done, ...), custom_call_target="tpu_custom_call" | custom-call | flops 4294967296 | bytes 12582912 | tf_op jit(solution)/shard_map/pallas_call | solution.py:198
  216.1 7.8 %all-to-all-done.1.first_ref = bf16[32,128,128]{2,1,0:T(8,128)(2,1)S(1)} async-done(((bf16[32,128,128]{2,1,0:T(8,128)(2,1)}), bf16[32,128,128]{2,1,0:T(8,128)(2,1)S(1)}, u32[]{:S(2)}, u32[]{:S(2)}) %all-to-all-start.1) | async-done | bytes 1048608 | tf_op jit(solution)/shard_map/all_to_all | solution.py:222
  223.9 0.0 copy-start.1
  223.9 33.3 %all_to_all.21.second_ref = bf16[32,128,128]{2,1,0:T(8,128)(2,1)} all-to-all(bf16[32,128,128]{2,1,0:T(8,128)(2,1)} %shard_map.48), channel_id=1, replica_groups=mesh['tm'=8,'seq'=32] {'seq'}, dimensions={0} | all-to-all | bytes 2097152 | tf_op jit(solution)/shard_map/all_to_all | solution.py:222
  257.2 0.0 copy-done.1
  257.2 5.8 %shard_map.49 = bf16[256,4096]{1,0:T(8,128)(2,1)} custom-call(bf16[32,128,128]{2,1,0:T(8,128)(2,1)} %copy-done.1, bf16[32,128,128]{2,1,0:T(8,128)(2,1)} %all_to_all.21.second_ref), custom_call_target="tpu_custom_call" | custom-call | tf_op jit(solution)/shard_map/pallas_call | solution.py:87
Async XLA Ops:
  138.0 2.9 %copy-start = (bf16[32,5,128,128]{3,2,1,0:T(8,128)(2,1)}, bf16[32,5,128,128]{3,2,1,0:T(8,128)(2,1)S(1)}, u32[]{:S(2)}) copy-start(bf16[32,5,128,128]{3,2,1,0:T(8,128)(2,1)S(1)} %all_to_all.20.query_hbm.own_hbm) | copy-start | bytes 15728644
  140.9 25.8 %collective-permute-start.1 = (bf16[16,4,128,128]{3,2,1,0:T(8,128)(2,1)}, bf16[16,4,128,128]{3,2,1,0:T(8,128)(2,1)}, u32[]{:S(2)}, u32[]{:S(2)}) collective-permute-start(bf16[16,4,128,128]{3,2,1,0:T(8,128)(2,1)} %get-tuple-element.11), channel_id=1, source_target_pairs={{32,0},{64,32},{96,64},{128,96},{160,128},{192,160},{224,192},{33,... | collective-permute-start | bytes 6291464 | tf_op jit(solution)/shard_map/ppermute | solution.py:234
  142.9 27.5 %collective-permute-start = (bf16[16,4,128,128]{3,2,1,0:T(8,128)(2,1)S(1)}, bf16[16,4,128,128]{3,2,1,0:T(8,128)(2,1)}, u32[]{:S(2)}, u32[]{:S(2)}) collective-permute-start(bf16[16,4,128,128]{3,2,1,0:T(8,128)(2,1)S(1)} %get-tuple-element.12), channel_id=1, source_target_pairs={{0,32},{32,64},{64,96},{96,128},{128,160},{160,192},{192,224},{1,3... | collective-permute-start | bytes 6291464 | tf_op jit(solution)/shard_map/ppermute | solution.py:233
  145.3 45.4 %all-to-all-start.2 = ((bf16[32,128,128]{2,1,0:T(8,128)(2,1)}), bf16[32,128,128]{2,1,0:T(8,128)(2,1)S(1)}, u32[]{:S(2)}, u32[]{:S(2)}) async-start(bf16[32,128,128]{2,1,0:T(8,128)(2,1)} %get-tuple-element.10), calls=%async_computation.2 | async-start | bytes 2097152 | tf_op jit(solution)/shard_map/all_to_all | solution.py:222
  190.7 5.1 %copy-start.2 = (bf16[32,128,128]{2,1,0:T(8,128)(2,1)}, bf16[32,128,128]{2,1,0:T(8,128)(2,1)S(1)}, u32[]{:S(2)}) copy-start(bf16[32,128,128]{2,1,0:T(8,128)(2,1)S(1)} %all-to-all-done.2) | copy-start | bytes 3145732
  190.7 33.2 %all-to-all-start.1 = ((bf16[32,128,128]{2,1,0:T(8,128)(2,1)}), bf16[32,128,128]{2,1,0:T(8,128)(2,1)S(1)}, u32[]{:S(2)}, u32[]{:S(2)}) async-start(bf16[32,128,128]{2,1,0:T(8,128)(2,1)} %shard_map.47), calls=%async_computation.1 | async-start | bytes 2097152 | tf_op jit(solution)/shard_map/all_to_all | solution.py:222
  223.9 33.3 %copy-start.1 = (bf16[32,128,128]{2,1,0:T(8,128)(2,1)}, bf16[32,128,128]{2,1,0:T(8,128)(2,1)S(1)}, u32[]{:S(2)}) copy-start(bf16[32,128,128]{2,1,0:T(8,128)(2,1)S(1)} %all-to-all-done.1.first_ref) | copy-start | bytes 3145732

commit v3 on v2

--- a/solution.py
+++ b/solution.py
@@ -12,21 +12,40 @@
 FRAME = 32
 KSEL = 16
 CHUNKS = 2
-HEADS_STEP = 4
+HEADS_STEP = 16
 NO_TILE = 128
 EXP2_SCALE = HEAD_DIM ** (-0.5) * 1.4426950408889634
 MIB = 1024 * 1024
 
 
-def split_kernel(extents, list_ref, query_ref, pair_ref, block_ref, second_ref, id_ref):
+def split_queries_kernel(query_ref, *block_refs):
+    for chunk, block_ref in enumerate(block_refs):
+        for head in range(block_ref.shape[0]):
+            columns = slice(head * HEAD_DIM, (head + 1) * HEAD_DIM)
+            block_ref[head] = query_ref[chunk * TILE : (chunk + 1) * TILE, columns]
+
+
+def split_queries(queries):
+    tok_dev, width_all = queries.shape
+    heads = width_all // HEAD_DIM
+    return pl.pallas_call(
+        split_queries_kernel,
+        grid=(heads // HEADS_STEP,),
+        in_specs=[pl.BlockSpec((tok_dev, HEADS_STEP * HEAD_DIM), lambda i: (0, i))],
+        out_specs=[pl.BlockSpec((HEADS_STEP, TILE, HEAD_DIM), lambda i: (i, 0, 0))] * CHUNKS,
+        out_shape=[jax.ShapeDtypeStruct((heads, TILE, HEAD_DIM), jnp.bfloat16)] * CHUNKS,
+        compiler_params=pltpu.CompilerParams(vmem_limit_bytes=60 * MIB),
+        cost_estimate=pl.CostEstimate(flops=0, bytes_accessed=4 * MIB, transcendentals=0),
+    )(queries)
+
+
+def split_pairs_kernel(extents, list_ref, pair_ref, block_ref, id_ref):
     for head in range(block_ref.shape[0]):
         columns = slice(head * HEAD_DIM, (head + 1) * HEAD_DIM)
         for part in range(2):
             for half in range(CHUNKS):
                 rows = slice(half * TILE, (half + 1) * TILE)
                 block_ref[head, part * CHUNKS + half] = pair_ref[part, rows, columns]
-        block_ref[head, 2 * CHUNKS] = query_ref[0:TILE, columns]
-        second_ref[head] = query_ref[TILE : 2 * TILE, columns]
 
     @pl.when(pl.program_id(0) == 0)
     def _():
@@ -44,59 +63,78 @@
         id_ref[1] = jnp.where(live, listed - shift, NO_TILE)
 
 
-def split_heads(queries, keys_values, extents, tile_lists):
-    tok_dev, width_all = queries.shape
+def split_pairs(keys_values, extents, tile_lists):
+    _, tok_dev, width_all = keys_values.shape
     heads = width_all // HEAD_DIM
-    width = HEADS_STEP * HEAD_DIM
-    parts = 2 * CHUNKS + 1
-    slots, rows = tile_lists.shape[1], tile_lists.shape[0]
-    return pl.pallas_call(
-        split_kernel,
+    parts = 2 * CHUNKS
+    rows, slots = tile_lists.shape
+    return pl.pallas_call(
+        split_pairs_kernel,
         grid=(heads // HEADS_STEP,),
         in_specs=[
             pl.BlockSpec(memory_space=pltpu.SMEM),
             pl.BlockSpec((slots, rows), lambda i: (0, 0)),
-            pl.BlockSpec((tok_dev, width), lambda i: (0, i)),
-            pl.BlockSpec((2, tok_dev, width), lambda i: (0, 0, i)),
+            pl.BlockSpec((2, tok_dev, HEADS_STEP * HEAD_DIM), lambda i: (0, 0, i)),
         ],
         out_specs=[
             pl.BlockSpec((HEADS_STEP, parts, TILE, HEAD_DIM), lambda i: (i, 0, 0, 0)),
-            pl.BlockSpec((HEADS_STEP, TILE, HEAD_DIM), lambda i: (i, 0, 0)),
             pl.BlockSpec((2, slots, rows), lambda i: (0, 0, 0)),
         ],
         out_shape=[
             jax.ShapeDtypeStruct((heads, parts, TILE, HEAD_DIM), jnp.bfloat16),
-            jax.ShapeDtypeStruct((heads, TILE, HEAD_DIM), jnp.bfloat16),
             jax.ShapeDtypeStruct((2, slots, rows), jnp.int32),
         ],
         compiler_params=pltpu.CompilerParams(vmem_limit_bytes=60 * MIB),
-    )(extents, tile_lists.T, queries, keys_values)
-
-
-def join_kernel(first_ref, second_ref, out_ref):
-    for head in range(first_ref.shape[0]):
-        columns = slice(head * HEAD_DIM, (head + 1) * HEAD_DIM)
-        out_ref[0:TILE, columns] = first_ref[head]
-        out_ref[TILE : 2 * TILE, columns] = second_ref[head]
+    )(extents, tile_lists.T, keys_values)
+
+
+def join_kernel(first_hbm, second_hbm, out_hbm, held, in_sems, out_sems):
+    sources = (first_hbm, second_hbm)
+    reads = [
+        [
+            pltpu.make_async_copy(
+                source.at[head],
+                held.at[pl.ds(chunk * TILE, TILE), pl.ds(head * HEAD_DIM, HEAD_DIM)],
+                in_sems.at[chunk, head],
+            )
+            for head in range(source.shape[0])
+        ]
+        for chunk, source in enumerate(sources)
+    ]
+    for copies in reads:
+        for copy in copies:
+            copy.start()
+    writes = []
+    for chunk, copies in enumerate(reads):
+        for copy in copies:
+            copy.wait()
+        rows = pl.ds(chunk * TILE, TILE)
+        writes.append(pltpu.make_async_copy(held.at[rows], out_hbm.at[rows], out_sems.at[chunk]))
+        writes[-1].start()
+    for copy in writes:
+        copy.wait()
 
 
 def join_heads(first, second):
     heads = first.shape[0]
-    width = HEADS_STEP * HEAD_DIM
-    block = pl.BlockSpec((HEADS_STEP, TILE, HEAD_DIM), lambda i: (i, 0, 0))
+    whole = pl.BlockSpec(memory_space=pl.ANY)
+    shape = (CHUNKS * TILE, heads * HEAD_DIM)
     return pl.pallas_call(
         join_kernel,
-        grid=(heads // HEADS_STEP,),
-        in_specs=[block, block],
-        out_specs=pl.BlockSpec((2 * TILE, width), lambda i: (0, i)),
-        out_shape=jax.ShapeDtypeStruct((2 * TILE, heads * HEAD_DIM), jnp.bfloat16),
+        in_specs=[whole, whole],
+        out_specs=whole,
+        out_shape=jax.ShapeDtypeStruct(shape, jnp.bfloat16),
+        scratch_shapes=[
+            pltpu.VMEM(shape, jnp.bfloat16),
+            pltpu.SemaphoreType.DMA((CHUNKS, heads)),
+            pltpu.SemaphoreType.DMA((CHUNKS,)),
+        ],
         compiler_params=pltpu.CompilerParams(vmem_limit_bytes=60 * MIB),
     )(first, second)
 
 
 def attend_kernel(
     chunk,
-    query_part,
     slot_ids,
     query_hbm,
     left_hbm,
@@ -114,7 +152,7 @@
     pairs = own_hbm.shape[0]
     rim = left_hbm.shape[0]
     places = ((own_hbm, rim), (left_hbm, 0), (right_hbm, rim + pairs))
-    copies = [pltpu.make_async_copy(query_hbm.at[:, query_part], query, sems.at[0])]
+    copies = [pltpu.make_async_copy(query_hbm, query, sems.at[0])]
     for part, held in enumerate((keys, values)):
         for source, start in places:
             copies.append(
@@ -190,13 +228,13 @@
     lax.fori_loop(0, count // 2, step, 0)
 
 
-def attend(chunk, ids, query_tiles, query_part, left, own, right):
+def attend(chunk, ids, query_tiles, left, own, right):
     count = query_tiles.shape[0]
     held = own.shape[0] + 2 * left.shape[0]
     whole = pl.BlockSpec(memory_space=pl.ANY)
     scalar = pl.BlockSpec(memory_space=pltpu.SMEM)
     return pl.pallas_call(
-        functools.partial(attend_kernel, chunk, query_part),
+        functools.partial(attend_kernel, chunk),
         in_specs=[scalar, whole, whole, whole, whole],
         out_specs=pl.BlockSpec(memory_space=pltpu.VMEM),
         out_shape=jax.ShapeDtypeStruct((count, TILE, HEAD_DIM), jnp.bfloat16),
@@ -225,17 +263,17 @@
 def per_device(queries, keys_values, extents, tile_lists):
     seq_size = lax.axis_size("seq")
     tm_size = lax.axis_size("tm")
-    blocks, second, ids = split_heads(queries, keys_values, extents, tile_lists)
+    blocks, ids = split_pairs(keys_values, extents, tile_lists)
+    first, second = split_queries(queries)
     own = exchange(blocks)
     half = seq_size // 2
     ends = tm_size - 1
-    rims = 2 * CHUNKS
-    left = lax.ppermute(own[half:, :rims], "tm", [(i, i + 1) for i in range(ends)])
-    right = lax.ppermute(own[:half, :rims], "tm", [(i + 1, i) for i in range(ends)])
-
-    second = exchange(second)[:, None]
-    first_out = exchange(attend(0, ids, own, rims, left, own, right))
-    second_out = exchange(attend(1, ids, second, 0, left, own, right))
+    left = lax.ppermute(own[half:], "tm", [(i, i + 1) for i in range(ends)])
+    right = lax.ppermute(own[:half], "tm", [(i + 1, i) for i in range(ends)])
+    first = exchange(first)
+    second = exchange(second)
+    first_out = exchange(attend(0, ids, first, left, own, right))
+    second_out = exchange(attend(1, ids, second, left, own, right))
     return join_heads(first_out, second_out)
 
 

time: 264 us -> 250 us (0.947)
  blocking collectives: 163 us -> 33.3 us
  waiting for transfers between devices: 27.8 us -> 129 us
  starting transfers between devices: 14.5 us -> 32 us
  Pallas kernels: 54.6 us -> 50.5 us
    all_to_all x2 -> x1, blocking collectives: 163 us -> 33.3 us  [exchange(): lax.all_to_all(blocks, 'seq', split_axis=0, concat_axis=0, tiled=True)]
    all_to_all x2 -> x4, waiting for transfers between devices: 7.81 us -> 129 us  [exchange(): lax.all_to_all(blocks, 'seq', split_axis=0, concat_axis=0, tiled=True)]
    ppermute x2, waiting for transfers between devices: 20 us -> 0.01 us  [the longest x1 0.01 us: per_device(): left = lax.ppermute(own[half:], 'tm', [(i, i + 1) for i in range(ends)])]
    all_to_all x2 -> x4, starting transfers between devices: 10.2 us -> 26.4 us  [exchange(): lax.all_to_all(blocks, 'seq', split_axis=0, concat_axis=0, tiled=True)]
    pallas_call x4 -> x5, Pallas kernels: 54.6 us -> 50.5 us  [the longest x2 40.7 us: attend(): pl.pallas_call(functools.partial(attend_kernel, chunk), in_specs=[scalar,...]
  transfers between devices with their start and end apart: 4 -> 6, of which waited for: 3 -> 4; matrix products, arithmetic and copies ran while one was open for 0% -> 2% of each run, Pallas kernels for 15% -> 17%
where the time goes in v3:
time: 250 us; the launch traced here: 249 us
  waiting for transfers between devices  129 us (52%)
  Pallas kernels  50.5 us (20%)
  blocking collectives  33.3 us (13%)
  starting transfers between devices  32 us (13%)
  local copies, waits for them, and re-layouts  4 us (2%)
    all_to_all x4, waiting for transfers between devices, exchange(): lax.all_to_all(blocks, 'seq', split_axis=0, concat_axis=0, tiled=True)  129 us
    pallas_call x2, Pallas kernels, attend(): pl.pallas_call(functools.partial(attend_kernel, chunk), in_specs=[scalar,...  40.7 us
    all_to_all x1, blocking collectives, exchange(): lax.all_to_all(blocks, 'seq', split_axis=0, concat_axis=0, tiled=True)  33.3 us
    all_to_all x4, starting transfers between devices, exchange(): lax.all_to_all(blocks, 'seq', split_axis=0, concat_axis=0, tiled=True)  26.4 us
  transfers between devices with their start and end apart: 6, of which 4 were waited for; matrix products, arithmetic and copies ran while one was open for 2% of the time, Pallas kernels for 17%

profile of v3, /device:TPU:8, one launch (start us, length us, event | category | flops | bytes accessed | tf_op | source)
XLA Modules:
  0.0 249.2 jit_solution(3083725666436725624)
XLA Ops:
  0.0 4.0 %shard_map.46 = (bf16[32,4,128,128]{3,2,1,0:T(8,128)(2,1)}, s32[2,16,64]{2,1,0:T(8,128)}) custom-call(s32[3,32]{1,0:T(4,128)} %extents.1, s32[16,64]{1,0:T(8,128)} %bitcast.1, bf16[2,256,4096]{2,1,0:T(8,128)(2,1)} %pair_ref.1), custom_call_target="tpu_custom_call" | custom-call | tf_op jit(solution)/shard_map/pallas_call | solution.py:71
  4.0 11.4 %all-to-all-start.1 = ((bf16[32,4,128,128]{3,2,1,0:T(8,128)(2,1)}), bf16[32,4,128,128]{3,2,1,0:T(8,128)(2,1)}, u32[]{:S(2)}, u32[]{:S(2)}) async-start(bf16[32,4,128,128]{3,2,1,0:T(8,128)(2,1)} %get-tuple-element.11), calls=%async_computation.1 | async-start | bytes 8388608 | tf_op jit(solution)/shard_map/all_to_all | solution.py:260
  15.4 2.8 %shard_map.47 = (bf16[32,128,128]{2,1,0:T(8,128)(2,1)}, bf16[32,128,128]{2,1,0:T(8,128)(2,1)}) custom-call(bf16[256,4096]{1,0:T(8,128)(2,1)} %query_ref.1), custom_call_target="tpu_custom_call" | custom-call | bytes 4194304 | tf_op jit(solution)/shard_map/pallas_call | solution.py:31
  18.2 94.4 %all-to-all-done.1.own_hbm = bf16[32,4,128,128]{3,2,1,0:T(8,128)(2,1)} async-done(((bf16[32,4,128,128]{3,2,1,0:T(8,128)(2,1)}), bf16[32,4,128,128]{3,2,1,0:T(8,128)(2,1)}, u32[]{:S(2)}, u32[]{:S(2)}) %all-to-all-start.1) | async-done | bytes 4194336 | tf_op jit(solution)/shard_map/all_to_all | solution.py:260
  112.6 4.9 %all-to-all-start.3 = ((bf16[32,128,128]{2,1,0:T(8,128)(2,1)}), bf16[32,128,128]{2,1,0:T(8,128)(2,1)S(1)}, u32[]{:S(2)}, u32[]{:S(2)}) async-start(bf16[32,128,128]{2,1,0:T(8,128)(2,1)} %get-tuple-element.12), calls=%async_computation.3 | async-start | bytes 2097152 | tf_op jit(solution)/shard_map/all_to_all | solution.py:260
  117.5 4.0 %fusion = (bf16[16,4,128,128]{3,2,1,0:T(8,128)(2,1)S(1)}, bf16[16,4,128,128]{3,2,1,0:T(8,128)(2,1)}) fusion(bf16[32,4,128,128]{3,2,1,0:T(8,128)(2,1)} %all-to-all-done.1.own_hbm), kind=kLoop, calls=%fused_computation | loop fusion | bytes 8388608 | tf_op jit(solution)/shard_map/slice | solution.py:272
  121.5 1.9 collective-permute-start
  123.5 3.6 %collective-permute-start.1 = (bf16[16,4,128,128]{3,2,1,0:T(8,128)(2,1)S(1)}, bf16[16,4,128,128]{3,2,1,0:T(8,128)(2,1)}, u32[]{:S(2)}, u32[]{:S(2)}) collective-permute-start(bf16[16,4,128,128]{3,2,1,0:T(8,128)(2,1)S(1)} %get-tuple-element.13), channel_id=1, source_target_pairs={{32,0},{64,32},{96,64},{128,96},{160,128},{192,160},{224,192},{33,... | collective-permute-start | bytes 6291464 | tf_op jit(solution)/shard_map/ppermute | solution.py:272
  127.1 19.0 %all-to-all-done.3.query_hbm = bf16[32,128,128]{2,1,0:T(8,128)(2,1)S(1)} async-done(((bf16[32,128,128]{2,1,0:T(8,128)(2,1)}), bf16[32,128,128]{2,1,0:T(8,128)(2,1)S(1)}, u32[]{:S(2)}, u32[]{:S(2)}) %all-to-all-start.3) | async-done | bytes 1048608 | tf_op jit(solution)/shard_map/all_to_all | solution.py:260
  146.1 0.0 copy-start.1
  146.1 5.1 %all-to-all-start = ((bf16[32,128,128]{2,1,0:T(8,128)(2,1)}), bf16[32,128,128]{2,1,0:T(8,128)(2,1)}, u32[]{:S(2)}, u32[]{:S(2)}) async-start(bf16[32,128,128]{2,1,0:T(8,128)(2,1)} %get-tuple-element.10), calls=%async_computation | async-start | bytes 2097152 | tf_op jit(solution)/shard_map/all_to_all | solution.py:260
  151.3 0.0 collective-permute-done.left_hbm
  151.3 0.0 collective-permute-done.1.right_hbm
  151.3 0.0 copy-done.1
  151.3 20.4 %shard_map.49 = bf16[32,128,128]{2,1,0:T(8,128)(2,1)} custom-call(s32[2,16,64]{2,1,0:T(8,128)} %get-tuple-element.9.slot_ids, bf16[32,128,128]{2,1,0:T(8,128)(2,1)} %copy-done.1, bf16[16,4,128,128]{3,2,1,0:T(8,128)(2,1)} %collective-permute-done.left_hbm, bf16[32,4,128,128]{3,2,1,0:T(8,128)(2,1)} %all-to-all-done.1.own_hbm, ...), custom_call_target="tpu_custom_call" | custom-call | flops 4294967296 | bytes 12582912 | tf_op jit(solution)/shard_map/pallas_call | solution.py:236
  171.7 7.9 %all-to-all-done.query_hbm = bf16[32,128,128]{2,1,0:T(8,128)(2,1)} async-done(((bf16[32,128,128]{2,1,0:T(8,128)(2,1)}), bf16[32,128,128]{2,1,0:T(8,128)(2,1)}, u32[]{:S(2)}, u32[]{:S(2)}) %all-to-all-start) | async-done | bytes 1048608 | tf_op jit(solution)/shard_map/all_to_all | solution.py:260
  179.6 4.9 %all-to-all-start.4 = ((bf16[32,128,128]{2,1,0:T(8,128)(2,1)}), bf16[32,128,128]{2,1,0:T(8,128)(2,1)S(1)}, u32[]{:S(2)}, u32[]{:S(2)}) async-start(bf16[32,128,128]{2,1,0:T(8,128)(2,1)} %shard_map.49), calls=%async_computation.4 | async-start | bytes 2097152 | tf_op jit(solution)/shard_map/all_to_all | solution.py:260
  184.5 20.3 %shard_map.48 = bf16[32,128,128]{2,1,0:T(8,128)(2,1)} custom-call(s32[2,16,64]{2,1,0:T(8,128)} %get-tuple-element.9.slot_ids, bf16[32,128,128]{2,1,0:T(8,128)(2,1)} %all-to-all-done.query_hbm, bf16[16,4,128,128]{3,2,1,0:T(8,128)(2,1)} %collective-permute-done.left_hbm, bf16[32,4,128,128]{3,2,1,0:T(8,128)(2,1)} %all-to-all-done.1.own_hbm, ...), custom_call_target="tpu_custom_call" | custom-call | flops 4294967296 | bytes 12582912 | tf_op jit(solution)/shard_map/pallas_call | solution.py:236
  204.8 8.0 %all-to-all-done.4.second_hbm = bf16[32,128,128]{2,1,0:T(8,128)(2,1)S(1)} async-done(((bf16[32,128,128]{2,1,0:T(8,128)(2,1)}), bf16[32,128,128]{2,1,0:T(8,128)(2,1)S(1)}, u32[]{:S(2)}, u32[]{:S(2)}) %all-to-all-start.4) | async-done | bytes 1048608 | tf_op jit(solution)/shard_map/all_to_all | solution.py:260
  212.8 0.0 copy-start
  212.8 33.3 %all_to_all.25.first_hbm = bf16[32,128,128]{2,1,0:T(8,128)(2,1)} all-to-all(bf16[32,128,128]{2,1,0:T(8,128)(2,1)} %shard_map.48), channel_id=1, replica_groups=mesh['tm'=8,'seq'=32] {'seq'}, dimensions={0} | all-to-all | bytes 2097152 | tf_op jit(solution)/shard_map/all_to_all | solution.py:260
  246.1 0.0 copy-done
  246.1 3.1 %shard_map.50 = bf16[256,4096]{1,0:T(8,128)(2,1)} custom-call(bf16[32,128,128]{2,1,0:T(8,128)(2,1)} %all_to_all.25.first_hbm, bf16[32,128,128]{2,1,0:T(8,128)(2,1)} %copy-done), custom_call_target="tpu_custom_call" | custom-call | tf_op jit(solution)/shard_map/pallas_call | solution.py:122
Async XLA Ops:
  4.0 108.6 %all-to-all-start.1 = ((bf16[32,4,128,128]{3,2,1,0:T(8,128)(2,1)}), bf16[32,4,128,128]{3,2,1,0:T(8,128)(2,1)}, u32[]{:S(2)}, u32[]{:S(2)}) async-start(bf16[32,4,128,128]{3,2,1,0:T(8,128)(2,1)} %get-tuple-element.11), calls=%async_computation.1 | async-start | bytes 8388608 | tf_op jit(solution)/shard_map/all_to_all | solution.py:260
  112.6 33.5 %all-to-all-start.3 = ((bf16[32,128,128]{2,1,0:T(8,128)(2,1)}), bf16[32,128,128]{2,1,0:T(8,128)(2,1)S(1)}, u32[]{:S(2)}, u32[]{:S(2)}) async-start(bf16[32,128,128]{2,1,0:T(8,128)(2,1)} %get-tuple-element.12), calls=%async_computation.3 | async-start | bytes 2097152 | tf_op jit(solution)/shard_map/all_to_all | solution.py:260
  121.5 29.7 %collective-permute-start = (bf16[16,4,128,128]{3,2,1,0:T(8,128)(2,1)}, bf16[16,4,128,128]{3,2,1,0:T(8,128)(2,1)}, u32[]{:S(2)}, u32[]{:S(2)}) collective-permute-start(bf16[16,4,128,128]{3,2,1,0:T(8,128)(2,1)} %get-tuple-element.14), channel_id=1, source_target_pairs={{0,32},{32,64},{64,96},{96,128},{128,160},{160,192},{192,224},{1,3... | collective-permute-start | bytes 6291464 | tf_op jit(solution)/shard_map/ppermute | solution.py:271
  123.5 27.8 %collective-permute-start.1 = (bf16[16,4,128,128]{3,2,1,0:T(8,128)(2,1)S(1)}, bf16[16,4,128,128]{3,2,1,0:T(8,128)(2,1)}, u32[]{:S(2)}, u32[]{:S(2)}) collective-permute-start(bf16[16,4,128,128]{3,2,1,0:T(8,128)(2,1)S(1)} %get-tuple-element.13), channel_id=1, source_target_pairs={{32,0},{64,32},{96,64},{128,96},{160,128},{192,160},{224,192},{33,... | collective-permute-start | bytes 6291464 | tf_op jit(solution)/shard_map/ppermute | solution.py:272
  146.1 5.2 %copy-start.1 = (bf16[32,128,128]{2,1,0:T(8,128)(2,1)}, bf16[32,128,128]{2,1,0:T(8,128)(2,1)S(1)}, u32[]{:S(2)}) copy-start(bf16[32,128,128]{2,1,0:T(8,128)(2,1)S(1)} %all-to-all-done.3.query_hbm) | copy-start | bytes 3145732
  146.1 33.4 %all-to-all-start = ((bf16[32,128,128]{2,1,0:T(8,128)(2,1)}), bf16[32,128,128]{2,1,0:T(8,128)(2,1)}, u32[]{:S(2)}, u32[]{:S(2)}) async-start(bf16[32,128,128]{2,1,0:T(8,128)(2,1)} %get-tuple-element.10), calls=%async_computation | async-start | bytes 2097152 | tf_op jit(solution)/shard_map/all_to_all | solution.py:260
  179.6 33.2 %all-to-all-start.4 = ((bf16[32,128,128]{2,1,0:T(8,128)(2,1)}), bf16[32,128,128]{2,1,0:T(8,128)(2,1)S(1)}, u32[]{:S(2)}, u32[]{:S(2)}) async-start(bf16[32,128,128]{2,1,0:T(8,128)(2,1)} %shard_map.49), calls=%async_computation.4 | async-start | bytes 2097152 | tf_op jit(solution)/shard_map/all_to_all | solution.py:260
  212.8 33.3 %copy-start = (bf16[32,128,128]{2,1,0:T(8,128)(2,1)}, bf16[32,128,128]{2,1,0:T(8,128)(2,1)S(1)}, u32[]{:S(2)}) copy-start(bf16[32,128,128]{2,1,0:T(8,128)(2,1)S(1)} %all-to-all-done.4.second_hbm) | copy-start | bytes 3145732

commit v4 on v3

--- a/solution.py
+++ b/solution.py
@@ -14,15 +14,17 @@
 CHUNKS = 2
 HEADS_STEP = 16
 NO_TILE = 128
+ALONG_X = 4
+ALONG_Z = 8
 EXP2_SCALE = HEAD_DIM ** (-0.5) * 1.4426950408889634
 MIB = 1024 * 1024
 
 
-def split_queries_kernel(query_ref, *block_refs):
-    for chunk, block_ref in enumerate(block_refs):
-        for head in range(block_ref.shape[0]):
-            columns = slice(head * HEAD_DIM, (head + 1) * HEAD_DIM)
-            block_ref[head] = query_ref[chunk * TILE : (chunk + 1) * TILE, columns]
+def split_queries_kernel(query_ref, block_ref):
+    for head in range(block_ref.shape[0]):
+        columns = slice(head * HEAD_DIM, (head + 1) * HEAD_DIM)
+        for chunk in range(CHUNKS):
+            block_ref[head, chunk] = query_ref[chunk * TILE : (chunk + 1) * TILE, columns]
 
 
 def split_queries(queries):
@@ -32,8 +34,8 @@
         split_queries_kernel,
         grid=(heads // HEADS_STEP,),
         in_specs=[pl.BlockSpec((tok_dev, HEADS_STEP * HEAD_DIM), lambda i: (0, i))],
-        out_specs=[pl.BlockSpec((HEADS_STEP, TILE, HEAD_DIM), lambda i: (i, 0, 0))] * CHUNKS,
-        out_shape=[jax.ShapeDtypeStruct((heads, TILE, HEAD_DIM), jnp.bfloat16)] * CHUNKS,
+        out_specs=pl.BlockSpec((HEADS_STEP, CHUNKS, TILE, HEAD_DIM), lambda i: (i, 0, 0, 0)),
+        out_shape=jax.ShapeDtypeStruct((heads, CHUNKS, TILE, HEAD_DIM), jnp.bfloat16),
         compiler_params=pltpu.CompilerParams(vmem_limit_bytes=60 * MIB),
         cost_estimate=pl.CostEstimate(flops=0, bytes_accessed=4 * MIB, transcendentals=0),
     )(queries)
@@ -170,6 +172,10 @@
     for copy in copies[:4]:
         copy.wait()
     count = query.shape[0]
+    here_x = lax.axis_index("seq") >> 3
+
+    def pair_of(tile):
+        return (((here_x - (tile & 3)) & 3) << 3) + (tile >> 2)
 
     def score_pair(row, tile_query, slot):
         ids = [slot_ids[0, slot + i, row] for i in range(2)]
@@ -192,8 +198,9 @@
         tops[place] = jnp.broadcast_to(jnp.max(best, axis=1, keepdims=True), (TILE, TILE))
 
     best = None
+    first_row = pair_of(0) * CHUNKS + chunk
     for slot in range(0, KSEL, 2):
-        score = score_pair(chunk, query[0], slot)
+        score = score_pair(first_row, query[0], slot)
         scores[0, slot // 2] = score
         best = fold(best, score)
     put_top(0, best)
@@ -204,7 +211,8 @@
         for now in range(2):
             tile = turn * 2 + now
             later = jnp.minimum(tile + 1, count - 1)
-            row, later_row = tile * CHUNKS + chunk, later * CHUNKS + chunk
+            pair = pair_of(tile)
+            row, later_row = pair * CHUNKS + chunk, pair_of(later) * CHUNKS + chunk
             top = tops[now]
             top = jnp.concatenate([top, top], axis=1)
             later_query = query[later]
@@ -222,7 +230,7 @@
                 )
                 mixed = part if mixed is None else mixed + part
             put_top(1 - now, best)
-            out_ref[tile] = (mixed[:, :HEAD_DIM] / mixed[:, HEAD_DIM:]).astype(jnp.bfloat16)
+            out_ref[pair] = (mixed[:, :HEAD_DIM] / mixed[:, HEAD_DIM:]).astype(jnp.bfloat16)
         return carry
 
     lax.fori_loop(0, count // 2, step, 0)
@@ -260,18 +268,48 @@
     return lax.all_to_all(blocks, "seq", split_axis=0, concat_axis=0, tiled=True)
 
 
+def exchange_z(blocks):
+    groups = [[x * ALONG_Z + z for z in range(ALONG_Z)] for x in range(ALONG_X)]
+    return lax.all_to_all(
+        blocks, "seq", split_axis=0, concat_axis=0, tiled=True, axis_index_groups=groups
+    )
+
+
+def shift_x(blocks, by):
+    pairs = [
+        (x * ALONG_Z + z, (x + by) % ALONG_X * ALONG_Z + z)
+        for x in range(ALONG_X)
+        for z in range(ALONG_Z)
+    ]
+    return lax.ppermute(blocks, "seq", pairs)
+
+
+def queries_by_x(queries):
+    blocks = split_queries(queries)
+    x = lax.axis_index("seq") // ALONG_Z
+    parts = []
+    for by in range(ALONG_X):
+        start = (x + by) % ALONG_X * ALONG_Z
+        part = lax.dynamic_slice_in_dim(blocks, start, ALONG_Z, axis=0)
+        parts.append(shift_x(part, by) if by else part)
+    return [
+        jnp.stack([part[:, chunk] for part in parts], axis=1).reshape(-1, TILE, HEAD_DIM)
+        for chunk in range(CHUNKS)
+    ]
+
+
 def per_device(queries, keys_values, extents, tile_lists):
     seq_size = lax.axis_size("seq")
     tm_size = lax.axis_size("tm")
     blocks, ids = split_pairs(keys_values, extents, tile_lists)
-    first, second = split_queries(queries)
+    first, second = queries_by_x(queries)
     own = exchange(blocks)
     half = seq_size // 2
     ends = tm_size - 1
     left = lax.ppermute(own[half:], "tm", [(i, i + 1) for i in range(ends)])
     right = lax.ppermute(own[:half], "tm", [(i + 1, i) for i in range(ends)])
-    first = exchange(first)
-    second = exchange(second)
+    first = exchange_z(first)
+    second = exchange_z(second)
     first_out = exchange(attend(0, ids, first, left, own, right))
     second_out = exchange(attend(1, ids, second, left, own, right))
     return join_heads(first_out, second_out)

time: 250 us -> 248 us (level)
  waiting for transfers between devices: 129 us -> 118 us
  local copies, waits for them, and re-layouts: 4 us -> 8.86 us
    all_to_all x4 -> x2, waiting for transfers between devices: 129 us -> 48 us  [exchange(): lax.all_to_all(blocks, 'seq', split_axis=0, concat_axis=0, tiled=True)]
    ppermute x0 -> x3, waiting for transfers between devices: none -> 43 us  [shift_x(): return lax.ppermute(blocks, 'seq', pairs)]
    all_to_all x0 -> x2, waiting for transfers between devices: none -> 25.6 us  [exchange_z(): lax.all_to_all(blocks, 'seq', split_axis=0, concat_axis=0, tiled=True, ax...]
    all_to_all x4 -> x2, starting transfers between devices: 26.4 us -> 16.2 us  [exchange(): lax.all_to_all(blocks, 'seq', split_axis=0, concat_axis=0, tiled=True)]
    all_to_all x0 -> x2, starting transfers between devices: none -> 7.8 us  [exchange_z(): lax.all_to_all(blocks, 'seq', split_axis=0, concat_axis=0, tiled=True, ax...]
    ppermute x0 -> x3, starting transfers between devices: none -> 5.33 us  [shift_x(): return lax.ppermute(blocks, 'seq', pairs)]
    slice x0 -> x4, local copies, waits for them, and re-layouts: none -> 3.32 us  [queries_by_x(): part[:, chunk]]
  transfers between devices with their start and end apart: 6 -> 9, of which waited for: 4 -> 7; matrix products, arithmetic and copies ran while one was open for 2% -> 5% of each run, Pallas kernels for 17% -> 18%
where the time goes in v4:
time: 248 us; the launch traced here: 247 us
  waiting for transfers between devices  118 us (48%)
  Pallas kernels  50.5 us (20%)
  starting transfers between devices  33.6 us (14%)
  blocking collectives  33.5 us (14%)
  local copies, waits for them, and re-layouts  8.86 us (4%)
    all_to_all x2, waiting for transfers between devices, exchange(): lax.all_to_all(blocks, 'seq', split_axis=0, concat_axis=0, tiled=True)  48 us
    ppermute x3, waiting for transfers between devices, shift_x(): return lax.ppermute(blocks, 'seq', pairs)  43 us
    pallas_call x2, Pallas kernels, attend(): pl.pallas_call(functools.partial(attend_kernel, chunk), in_specs=[scalar,...  40.7 us
    all_to_all x1, blocking collectives, exchange(): lax.all_to_all(blocks, 'seq', split_axis=0, concat_axis=0, tiled=True)  33.5 us
    all_to_all x2, waiting for transfers between devices, exchange_z(): lax.all_to_all(blocks, 'seq', split_axis=0, concat_axis=0, tiled=True, ax...  25.6 us
    all_to_all x2, starting transfers between devices, exchange(): lax.all_to_all(blocks, 'seq', split_axis=0, concat_axis=0, tiled=True)  16.2 us
    all_to_all x2, starting transfers between devices, exchange_z(): lax.all_to_all(blocks, 'seq', split_axis=0, concat_axis=0, tiled=True, ax...  7.8 us
    ppermute x3, starting transfers between devices, shift_x(): return lax.ppermute(blocks, 'seq', pairs)  5.33 us
  transfers between devices with their start and end apart: 9, of which 7 were waited for; matrix products, arithmetic and copies ran while one was open for 5% of the time, Pallas kernels for 18%

profile of v4, /device:TPU:8, one launch (start us, length us, event | category | flops | bytes accessed | tf_op | source)
XLA Modules:
  0.0 247.1 jit_solution(18096322648809683387)
XLA Ops:
  0.0 4.0 %shard_map.46 = (bf16[32,4,128,128]{3,2,1,0:T(8,128)(2,1)}, s32[2,16,64]{2,1,0:T(8,128)}) custom-call(s32[3,32]{1,0:T(4,128)} %extents.1, s32[16,64]{1,0:T(8,128)} %bitcast.3, bf16[2,256,4096]{2,1,0:T(8,128)(2,1)} %pair_ref.1), custom_call_target="tpu_custom_call" | custom-call | tf_op jit(solution)/shard_map/pallas_call | solution.py:73
  4.0 11.4 %all-to-all-start.1 = ((bf16[32,4,128,128]{3,2,1,0:T(8,128)(2,1)}), bf16[32,4,128,128]{3,2,1,0:T(8,128)(2,1)}, u32[]{:S(2)}, u32[]{:S(2)}) async-start(bf16[32,4,128,128]{3,2,1,0:T(8,128)(2,1)} %get-tuple-element.8), calls=%async_computation.1 | async-start | bytes 8388608 | tf_op jit(solution)/shard_map/all_to_all | solution.py:268
  15.5 2.7 %shard_map.47 = bf16[32,2,128,128]{3,2,1,0:T(8,128)(2,1)} custom-call(bf16[256,4096]{1,0:T(8,128)(2,1)} %query_ref.1), custom_call_target="tpu_custom_call" | custom-call | bytes 4194304 | tf_op jit(solution)/shard_map/pallas_call | solution.py:33
  18.3 1.5 constant_dynamic-slice_fusion.3
  19.7 1.8 collective-permute-start
  21.5 1.5 collective-permute-start.2
  23.0 2.0 collective-permute-start.1
  25.0 1.1 constant_dynamic-slice_fusion.4
  26.1 23.7 %collective-permute-done = bf16[8,2,128,128]{3,2,1,0:T(8,128)(2,1)S(1)} collective-permute-done((bf16[8,2,128,128]{3,2,1,0:T(8,128)(2,1)S(1)}, bf16[8,2,128,128]{3,2,1,0:T(8,128)(2,1)S(1)}, u32[]{:S(2)}, u32[]{:S(2)}) %collective-permute-start) | collective-permute-done | bytes 524320 | tf_op jit(solution)/shard_map/ppermute | solution.py:284
  49.8 0.8 fusion.1
  50.6 0.0 collective-permute-done.2
  50.6 0.8 fusion.3
  51.3 19.3 %collective-permute-done.1 = bf16[8,2,128,128]{3,2,1,0:T(8,128)(2,1)S(1)} collective-permute-done((bf16[8,2,128,128]{3,2,1,0:T(8,128)(2,1)S(1)}, bf16[8,2,128,128]{3,2,1,0:T(8,128)(2,1)S(1)}, u32[]{:S(2)}, u32[]{:S(2)}) %collective-permute-start.1) | collective-permute-done | bytes 524320 | tf_op jit(solution)/shard_map/ppermute | solution.py:284
  70.6 0.7 fusion.2
  71.4 1.2 pad_maximum_fusion
  72.6 39.6 %all-to-all-done.1.own_hbm = bf16[32,4,128,128]{3,2,1,0:T(8,128)(2,1)} async-done(((bf16[32,4,128,128]{3,2,1,0:T(8,128)(2,1)}), bf16[32,4,128,128]{3,2,1,0:T(8,128)(2,1)}, u32[]{:S(2)}, u32[]{:S(2)}) %all-to-all-start.1) | async-done | bytes 4194336 | tf_op jit(solution)/shard_map/all_to_all | solution.py:268
  112.2 3.6 %all-to-all-start = ((bf16[32,128,128]{2,1,0:T(8,128)(2,1)}), bf16[32,128,128]{2,1,0:T(8,128)(2,1)S(1)}, u32[]{:S(2)}, u32[]{:S(2)}) async-start(bf16[32,128,128]{2,1,0:T(8,128)(2,1)} %bitcast.1), calls=%async_computation | async-start | bytes 2097152 | tf_op jit(solution)/shard_map/all_to_all | solution.py:273
  115.8 4.1 %fusion = (bf16[16,4,128,128]{3,2,1,0:T(8,128)(2,1)}, bf16[16,4,128,128]{3,2,1,0:T(8,128)(2,1)S(1)}) fusion(bf16[32,4,128,128]{3,2,1,0:T(8,128)(2,1)} %all-to-all-done.1.own_hbm), kind=kLoop, calls=%fused_computation.7 | loop fusion | bytes 8388608 | tf_op jit(solution)/shard_map/slice | solution.py:310
  119.9 1.9 collective-permute-start.4
  121.8 2.4 collective-permute-start.3
  124.2 1.1 pad_maximum_fusion.1
  125.3 18.2 %all-to-all-done.query_hbm = bf16[32,128,128]{2,1,0:T(8,128)(2,1)S(1)} async-done(((bf16[32,128,128]{2,1,0:T(8,128)(2,1)}), bf16[32,128,128]{2,1,0:T(8,128)(2,1)S(1)}, u32[]{:S(2)}, u32[]{:S(2)}) %all-to-all-start) | async-done | bytes 1048608 | tf_op jit(solution)/shard_map/all_to_all | solution.py:273
  143.5 4.2 %all-to-all-start.3 = ((bf16[32,128,128]{2,1,0:T(8,128)(2,1)}), bf16[32,128,128]{2,1,0:T(8,128)(2,1)}, u32[]{:S(2)}, u32[]{:S(2)}) async-start(bf16[32,128,128]{2,1,0:T(8,128)(2,1)} %bitcast.2), calls=%async_computation.3 | async-start | bytes 2097152 | tf_op jit(solution)/shard_map/all_to_all | solution.py:273
  147.8 0.0 collective-permute-done.4.right_hbm
  147.8 1.4 collective-permute-done.3.left_hbm
  149.2 20.3 %shard_map.48 = bf16[32,128,128]{2,1,0:T(8,128)(2,1)} custom-call(s32[2,16,64]{2,1,0:T(8,128)} %get-tuple-element.7.slot_ids, bf16[32,128,128]{2,1,0:T(8,128)(2,1)} %copy-done.1, bf16[16,4,128,128]{3,2,1,0:T(8,128)(2,1)} %collective-permute-done.3.left_hbm, bf16[32,4,128,128]{3,2,1,0:T(8,128)(2,1)} %all-to-all-done.1.own_hbm, ...), custom_call_target="tpu_custom_call" | custom-call | flops 4294967296 | bytes 12582912 | tf_op jit(solution)/shard_map/pallas_call | solution.py:244
  169.6 7.4 %all-to-all-done.3.query_hbm = bf16[32,128,128]{2,1,0:T(8,128)(2,1)} async-done(((bf16[32,128,128]{2,1,0:T(8,128)(2,1)}), bf16[32,128,128]{2,1,0:T(8,128)(2,1)}, u32[]{:S(2)}, u32[]{:S(2)}) %all-to-all-start.3) | async-done | bytes 1048608 | tf_op jit(solution)/shard_map/all_to_all | solution.py:273
  177.0 4.7 %all-to-all-start.2 = ((bf16[32,128,128]{2,1,0:T(8,128)(2,1)}), bf16[32,128,128]{2,1,0:T(8,128)(2,1)S(1)}, u32[]{:S(2)}, u32[]{:S(2)}) async-start(bf16[32,128,128]{2,1,0:T(8,128)(2,1)} %shard_map.48), calls=%async_computation.2 | async-start | bytes 2097152 | tf_op jit(solution)/shard_map/all_to_all | solution.py:268
  181.7 20.4 %shard_map.49 = bf16[32,128,128]{2,1,0:T(8,128)(2,1)} custom-call(s32[2,16,64]{2,1,0:T(8,128)} %get-tuple-element.7.slot_ids, bf16[32,128,128]{2,1,0:T(8,128)(2,1)} %all-to-all-done.3.query_hbm, bf16[16,4,128,128]{3,2,1,0:T(8,128)(2,1)} %collective-permute-done.3.left_hbm, bf16[32,4,128,128]{3,2,1,0:T(8,128)(2,1)} %all-to-all-done.1.own_hbm, ...), custom_call_target="tpu_custom_call" | custom-call | flops 4294967296 | bytes 12582912 | tf_op jit(solution)/shard_map/pallas_call | solution.py:244
  202.2 8.4 %all-to-all-done.2.first_hbm = bf16[32,128,128]{2,1,0:T(8,128)(2,1)S(1)} async-done(((bf16[32,128,128]{2,1,0:T(8,128)(2,1)}), bf16[32,128,128]{2,1,0:T(8,128)(2,1)S(1)}, u32[]{:S(2)}, u32[]{:S(2)}) %all-to-all-start.2) | async-done | bytes 1048608 | tf_op jit(solution)/shard_map/all_to_all | solution.py:268
  210.5 33.5 %all_to_all.25.second_hbm = bf16[32,128,128]{2,1,0:T(8,128)(2,1)} all-to-all(bf16[32,128,128]{2,1,0:T(8,128)(2,1)} %shard_map.49), channel_id=1, replica_groups=mesh['tm'=8,'seq'=32] {'seq'}, dimensions={0} | all-to-all | bytes 2097152 | tf_op jit(solution)/shard_map/all_to_all | solution.py:268
  244.1 3.1 %shard_map.50 = bf16[256,4096]{1,0:T(8,128)(2,1)} custom-call(bf16[32,128,128]{2,1,0:T(8,128)(2,1)} %copy-done, bf16[32,128,128]{2,1,0:T(8,128)(2,1)} %all_to_all.25.second_hbm), custom_call_target="tpu_custom_call" | custom-call | tf_op jit(solution)/shard_map/pallas_call | solution.py:124
  (10 shorter events, 0.0 us)
Async XLA Ops:
  4.0 108.2 %all-to-all-start.1 = ((bf16[32,4,128,128]{3,2,1,0:T(8,128)(2,1)}), bf16[32,4,128,128]{3,2,1,0:T(8,128)(2,1)}, u32[]{:S(2)}, u32[]{:S(2)}) async-start(bf16[32,4,128,128]{3,2,1,0:T(8,128)(2,1)} %get-tuple-element.8), calls=%async_computation.1 | async-start | bytes 8388608 | tf_op jit(solution)/shard_map/all_to_all | solution.py:268
  19.7 30.1 %collective-permute-start = (bf16[8,2,128,128]{3,2,1,0:T(8,128)(2,1)S(1)}, bf16[8,2,128,128]{3,2,1,0:T(8,128)(2,1)S(1)}, u32[]{:S(2)}, u32[]{:S(2)}) collective-permute-start(bf16[8,2,128,128]{3,2,1,0:T(8,128)(2,1)S(1)} %get-tuple-element.13), channel_id=1, source_target_pairs={{0,8},{1,9},{2,10},{3,11},{4,12},{5,13},{6,14},{7,15},{8,16},{9,17... | collective-permute-start | bytes 1572872 | tf_op jit(solution)/shard_map/ppermute | solution.py:284
  21.5 29.1 %collective-permute-start.2 = (bf16[8,2,128,128]{3,2,1,0:T(8,128)(2,1)S(1)}, bf16[8,2,128,128]{3,2,1,0:T(8,128)(2,1)S(1)}, u32[]{:S(2)}, u32[]{:S(2)}) collective-permute-start(bf16[8,2,128,128]{3,2,1,0:T(8,128)(2,1)S(1)} %get-tuple-element.14), channel_id=1, source_target_pairs={{0,24},{1,25},{2,26},{3,27},{4,28},{5,29},{6,30},{7,31},{8,0},{9,1... | collective-permute-start | bytes 1572872 | tf_op jit(solution)/shard_map/ppermute | solution.py:284
  23.0 47.6 %collective-permute-start.1 = (bf16[8,2,128,128]{3,2,1,0:T(8,128)(2,1)S(1)}, bf16[8,2,128,128]{3,2,1,0:T(8,128)(2,1)S(1)}, u32[]{:S(2)}, u32[]{:S(2)}) collective-permute-start(bf16[8,2,128,128]{3,2,1,0:T(8,128)(2,1)S(1)} %get-tuple-element.15), channel_id=1, source_target_pairs={{0,16},{1,17},{2,18},{3,19},{4,20},{5,21},{6,22},{7,23},{8,24},{9,... | collective-permute-start | bytes 1572872 | tf_op jit(solution)/shard_map/ppermute | solution.py:284
  112.2 31.3 %all-to-all-start = ((bf16[32,128,128]{2,1,0:T(8,128)(2,1)}), bf16[32,128,128]{2,1,0:T(8,128)(2,1)S(1)}, u32[]{:S(2)}, u32[]{:S(2)}) async-start(bf16[32,128,128]{2,1,0:T(8,128)(2,1)} %bitcast.1), calls=%async_computation | async-start | bytes 2097152 | tf_op jit(solution)/shard_map/all_to_all | solution.py:273
  115.8 8.4 %copy-start.2 = (bf16[8,1,128,128]{3,2,1,0:T(8,128)(2,1)S(1)}, bf16[8,1,128,128]{3,2,1,0:T(8,128)(2,1)}, u32[]{:S(2)}) copy-start(bf16[8,1,128,128]{3,2,1,0:T(8,128)(2,1)} %get-tuple-element.16) | copy-start | bytes 786436
  115.8 8.4 %copy-start.3 = (bf16[8,1,128,128]{3,2,1,0:T(8,128)(2,1)S(1)}, bf16[8,1,128,128]{3,2,1,0:T(8,128)(2,1)}, u32[]{:S(2)}) copy-start(bf16[8,1,128,128]{3,2,1,0:T(8,128)(2,1)} %get-tuple-element.20) | copy-start | bytes 786436
  115.8 8.4 %copy-start.4 = (bf16[8,1,128,128]{3,2,1,0:T(8,128)(2,1)S(1)}, bf16[8,1,128,128]{3,2,1,0:T(8,128)(2,1)}, u32[]{:S(2)}) copy-start(bf16[8,1,128,128]{3,2,1,0:T(8,128)(2,1)} %get-tuple-element.18) | copy-start | bytes 786436
  119.9 27.9 %collective-permute-start.4 = (bf16[16,4,128,128]{3,2,1,0:T(8,128)(2,1)}, bf16[16,4,128,128]{3,2,1,0:T(8,128)(2,1)}, u32[]{:S(2)}, u32[]{:S(2)}) collective-permute-start(bf16[16,4,128,128]{3,2,1,0:T(8,128)(2,1)} %get-tuple-element.9), channel_id=1, source_target_pairs={{32,0},{64,32},{96,64},{128,96},{160,128},{192,160},{224,192},{33,... | collective-permute-start | bytes 6291464 | tf_op jit(solution)/shard_map/ppermute | solution.py:310
  121.8 27.5 %collective-permute-start.3 = (bf16[16,4,128,128]{3,2,1,0:T(8,128)(2,1)S(1)}, bf16[16,4,128,128]{3,2,1,0:T(8,128)(2,1)}, u32[]{:S(2)}, u32[]{:S(2)}) collective-permute-start(bf16[16,4,128,128]{3,2,1,0:T(8,128)(2,1)S(1)} %get-tuple-element.10), channel_id=1, source_target_pairs={{0,32},{32,64},{64,96},{96,128},{128,160},{160,192},{192,224},{1,3... | collective-permute-start | bytes 6291464 | tf_op jit(solution)/shard_map/ppermute | solution.py:309
  143.5 5.7 %copy-start.1 = (bf16[32,128,128]{2,1,0:T(8,128)(2,1)}, bf16[32,128,128]{2,1,0:T(8,128)(2,1)S(1)}, u32[]{:S(2)}) copy-start(bf16[32,128,128]{2,1,0:T(8,128)(2,1)S(1)} %all-to-all-done.query_hbm) | copy-start | bytes 3145732
  143.5 33.5 %all-to-all-start.3 = ((bf16[32,128,128]{2,1,0:T(8,128)(2,1)}), bf16[32,128,128]{2,1,0:T(8,128)(2,1)}, u32[]{:S(2)}, u32[]{:S(2)}) async-start(bf16[32,128,128]{2,1,0:T(8,128)(2,1)} %bitcast.2), calls=%async_computation.3 | async-start | bytes 2097152 | tf_op jit(solution)/shard_map/all_to_all | solution.py:273
  177.0 33.5 %all-to-all-start.2 = ((bf16[32,128,128]{2,1,0:T(8,128)(2,1)}), bf16[32,128,128]{2,1,0:T(8,128)(2,1)S(1)}, u32[]{:S(2)}, u32[]{:S(2)}) async-start(bf16[32,128,128]{2,1,0:T(8,128)(2,1)} %shard_map.48), calls=%async_computation.2 | async-start | bytes 2097152 | tf_op jit(solution)/shard_map/all_to_all | solution.py:268
  210.5 33.5 %copy-start = (bf16[32,128,128]{2,1,0:T(8,128)(2,1)}, bf16[32,128,128]{2,1,0:T(8,128)(2,1)S(1)}, u32[]{:S(2)}) copy-start(bf16[32,128,128]{2,1,0:T(8,128)(2,1)S(1)} %all-to-all-done.2.first_hbm) | copy-start | bytes 3145732

commit v5 on v4

--- a/solution.py
+++ b/solution.py
@@ -90,49 +90,41 @@
     )(extents, tile_lists.T, keys_values)
 
 
-def join_kernel(first_hbm, second_hbm, out_hbm, held, in_sems, out_sems):
-    sources = (first_hbm, second_hbm)
+def join_kernel(chunk, source_hbm, *refs):
+    out_hbm, held, in_sems, out_sem = refs[-4:]
     reads = [
-        [
-            pltpu.make_async_copy(
-                source.at[head],
-                held.at[pl.ds(chunk * TILE, TILE), pl.ds(head * HEAD_DIM, HEAD_DIM)],
-                in_sems.at[chunk, head],
-            )
-            for head in range(source.shape[0])
-        ]
-        for chunk, source in enumerate(sources)
+        pltpu.make_async_copy(
+            source_hbm.at[head], held.at[:, pl.ds(head * HEAD_DIM, HEAD_DIM)], in_sems.at[head]
+        )
+        for head in range(source_hbm.shape[0])
     ]
-    for copies in reads:
-        for copy in copies:
-            copy.start()
-    writes = []
-    for chunk, copies in enumerate(reads):
-        for copy in copies:
-            copy.wait()
-        rows = pl.ds(chunk * TILE, TILE)
-        writes.append(pltpu.make_async_copy(held.at[rows], out_hbm.at[rows], out_sems.at[chunk]))
-        writes[-1].start()
-    for copy in writes:
+    for copy in reads:
+        copy.start()
+    for copy in reads:
         copy.wait()
-
-
-def join_heads(first, second):
-    heads = first.shape[0]
+    write = pltpu.make_async_copy(held, out_hbm.at[pl.ds(chunk * TILE, TILE)], out_sem)
+    write.start()
+    write.wait()
+
+
+def join_heads(chunk, source, *joined):
+    heads = source.shape[0]
+    width = heads * HEAD_DIM
     whole = pl.BlockSpec(memory_space=pl.ANY)
-    shape = (CHUNKS * TILE, heads * HEAD_DIM)
     return pl.pallas_call(
-        join_kernel,
-        in_specs=[whole, whole],
+        functools.partial(join_kernel, chunk),
+        in_specs=[whole] * (1 + len(joined)),
         out_specs=whole,
-        out_shape=jax.ShapeDtypeStruct(shape, jnp.bfloat16),
+        out_shape=jax.ShapeDtypeStruct((CHUNKS * TILE, width), jnp.bfloat16),
+        input_output_aliases={1: 0} if joined else {},
         scratch_shapes=[
-            pltpu.VMEM(shape, jnp.bfloat16),
-            pltpu.SemaphoreType.DMA((CHUNKS, heads)),
-            pltpu.SemaphoreType.DMA((CHUNKS,)),
-        ],
-        compiler_params=pltpu.CompilerParams(vmem_limit_bytes=60 * MIB),
-    )(first, second)
+            pltpu.VMEM((TILE, width), jnp.bfloat16),
+            pltpu.SemaphoreType.DMA((heads,)),
+            pltpu.SemaphoreType.DMA,
+        ],
+        compiler_params=pltpu.CompilerParams(vmem_limit_bytes=8 * MIB),
+        cost_estimate=pl.CostEstimate(flops=0, bytes_accessed=4 * MIB, transcendentals=0),
+    )(source, *joined)
 
 
 def attend_kernel(
@@ -255,7 +247,7 @@
             pltpu.VMEM((2, TILE, TILE), jnp.float32),
             pltpu.SemaphoreType.DMA((7,)),
         ],
-        compiler_params=pltpu.CompilerParams(vmem_limit_bytes=60 * MIB),
+        compiler_params=pltpu.CompilerParams(vmem_limit_bytes=16 * MIB),
         cost_estimate=pl.CostEstimate(
             flops=count * KSEL * TILE * TILE * HEAD_DIM * 4,
             bytes_accessed=12 * MIB,
@@ -312,7 +304,7 @@
     second = exchange_z(second)
     first_out = exchange(attend(0, ids, first, left, own, right))
     second_out = exchange(attend(1, ids, second, left, own, right))
-    return join_heads(first_out, second_out)
+    return join_heads(1, second_out, join_heads(0, first_out))
 
 
 def solution(mesh):

time: 248 us -> 245 us (0.988)
  blocking collectives: 33.5 us -> 0 us
  waiting for transfers between devices: 118 us -> 146 us
  starting transfers between devices: 33.6 us -> 38 us
    all_to_all x1 -> x0, blocking collectives: 33.5 us -> none  [exchange(): lax.all_to_all(blocks, 'seq', split_axis=0, concat_axis=0, tiled=True)]
    all_to_all x2 -> x3, waiting for transfers between devices: 48 us -> 75.8 us  [exchange(): lax.all_to_all(blocks, 'seq', split_axis=0, concat_axis=0, tiled=True)]
    all_to_all x2 -> x3, starting transfers between devices: 16.2 us -> 21.3 us  [exchange(): lax.all_to_all(blocks, 'seq', split_axis=0, concat_axis=0, tiled=True)]
  transfers between devices with their start and end apart: 9 -> 10, of which waited for: 7 -> 8; matrix products, arithmetic and copies ran while one was open for 5% -> 4% of each run, Pallas kernels for 18% -> 18%
where the time goes in v5:
time: 245 us
  waiting for transfers between devices  146 us (60%)
  Pallas kernels  50 us (20%)
  starting transfers between devices  38 us (16%)
  local copies, waits for them, and re-layouts  8.59 us (4%)
    all_to_all x3, waiting for transfers between devices, exchange(): lax.all_to_all(blocks, 'seq', split_axis=0, concat_axis=0, tiled=True)  75.8 us
    ppermute x3, waiting for transfers between devices, shift_x(): return lax.ppermute(blocks, 'seq', pairs)  43.4 us
    pallas_call x2, Pallas kernels, attend(): pl.pallas_call(functools.partial(attend_kernel, chunk), in_specs=[scalar,...  40.1 us
    all_to_all x2, waiting for transfers between devices, exchange_z(): lax.all_to_all(blocks, 'seq', split_axis=0, concat_axis=0, tiled=True, ax...  23.4 us
    all_to_all x3, starting transfers between devices, exchange(): lax.all_to_all(blocks, 'seq', split_axis=0, concat_axis=0, tiled=True)  21.3 us
    all_to_all x2, starting transfers between devices, exchange_z(): lax.all_to_all(blocks, 'seq', split_axis=0, concat_axis=0, tiled=True, ax...  7.11 us
    ppermute x3, starting transfers between devices, shift_x(): return lax.ppermute(blocks, 'seq', pairs)  5.33 us
  transfers between devices with their start and end apart: 10, of which 8 were waited for; matrix products, arithmetic and copies ran while one was open for 4% of the time, Pallas kernels for 18%

profile of v5, /device:TPU:8, one launch (start us, length us, event | category | flops | bytes accessed | tf_op | source)
XLA Modules:
  0.0 244.8 jit_solution(2443700383079773617)
XLA Ops:
  0.0 4.0 %shard_map.46 = (bf16[32,4,128,128]{3,2,1,0:T(8,128)(2,1)}, s32[2,16,64]{2,1,0:T(8,128)}) custom-call(s32[3,32]{1,0:T(4,128)} %extents.1, s32[16,64]{1,0:T(8,128)} %bitcast.3, bf16[2,256,4096]{2,1,0:T(8,128)(2,1)} %pair_ref.1), custom_call_target="tpu_custom_call" | custom-call | tf_op jit(solution)/shard_map/pallas_call | solution.py:73
  4.0 11.4 %all-to-all-start.1 = ((bf16[32,4,128,128]{3,2,1,0:T(8,128)(2,1)}), bf16[32,4,128,128]{3,2,1,0:T(8,128)(2,1)}, u32[]{:S(2)}, u32[]{:S(2)}) async-start(bf16[32,4,128,128]{3,2,1,0:T(8,128)(2,1)} %get-tuple-element.8), calls=%async_computation.1 | async-start | bytes 8388608 | tf_op jit(solution)/shard_map/all_to_all | solution.py:260
  15.5 2.7 %shard_map.47 = bf16[32,2,128,128]{3,2,1,0:T(8,128)(2,1)} custom-call(bf16[256,4096]{1,0:T(8,128)(2,1)} %query_ref.1), custom_call_target="tpu_custom_call" | custom-call | bytes 4194304 | tf_op jit(solution)/shard_map/pallas_call | solution.py:33
  18.3 1.5 constant_dynamic-slice_fusion.3
  19.7 1.8 collective-permute-start
  21.5 1.5 collective-permute-start.2
  23.1 2.0 collective-permute-start.1
  25.1 1.1 constant_dynamic-slice_fusion.4
  26.1 23.8 %collective-permute-done = bf16[8,2,128,128]{3,2,1,0:T(8,128)(2,1)} collective-permute-done((bf16[8,2,128,128]{3,2,1,0:T(8,128)(2,1)S(1)}, bf16[8,2,128,128]{3,2,1,0:T(8,128)(2,1)}, u32[]{:S(2)}, u32[]{:S(2)}) %collective-permute-start) | collective-permute-done | bytes 524320 | tf_op jit(solution)/shard_map/ppermute | solution.py:276
  49.9 1.1 fusion.1
  51.0 0.0 collective-permute-done.2
  51.1 19.6 %collective-permute-done.1 = bf16[8,2,128,128]{3,2,1,0:T(8,128)(2,1)S(1)} collective-permute-done((bf16[8,2,128,128]{3,2,1,0:T(8,128)(2,1)S(1)}, bf16[8,2,128,128]{3,2,1,0:T(8,128)(2,1)S(1)}, u32[]{:S(2)}, u32[]{:S(2)}) %collective-permute-start.1) | collective-permute-done | bytes 524320 | tf_op jit(solution)/shard_map/ppermute | solution.py:276
  70.7 1.1 pad_maximum_fusion.1
  71.8 40.4 %all-to-all-done.1.own_hbm = bf16[32,4,128,128]{3,2,1,0:T(8,128)(2,1)} async-done(((bf16[32,4,128,128]{3,2,1,0:T(8,128)(2,1)}), bf16[32,4,128,128]{3,2,1,0:T(8,128)(2,1)}, u32[]{:S(2)}, u32[]{:S(2)}) %all-to-all-start.1) | async-done | bytes 4194336 | tf_op jit(solution)/shard_map/all_to_all | solution.py:260
  112.2 3.6 %all-to-all-start.3 = ((bf16[32,128,128]{2,1,0:T(8,128)(2,1)}), bf16[32,128,128]{2,1,0:T(8,128)(2,1)S(1)}, u32[]{:S(2)}, u32[]{:S(2)}) async-start(bf16[32,128,128]{2,1,0:T(8,128)(2,1)} %bitcast.2), calls=%async_computation.3 | async-start | bytes 2097152 | tf_op jit(solution)/shard_map/all_to_all | solution.py:265
  115.8 4.9 %fusion = (bf16[16,4,128,128]{3,2,1,0:T(8,128)(2,1)}, bf16[16,4,128,128]{3,2,1,0:T(8,128)(2,1)}) fusion(bf16[32,4,128,128]{3,2,1,0:T(8,128)(2,1)} %all-to-all-done.1.own_hbm), kind=kLoop, calls=%fused_computation.7 | loop fusion | bytes 8388608 | tf_op jit(solution)/shard_map/slice | solution.py:302
  120.7 1.9 collective-permute-start.4
  122.6 2.4 collective-permute-start.3
  125.0 1.1 pad_maximum_fusion
  126.1 17.4 %all-to-all-done.3.query_hbm = bf16[32,128,128]{2,1,0:T(8,128)(2,1)S(1)} async-done(((bf16[32,128,128]{2,1,0:T(8,128)(2,1)}), bf16[32,128,128]{2,1,0:T(8,128)(2,1)S(1)}, u32[]{:S(2)}, u32[]{:S(2)}) %all-to-all-start.3) | async-done | bytes 1048608 | tf_op jit(solution)/shard_map/all_to_all | solution.py:265
  143.5 3.6 %all-to-all-start = ((bf16[32,128,128]{2,1,0:T(8,128)(2,1)}), bf16[32,128,128]{2,1,0:T(8,128)(2,1)S(1)}, u32[]{:S(2)}, u32[]{:S(2)}) async-start(bf16[32,128,128]{2,1,0:T(8,128)(2,1)} %bitcast.1), calls=%async_computation | async-start | bytes 2097152 | tf_op jit(solution)/shard_map/all_to_all | solution.py:265
  147.1 0.0 collective-permute-done.4.right_hbm
  147.1 3.1 %collective-permute-done.3.left_hbm = bf16[16,4,128,128]{3,2,1,0:T(8,128)(2,1)} collective-permute-done((bf16[16,4,128,128]{3,2,1,0:T(8,128)(2,1)}, bf16[16,4,128,128]{3,2,1,0:T(8,128)(2,1)}, u32[]{:S(2)}, u32[]{:S(2)}) %collective-permute-start.3) | collective-permute-done | bytes 2097184 | tf_op jit(solution)/shard_map/ppermute | solution.py:301
  150.2 20.0 %shard_map.49 = bf16[32,128,128]{2,1,0:T(8,128)(2,1)} custom-call(s32[2,16,64]{2,1,0:T(8,128)S(1)} %copy-done, bf16[32,128,128]{2,1,0:T(8,128)(2,1)S(1)} %all-to-all-done.3.query_hbm, bf16[16,4,128,128]{3,2,1,0:T(8,128)(2,1)} %collective-permute-done.3.left_hbm, bf16[32,4,128,128]{3,2,1,0:T(8,128)(2,1)} %all-to-all-done.1.own_hbm, ...), custom_call_target="tpu_custom_call" | custom-call | flops 4294967296 | bytes 12582912 | tf_op jit(solution)/shard_map/pallas_call | solution.py:236
  170.2 6.0 %all-to-all-done.query_hbm = bf16[32,128,128]{2,1,0:T(8,128)(2,1)S(1)} async-done(((bf16[32,128,128]{2,1,0:T(8,128)(2,1)}), bf16[32,128,128]{2,1,0:T(8,128)(2,1)S(1)}, u32[]{:S(2)}, u32[]{:S(2)}) %all-to-all-start) | async-done | bytes 1048608 | tf_op jit(solution)/shard_map/all_to_all | solution.py:265
  176.2 4.7 %all-to-all-start.4 = ((bf16[32,128,128]{2,1,0:T(8,128)(2,1)}), bf16[32,128,128]{2,1,0:T(8,128)(2,1)S(1)}, u32[]{:S(2)}, u32[]{:S(2)}) async-start(bf16[32,128,128]{2,1,0:T(8,128)(2,1)} %shard_map.49), calls=%async_computation.4 | async-start | bytes 2097152 | tf_op jit(solution)/shard_map/all_to_all | solution.py:260
  181.0 20.1 %shard_map.48 = bf16[32,128,128]{2,1,0:T(8,128)(2,1)} custom-call(s32[2,16,64]{2,1,0:T(8,128)S(1)} %copy-done, bf16[32,128,128]{2,1,0:T(8,128)(2,1)S(1)} %all-to-all-done.query_hbm, bf16[16,4,128,128]{3,2,1,0:T(8,128)(2,1)} %collective-permute-done.3.left_hbm, bf16[32,4,128,128]{3,2,1,0:T(8,128)(2,1)} %all-to-all-done.1.own_hbm, ...), custom_call_target="tpu_custom_call" | custom-call | flops 4294967296 | bytes 12582912 | tf_op jit(solution)/shard_map/pallas_call | solution.py:236
  201.1 8.7 %all-to-all-done.4.source_hbm = bf16[32,128,128]{2,1,0:T(8,128)(2,1)S(1)} async-done(((bf16[32,128,128]{2,1,0:T(8,128)(2,1)}), bf16[32,128,128]{2,1,0:T(8,128)(2,1)S(1)}, u32[]{:S(2)}, u32[]{:S(2)}) %all-to-all-start.4) | async-done | bytes 1048608 | tf_op jit(solution)/shard_map/all_to_all | solution.py:260
  209.8 5.1 %all-to-all-start.2 = ((bf16[32,128,128]{2,1,0:T(8,128)(2,1)}), bf16[32,128,128]{2,1,0:T(8,128)(2,1)S(1)}, u32[]{:S(2)}, u32[]{:S(2)}) async-start(bf16[32,128,128]{2,1,0:T(8,128)(2,1)} %shard_map.48), calls=%async_computation.2 | async-start | bytes 2097152 | tf_op jit(solution)/shard_map/all_to_all | solution.py:260
  214.9 1.6 shard_map.50.refs_0_
  216.5 26.7 %all-to-all-done.2.source_hbm = bf16[32,128,128]{2,1,0:T(8,128)(2,1)S(1)} async-done(((bf16[32,128,128]{2,1,0:T(8,128)(2,1)}), bf16[32,128,128]{2,1,0:T(8,128)(2,1)S(1)}, u32[]{:S(2)}, u32[]{:S(2)}) %all-to-all-start.2) | async-done | bytes 1048608 | tf_op jit(solution)/shard_map/all_to_all | solution.py:260
  243.2 1.6 shard_map.51
  (4 shorter events, 0.1 us)
Async XLA Ops:
  4.0 108.2 %all-to-all-start.1 = ((bf16[32,4,128,128]{3,2,1,0:T(8,128)(2,1)}), bf16[32,4,128,128]{3,2,1,0:T(8,128)(2,1)}, u32[]{:S(2)}, u32[]{:S(2)}) async-start(bf16[32,4,128,128]{3,2,1,0:T(8,128)(2,1)} %get-tuple-element.8), calls=%async_computation.1 | async-start | bytes 8388608 | tf_op jit(solution)/shard_map/all_to_all | solution.py:260
  19.7 30.2 %collective-permute-start = (bf16[8,2,128,128]{3,2,1,0:T(8,128)(2,1)S(1)}, bf16[8,2,128,128]{3,2,1,0:T(8,128)(2,1)}, u32[]{:S(2)}, u32[]{:S(2)}) collective-permute-start(bf16[8,2,128,128]{3,2,1,0:T(8,128)(2,1)S(1)} %get-tuple-element.13), channel_id=1, source_target_pairs={{0,8},{1,9},{2,10},{3,11},{4,12},{5,13},{6,14},{7,15},{8,16},{9,17... | collective-permute-start | bytes 1572872 | tf_op jit(solution)/shard_map/ppermute | solution.py:276
  21.5 29.5 %collective-permute-start.2 = (bf16[8,2,128,128]{3,2,1,0:T(8,128)(2,1)S(1)}, bf16[8,2,128,128]{3,2,1,0:T(8,128)(2,1)S(1)}, u32[]{:S(2)}, u32[]{:S(2)}) collective-permute-start(bf16[8,2,128,128]{3,2,1,0:T(8,128)(2,1)S(1)} %get-tuple-element.14), channel_id=1, source_target_pairs={{0,24},{1,25},{2,26},{3,27},{4,28},{5,29},{6,30},{7,31},{8,0},{9,1... | collective-permute-start | bytes 1572872 | tf_op jit(solution)/shard_map/ppermute | solution.py:276
  23.1 47.6 %collective-permute-start.1 = (bf16[8,2,128,128]{3,2,1,0:T(8,128)(2,1)S(1)}, bf16[8,2,128,128]{3,2,1,0:T(8,128)(2,1)S(1)}, u32[]{:S(2)}, u32[]{:S(2)}) collective-permute-start(bf16[8,2,128,128]{3,2,1,0:T(8,128)(2,1)S(1)} %get-tuple-element.15), channel_id=1, source_target_pairs={{0,16},{1,17},{2,18},{3,19},{4,20},{5,21},{6,22},{7,23},{8,24},{9,... | collective-permute-start | bytes 1572872 | tf_op jit(solution)/shard_map/ppermute | solution.py:276
  112.2 31.3 %all-to-all-start.3 = ((bf16[32,128,128]{2,1,0:T(8,128)(2,1)}), bf16[32,128,128]{2,1,0:T(8,128)(2,1)S(1)}, u32[]{:S(2)}, u32[]{:S(2)}) async-start(bf16[32,128,128]{2,1,0:T(8,128)(2,1)} %bitcast.2), calls=%async_computation.3 | async-start | bytes 2097152 | tf_op jit(solution)/shard_map/all_to_all | solution.py:265
  120.7 26.4 %collective-permute-start.4 = (bf16[16,4,128,128]{3,2,1,0:T(8,128)(2,1)}, bf16[16,4,128,128]{3,2,1,0:T(8,128)(2,1)}, u32[]{:S(2)}, u32[]{:S(2)}) collective-permute-start(bf16[16,4,128,128]{3,2,1,0:T(8,128)(2,1)} %get-tuple-element.9), channel_id=1, source_target_pairs={{32,0},{64,32},{96,64},{128,96},{160,128},{192,160},{224,192},{33,... | collective-permute-start | bytes 6291464 | tf_op jit(solution)/shard_map/ppermute | solution.py:302
  122.6 27.7 %collective-permute-start.3 = (bf16[16,4,128,128]{3,2,1,0:T(8,128)(2,1)}, bf16[16,4,128,128]{3,2,1,0:T(8,128)(2,1)}, u32[]{:S(2)}, u32[]{:S(2)}) collective-permute-start(bf16[16,4,128,128]{3,2,1,0:T(8,128)(2,1)} %get-tuple-element.10), channel_id=1, source_target_pairs={{0,32},{32,64},{64,96},{96,128},{128,160},{160,192},{192,224},{1,3... | collective-permute-start | bytes 6291464 | tf_op jit(solution)/shard_map/ppermute | solution.py:301
  125.0 25.3 %copy-start = (s32[2,16,64]{2,1,0:T(8,128)S(1)}, s32[2,16,64]{2,1,0:T(8,128)}, u32[]{:S(2)}) copy-start(s32[2,16,64]{2,1,0:T(8,128)} %get-tuple-element.7.slot_ids) | copy-start | bytes 24580
  143.5 32.7 %all-to-all-start = ((bf16[32,128,128]{2,1,0:T(8,128)(2,1)}), bf16[32,128,128]{2,1,0:T(8,128)(2,1)S(1)}, u32[]{:S(2)}, u32[]{:S(2)}) async-start(bf16[32,128,128]{2,1,0:T(8,128)(2,1)} %bitcast.1), calls=%async_computation | async-start | bytes 2097152 | tf_op jit(solution)/shard_map/all_to_all | solution.py:265
  176.2 33.5 %all-to-all-start.4 = ((bf16[32,128,128]{2,1,0:T(8,128)(2,1)}), bf16[32,128,128]{2,1,0:T(8,128)(2,1)S(1)}, u32[]{:S(2)}, u32[]{:S(2)}) async-start(bf16[32,128,128]{2,1,0:T(8,128)(2,1)} %shard_map.49), calls=%async_computation.4 | async-start | bytes 2097152 | tf_op jit(solution)/shard_map/all_to_all | solution.py:260
  209.8 33.4 %all-to-all-start.2 = ((bf16[32,128,128]{2,1,0:T(8,128)(2,1)}), bf16[32,128,128]{2,1,0:T(8,128)(2,1)S(1)}, u32[]{:S(2)}, u32[]{:S(2)}) async-start(bf16[32,128,128]{2,1,0:T(8,128)(2,1)} %shard_map.48), calls=%async_computation.2 | async-start | bytes 2097152 | tf_op jit(solution)/shard_map/all_to_all | solution.py:260

commit v6 on v5

--- a/solution.py
+++ b/solution.py
@@ -90,14 +90,19 @@
     )(extents, tile_lists.T, keys_values)
 
 
-def join_kernel(chunk, source_hbm, *refs):
-    out_hbm, held, in_sems, out_sem = refs[-4:]
-    reads = [
-        pltpu.make_async_copy(
-            source_hbm.at[head], held.at[:, pl.ds(head * HEAD_DIM, HEAD_DIM)], in_sems.at[head]
-        )
-        for head in range(source_hbm.shape[0])
-    ]
+def join_kernel(chunk, count, *refs):
+    sources, (out_hbm, held, in_sems, out_sem) = refs[:count], refs[-4:]
+    here_x = lax.axis_index("seq") >> 3
+    reads = []
+    for by, source_hbm in enumerate(sources):
+        for place in range(source_hbm.shape[0]):
+            head = place if count == 1 else ((here_x + by) & 3) * ALONG_Z + place
+            columns = pl.ds(pl.multiple_of(head * HEAD_DIM, HEAD_DIM), HEAD_DIM)
+            reads.append(
+                pltpu.make_async_copy(
+                    source_hbm.at[place], held.at[:, columns], in_sems.at[len(reads)]
+                )
+            )
     for copy in reads:
         copy.start()
     for copy in reads:
@@ -107,16 +112,16 @@
     write.wait()
 
 
-def join_heads(chunk, source, *joined):
-    heads = source.shape[0]
+def join_heads(chunk, sources, *joined):
+    heads = sum(source.shape[0] for source in sources)
     width = heads * HEAD_DIM
     whole = pl.BlockSpec(memory_space=pl.ANY)
     return pl.pallas_call(
-        functools.partial(join_kernel, chunk),
-        in_specs=[whole] * (1 + len(joined)),
+        functools.partial(join_kernel, chunk, len(sources)),
+        in_specs=[whole] * (len(sources) + len(joined)),
         out_specs=whole,
         out_shape=jax.ShapeDtypeStruct((CHUNKS * TILE, width), jnp.bfloat16),
-        input_output_aliases={1: 0} if joined else {},
+        input_output_aliases={len(sources): 0} if joined else {},
         scratch_shapes=[
             pltpu.VMEM((TILE, width), jnp.bfloat16),
             pltpu.SemaphoreType.DMA((heads,)),
@@ -124,7 +129,7 @@
         ],
         compiler_params=pltpu.CompilerParams(vmem_limit_bytes=8 * MIB),
         cost_estimate=pl.CostEstimate(flops=0, bytes_accessed=4 * MIB, transcendentals=0),
-    )(source, *joined)
+    )(*sources, *joined)
 
 
 def attend_kernel(
@@ -222,7 +227,7 @@
                 )
                 mixed = part if mixed is None else mixed + part
             put_top(1 - now, best)
-            out_ref[pair] = (mixed[:, :HEAD_DIM] / mixed[:, HEAD_DIM:]).astype(jnp.bfloat16)
+            out_ref[tile if chunk == 0 else pair] = (mixed[:, :HEAD_DIM] / mixed[:, HEAD_DIM:]).astype(jnp.bfloat16)
         return carry
 
     lax.fori_loop(0, count // 2, step, 0)
@@ -290,6 +295,13 @@
     ]
 
 
+def outputs_by_x(blocks):
+    blocks = blocks.reshape(ALONG_Z, ALONG_X, TILE, HEAD_DIM)
+    return [
+        shift_x(blocks[:, by], ALONG_X - by) if by else blocks[:, by] for by in range(ALONG_X)
+    ]
+
+
 def per_device(queries, keys_values, extents, tile_lists):
     seq_size = lax.axis_size("seq")
     tm_size = lax.axis_size("tm")
@@ -302,9 +314,10 @@
     right = lax.ppermute(own[:half], "tm", [(i + 1, i) for i in range(ends)])
     first = exchange_z(first)
     second = exchange_z(second)
-    first_out = exchange(attend(0, ids, first, left, own, right))
+    first_out = exchange_z(attend(0, ids, first, left, own, right))
+    first_out = outputs_by_x(first_out)
     second_out = exchange(attend(1, ids, second, left, own, right))
-    return join_heads(1, second_out, join_heads(0, first_out))
+    return join_heads(1, [second_out], join_heads(0, first_out))
 
 
 def solution(mesh):

time: 245 us -> 245 us (level)
  waiting for transfers between devices: 146 us -> 140 us
  starting transfers between devices: 38 us -> 42.5 us
    all_to_all x3 -> x2, waiting for transfers between devices: 75.8 us -> 41.8 us  [exchange(): lax.all_to_all(blocks, 'seq', split_axis=0, concat_axis=0, tiled=True)]
    ppermute x3 -> x6, waiting for transfers between devices: 43.4 us -> 63.1 us  [shift_x(): return lax.ppermute(blocks, 'seq', pairs)]
    all_to_all x2 -> x3, waiting for transfers between devices: 23.4 us -> 32.4 us  [exchange_z(): lax.all_to_all(blocks, 'seq', split_axis=0, concat_axis=0, tiled=True, ax...]
    ppermute x3 -> x6, starting transfers between devices: 5.33 us -> 11.3 us  [shift_x(): return lax.ppermute(blocks, 'seq', pairs)]
    all_to_all x3 -> x2, starting transfers between devices: 21.3 us -> 16.2 us  [exchange(): lax.all_to_all(blocks, 'seq', split_axis=0, concat_axis=0, tiled=True)]
    all_to_all x2 -> x3, starting transfers between devices: 7.11 us -> 10.7 us  [exchange_z(): lax.all_to_all(blocks, 'seq', split_axis=0, concat_axis=0, tiled=True, ax...]
  transfers between devices with their start and end apart: 10 -> 13, of which waited for: 8 -> 10; matrix products, arithmetic and copies ran while one was open for 4% -> 4% of each run, Pallas kernels for 18% -> 18%
where the time goes in v6:
time: 245 us; the launch traced here: 244 us
  waiting for transfers between devices  140 us (57%)
  Pallas kernels  50.1 us (20%)
  starting transfers between devices  42.5 us (17%)
  local copies, waits for them, and re-layouts  8.67 us (4%)
    ppermute x6, waiting for transfers between devices, shift_x(): return lax.ppermute(blocks, 'seq', pairs)  63.1 us
    all_to_all x2, waiting for transfers between devices, exchange(): lax.all_to_all(blocks, 'seq', split_axis=0, concat_axis=0, tiled=True)  41.8 us
    pallas_call x2, Pallas kernels, attend(): pl.pallas_call(functools.partial(attend_kernel, chunk), in_specs=[scalar,...  40.1 us
    all_to_all x3, waiting for transfers between devices, exchange_z(): lax.all_to_all(blocks, 'seq', split_axis=0, concat_axis=0, tiled=True, ax...  32.4 us
    all_to_all x2, starting transfers between devices, exchange(): lax.all_to_all(blocks, 'seq', split_axis=0, concat_axis=0, tiled=True)  16.2 us
    ppermute x6, starting transfers between devices, shift_x(): return lax.ppermute(blocks, 'seq', pairs)  11.3 us
    all_to_all x3, starting transfers between devices, exchange_z(): lax.all_to_all(blocks, 'seq', split_axis=0, concat_axis=0, tiled=True, ax...  10.7 us
    slice x1, local copies, waits for them, and re-layouts, per_device(): right = lax.ppermute(own[:half], 'tm', [(i + 1, i) for i in range(ends)])  4.9 us
  transfers between devices with their start and end apart: 13, of which 10 were waited for; matrix products, arithmetic and copies ran while one was open for 4% of the time, Pallas kernels for 18%

profile of v6, /device:TPU:8, one launch (start us, length us, event | category | flops | bytes accessed | tf_op | source)
XLA Modules:
  0.0 244.1 jit_solution(1879588732397191021)
XLA Ops:
  0.0 4.0 %shard_map.46 = (bf16[32,4,128,128]{3,2,1,0:T(8,128)(2,1)}, s32[2,16,64]{2,1,0:T(8,128)}) custom-call(s32[3,32]{1,0:T(4,128)} %extents.1, s32[16,64]{1,0:T(8,128)} %bitcast.21, bf16[2,256,4096]{2,1,0:T(8,128)(2,1)} %pair_ref.1), custom_call_target="tpu_custom_call" | custom-call | tf_op jit(solution)/shard_map/pallas_call | solution.py:73
  4.0 11.4 %all-to-all-start.1 = ((bf16[32,4,128,128]{3,2,1,0:T(8,128)(2,1)}), bf16[32,4,128,128]{3,2,1,0:T(8,128)(2,1)}, u32[]{:S(2)}, u32[]{:S(2)}) async-start(bf16[32,4,128,128]{3,2,1,0:T(8,128)(2,1)} %get-tuple-element.8), calls=%async_computation.1 | async-start | bytes 8388608 | tf_op jit(solution)/shard_map/all_to_all | solution.py:265
  15.5 2.7 %shard_map.47 = bf16[32,2,128,128]{3,2,1,0:T(8,128)(2,1)} custom-call(bf16[256,4096]{1,0:T(8,128)(2,1)} %query_ref.1), custom_call_target="tpu_custom_call" | custom-call | bytes 4194304 | tf_op jit(solution)/shard_map/pallas_call | solution.py:33
  18.3 1.5 constant_dynamic-slice_fusion.3
  19.8 1.8 collective-permute-start
  21.6 1.5 collective-permute-start.2
  23.1 2.0 collective-permute-start.1
  26.2 23.8 %collective-permute-done = bf16[8,2,128,128]{3,2,1,0:T(8,128)(2,1)} collective-permute-done((bf16[8,2,128,128]{3,2,1,0:T(8,128)(2,1)S(1)}, bf16[8,2,128,128]{3,2,1,0:T(8,128)(2,1)}, u32[]{:S(2)}, u32[]{:S(2)}) %collective-permute-start) | collective-permute-done | bytes 524320 | tf_op jit(solution)/shard_map/ppermute | solution.py:281
  51.1 19.6 %collective-permute-done.1 = bf16[8,2,128,128]{3,2,1,0:T(8,128)(2,1)S(1)} collective-permute-done((bf16[8,2,128,128]{3,2,1,0:T(8,128)(2,1)S(1)}, bf16[8,2,128,128]{3,2,1,0:T(8,128)(2,1)S(1)}, u32[]{:S(2)}, u32[]{:S(2)}) %collective-permute-start.1) | collective-permute-done | bytes 524320 | tf_op jit(solution)/shard_map/ppermute | solution.py:281
  71.8 40.4 %all-to-all-done.1.own_hbm = bf16[32,4,128,128]{3,2,1,0:T(8,128)(2,1)} async-done(((bf16[32,4,128,128]{3,2,1,0:T(8,128)(2,1)}), bf16[32,4,128,128]{3,2,1,0:T(8,128)(2,1)}, u32[]{:S(2)}, u32[]{:S(2)}) %all-to-all-start.1) | async-done | bytes 4194336 | tf_op jit(solution)/shard_map/all_to_all | solution.py:265
  112.2 3.6 %all-to-all-start.3 = ((bf16[32,128,128]{2,1,0:T(8,128)(2,1)}), bf16[32,128,128]{2,1,0:T(8,128)(2,1)S(1)}, u32[]{:S(2)}, u32[]{:S(2)}) async-start(bf16[32,128,128]{2,1,0:T(8,128)(2,1)} %bitcast.2), calls=%async_computation.3 | async-start | bytes 2097152 | tf_op jit(solution)/shard_map/all_to_all | solution.py:270
  115.8 4.9 %fusion = (bf16[16,4,128,128]{3,2,1,0:T(8,128)(2,1)}, bf16[16,4,128,128]{3,2,1,0:T(8,128)(2,1)}) fusion(bf16[32,4,128,128]{3,2,1,0:T(8,128)(2,1)} %all-to-all-done.1.own_hbm), kind=kLoop, calls=%fused_computation.11 | loop fusion | bytes 8388608 | tf_op jit(solution)/shard_map/slice | solution.py:314
  120.7 1.9 collective-permute-start.4
  122.6 2.4 collective-permute-start.3
  125.0 1.1 pad_maximum_fusion
  126.2 17.4 %all-to-all-done.3.query_hbm = bf16[32,128,128]{2,1,0:T(8,128)(2,1)S(1)} async-done(((bf16[32,128,128]{2,1,0:T(8,128)(2,1)}), bf16[32,128,128]{2,1,0:T(8,128)(2,1)S(1)}, u32[]{:S(2)}, u32[]{:S(2)}) %all-to-all-start.3) | async-done | bytes 1048608 | tf_op jit(solution)/shard_map/all_to_all | solution.py:270
  143.6 3.6 %all-to-all-start = ((bf16[32,128,128]{2,1,0:T(8,128)(2,1)}), bf16[32,128,128]{2,1,0:T(8,128)(2,1)S(1)}, u32[]{:S(2)}, u32[]{:S(2)}) async-start(bf16[32,128,128]{2,1,0:T(8,128)(2,1)} %bitcast.1), calls=%async_computation | async-start | bytes 2097152 | tf_op jit(solution)/shard_map/all_to_all | solution.py:270
  147.1 3.1 %collective-permute-done.3.left_hbm = bf16[16,4,128,128]{3,2,1,0:T(8,128)(2,1)} collective-permute-done((bf16[16,4,128,128]{3,2,1,0:T(8,128)(2,1)}, bf16[16,4,128,128]{3,2,1,0:T(8,128)(2,1)}, u32[]{:S(2)}, u32[]{:S(2)}) %collective-permute-start.3) | collective-permute-done | bytes 2097184 | tf_op jit(solution)/shard_map/ppermute | solution.py:313
  150.3 20.0 %shard_map.49 = bf16[32,128,128]{2,1,0:T(8,128)(2,1)} custom-call(s32[2,16,64]{2,1,0:T(8,128)S(1)} %copy-done, bf16[32,128,128]{2,1,0:T(8,128)(2,1)S(1)} %all-to-all-done.3.query_hbm, bf16[16,4,128,128]{3,2,1,0:T(8,128)(2,1)} %collective-permute-done.3.left_hbm, bf16[32,4,128,128]{3,2,1,0:T(8,128)(2,1)} %all-to-all-done.1.own_hbm, ...), custom_call_target="tpu_custom_call" | custom-call | flops 4294967296 | bytes 12582912 | tf_op jit(solution)/shard_map/pallas_call | solution.py:241
  170.3 6.0 %all-to-all-done.query_hbm = bf16[32,128,128]{2,1,0:T(8,128)(2,1)S(1)} async-done(((bf16[32,128,128]{2,1,0:T(8,128)(2,1)}), bf16[32,128,128]{2,1,0:T(8,128)(2,1)S(1)}, u32[]{:S(2)}, u32[]{:S(2)}) %all-to-all-start) | async-done | bytes 1048608 | tf_op jit(solution)/shard_map/all_to_all | solution.py:270
  176.3 3.6 %all-to-all-start.4 = ((bf16[32,128,128]{2,1,0:T(8,128)(2,1)}), bf16[32,128,128]{2,1,0:T(8,128)(2,1)S(1)}, u32[]{:S(2)}, u32[]{:S(2)}) async-start(bf16[32,128,128]{2,1,0:T(8,128)(2,1)} %shard_map.49), calls=%async_computation.4 | async-start | bytes 2097152 | tf_op jit(solution)/shard_map/all_to_all | solution.py:270
  179.8 20.1 %shard_map.48 = bf16[32,128,128]{2,1,0:T(8,128)(2,1)} custom-call(s32[2,16,64]{2,1,0:T(8,128)S(1)} %copy-done, bf16[32,128,128]{2,1,0:T(8,128)(2,1)S(1)} %all-to-all-done.query_hbm, bf16[16,4,128,128]{3,2,1,0:T(8,128)(2,1)} %collective-permute-done.3.left_hbm, bf16[32,4,128,128]{3,2,1,0:T(8,128)(2,1)} %all-to-all-done.1.own_hbm, ...), custom_call_target="tpu_custom_call" | custom-call | flops 4294967296 | bytes 12582912 | tf_op jit(solution)/shard_map/pallas_call | solution.py:241
  200.0 9.0 %all-to-all-done.4 = bf16[32,128,128]{2,1,0:T(8,128)(2,1)S(1)} async-done(((bf16[32,128,128]{2,1,0:T(8,128)(2,1)}), bf16[32,128,128]{2,1,0:T(8,128)(2,1)S(1)}, u32[]{:S(2)}, u32[]{:S(2)}) %all-to-all-start.4) | async-done | bytes 1048608 | tf_op jit(solution)/shard_map/all_to_all | solution.py:270
  209.0 4.7 %all-to-all-start.2 = ((bf16[32,128,128]{2,1,0:T(8,128)(2,1)}), bf16[32,128,128]{2,1,0:T(8,128)(2,1)S(1)}, u32[]{:S(2)}, u32[]{:S(2)}) async-start(bf16[32,128,128]{2,1,0:T(8,128)(2,1)} %shard_map.48), calls=%async_computation.2 | async-start | bytes 2097152 | tf_op jit(solution)/shard_map/all_to_all | solution.py:265
  213.8 1.9 collective-permute-start.7
  215.7 2.7 %collective-permute-start.6 = (bf16[8,128,128]{2,1,0:T(8,128)(2,1)S(1)}, bf16[8,128,128]{2,1,0:T(8,128)(2,1)S(1)}, u32[]{:S(2)}, u32[]{:S(2)}) collective-permute-start(bf16[8,128,128]{2,1,0:T(8,128)(2,1)S(1)} %get-tuple-element.17), channel_id=1, source_target_pairs={{0,16},{1,17},{2,18},{3,19},{4,20},{5,21},{6,22},{7,23},{8,24},{9,... | collective-permute-start | bytes 786440 | tf_op jit(solution)/shard_map/ppermute | solution.py:281
  218.4 1.4 collective-permute-start.5
  219.8 8.8 %collective-permute-done.7.refs_3_ = bf16[8,128,128]{2,1,0:T(8,128)(2,1)S(1)} collective-permute-done((bf16[8,128,128]{2,1,0:T(8,128)(2,1)S(1)}, bf16[8,128,128]{2,1,0:T(8,128)(2,1)S(1)}, u32[]{:S(2)}, u32[]{:S(2)}) %collective-permute-start.7) | collective-permute-done | bytes 262176 | tf_op jit(solution)/shard_map/ppermute | solution.py:281
  228.6 10.9 %collective-permute-done.6.refs_2_ = bf16[8,128,128]{2,1,0:T(8,128)(2,1)S(1)} collective-permute-done((bf16[8,128,128]{2,1,0:T(8,128)(2,1)S(1)}, bf16[8,128,128]{2,1,0:T(8,128)(2,1)S(1)}, u32[]{:S(2)}, u32[]{:S(2)}) %collective-permute-start.6) | collective-permute-done | bytes 262176 | tf_op jit(solution)/shard_map/ppermute | solution.py:281
  239.6 1.6 shard_map.50.refs_1_
  241.2 1.3 all-to-all-done.2.refs_0_
  242.5 1.6 shard_map.51
  (11 shorter events, 3.4 us)
Async XLA Ops:
  4.0 108.2 %all-to-all-start.1 = ((bf16[32,4,128,128]{3,2,1,0:T(8,128)(2,1)}), bf16[32,4,128,128]{3,2,1,0:T(8,128)(2,1)}, u32[]{:S(2)}, u32[]{:S(2)}) async-start(bf16[32,4,128,128]{3,2,1,0:T(8,128)(2,1)} %get-tuple-element.8), calls=%async_computation.1 | async-start | bytes 8388608 | tf_op jit(solution)/shard_map/all_to_all | solution.py:265
  19.8 30.2 %collective-permute-start = (bf16[8,2,128,128]{3,2,1,0:T(8,128)(2,1)S(1)}, bf16[8,2,128,128]{3,2,1,0:T(8,128)(2,1)}, u32[]{:S(2)}, u32[]{:S(2)}) collective-permute-start(bf16[8,2,128,128]{3,2,1,0:T(8,128)(2,1)S(1)} %get-tuple-element.13), channel_id=1, source_target_pairs={{0,8},{1,9},{2,10},{3,11},{4,12},{5,13},{6,14},{7,15},{8,16},{9,17... | collective-permute-start | bytes 1572872 | tf_op jit(solution)/shard_map/ppermute | solution.py:281
  21.6 29.5 %collective-permute-start.2 = (bf16[8,2,128,128]{3,2,1,0:T(8,128)(2,1)S(1)}, bf16[8,2,128,128]{3,2,1,0:T(8,128)(2,1)S(1)}, u32[]{:S(2)}, u32[]{:S(2)}) collective-permute-start(bf16[8,2,128,128]{3,2,1,0:T(8,128)(2,1)S(1)} %get-tuple-element.14), channel_id=1, source_target_pairs={{0,24},{1,25},{2,26},{3,27},{4,28},{5,29},{6,30},{7,31},{8,0},{9,1... | collective-permute-start | bytes 1572872 | tf_op jit(solution)/shard_map/ppermute | solution.py:281
  23.1 47.6 %collective-permute-start.1 = (bf16[8,2,128,128]{3,2,1,0:T(8,128)(2,1)S(1)}, bf16[8,2,128,128]{3,2,1,0:T(8,128)(2,1)S(1)}, u32[]{:S(2)}, u32[]{:S(2)}) collective-permute-start(bf16[8,2,128,128]{3,2,1,0:T(8,128)(2,1)S(1)} %get-tuple-element.15), channel_id=1, source_target_pairs={{0,16},{1,17},{2,18},{3,19},{4,20},{5,21},{6,22},{7,23},{8,24},{9,... | collective-permute-start | bytes 1572872 | tf_op jit(solution)/shard_map/ppermute | solution.py:281
  112.2 31.3 %all-to-all-start.3 = ((bf16[32,128,128]{2,1,0:T(8,128)(2,1)}), bf16[32,128,128]{2,1,0:T(8,128)(2,1)S(1)}, u32[]{:S(2)}, u32[]{:S(2)}) async-start(bf16[32,128,128]{2,1,0:T(8,128)(2,1)} %bitcast.2), calls=%async_computation.3 | async-start | bytes 2097152 | tf_op jit(solution)/shard_map/all_to_all | solution.py:270
  120.7 26.4 %collective-permute-start.4 = (bf16[16,4,128,128]{3,2,1,0:T(8,128)(2,1)}, bf16[16,4,128,128]{3,2,1,0:T(8,128)(2,1)}, u32[]{:S(2)}, u32[]{:S(2)}) collective-permute-start(bf16[16,4,128,128]{3,2,1,0:T(8,128)(2,1)} %get-tuple-element.9), channel_id=1, source_target_pairs={{32,0},{64,32},{96,64},{128,96},{160,128},{192,160},{224,192},{33,... | collective-permute-start | bytes 6291464 | tf_op jit(solution)/shard_map/ppermute | solution.py:314
  122.6 27.7 %collective-permute-start.3 = (bf16[16,4,128,128]{3,2,1,0:T(8,128)(2,1)}, bf16[16,4,128,128]{3,2,1,0:T(8,128)(2,1)}, u32[]{:S(2)}, u32[]{:S(2)}) collective-permute-start(bf16[16,4,128,128]{3,2,1,0:T(8,128)(2,1)} %get-tuple-element.10), channel_id=1, source_target_pairs={{0,32},{32,64},{64,96},{96,128},{128,160},{160,192},{192,224},{1,3... | collective-permute-start | bytes 6291464 | tf_op jit(solution)/shard_map/ppermute | solution.py:313
  125.0 25.3 %copy-start = (s32[2,16,64]{2,1,0:T(8,128)S(1)}, s32[2,16,64]{2,1,0:T(8,128)}, u32[]{:S(2)}) copy-start(s32[2,16,64]{2,1,0:T(8,128)} %get-tuple-element.7.slot_ids) | copy-start | bytes 24580
  143.6 32.7 %all-to-all-start = ((bf16[32,128,128]{2,1,0:T(8,128)(2,1)}), bf16[32,128,128]{2,1,0:T(8,128)(2,1)S(1)}, u32[]{:S(2)}, u32[]{:S(2)}) async-start(bf16[32,128,128]{2,1,0:T(8,128)(2,1)} %bitcast.1), calls=%async_computation | async-start | bytes 2097152 | tf_op jit(solution)/shard_map/all_to_all | solution.py:270
  176.3 32.7 %all-to-all-start.4 = ((bf16[32,128,128]{2,1,0:T(8,128)(2,1)}), bf16[32,128,128]{2,1,0:T(8,128)(2,1)S(1)}, u32[]{:S(2)}, u32[]{:S(2)}) async-start(bf16[32,128,128]{2,1,0:T(8,128)(2,1)} %shard_map.49), calls=%async_computation.4 | async-start | bytes 2097152 | tf_op jit(solution)/shard_map/all_to_all | solution.py:270
  209.0 33.5 %all-to-all-start.2 = ((bf16[32,128,128]{2,1,0:T(8,128)(2,1)}), bf16[32,128,128]{2,1,0:T(8,128)(2,1)S(1)}, u32[]{:S(2)}, u32[]{:S(2)}) async-start(bf16[32,128,128]{2,1,0:T(8,128)(2,1)} %shard_map.48), calls=%async_computation.2 | async-start | bytes 2097152 | tf_op jit(solution)/shard_map/all_to_all | solution.py:265
  213.8 14.8 %collective-permute-start.7 = (bf16[8,128,128]{2,1,0:T(8,128)(2,1)S(1)}, bf16[8,128,128]{2,1,0:T(8,128)(2,1)S(1)}, u32[]{:S(2)}, u32[]{:S(2)}) collective-permute-start(bf16[8,128,128]{2,1,0:T(8,128)(2,1)S(1)} %get-tuple-element.16), channel_id=1, source_target_pairs={{0,8},{1,9},{2,10},{3,11},{4,12},{5,13},{6,14},{7,15},{8,16},{9,17... | collective-permute-start | bytes 786440 | tf_op jit(solution)/shard_map/ppermute | solution.py:281
  215.7 23.9 %collective-permute-start.6 = (bf16[8,128,128]{2,1,0:T(8,128)(2,1)S(1)}, bf16[8,128,128]{2,1,0:T(8,128)(2,1)S(1)}, u32[]{:S(2)}, u32[]{:S(2)}) collective-permute-start(bf16[8,128,128]{2,1,0:T(8,128)(2,1)S(1)} %get-tuple-element.17), channel_id=1, source_target_pairs={{0,16},{1,17},{2,18},{3,19},{4,20},{5,21},{6,22},{7,23},{8,24},{9,... | collective-permute-start | bytes 786440 | tf_op jit(solution)/shard_map/ppermute | solution.py:281
  218.4 21.2 %collective-permute-start.5 = (bf16[8,128,128]{2,1,0:T(8,128)(2,1)S(1)}, bf16[8,128,128]{2,1,0:T(8,128)(2,1)S(1)}, u32[]{:S(2)}, u32[]{:S(2)}) collective-permute-start(bf16[8,128,128]{2,1,0:T(8,128)(2,1)S(1)} %get-tuple-element.18), channel_id=1, source_target_pairs={{0,24},{1,25},{2,26},{3,27},{4,28},{5,29},{6,30},{7,31},{8,0},{9,1... | collective-permute-start | bytes 786440 | tf_op jit(solution)/shard_map/ppermute | solution.py:281

commit v7 on v6

--- a/solution.py
+++ b/solution.py
@@ -15,6 +15,7 @@
 HEADS_STEP = 16
 NO_TILE = 128
 ALONG_X = 4
+PIECE = 32
 ALONG_Z = 8
 EXP2_SCALE = HEAD_DIM ** (-0.5) * 1.4426950408889634
 MIB = 1024 * 1024
@@ -41,50 +42,67 @@
     )(queries)
 
 
-def split_pairs_kernel(extents, list_ref, pair_ref, block_ref, id_ref):
-    for head in range(block_ref.shape[0]):
-        columns = slice(head * HEAD_DIM, (head + 1) * HEAD_DIM)
-        for part in range(2):
-            for half in range(CHUNKS):
-                rows = slice(half * TILE, (half + 1) * TILE)
-                block_ref[head, part * CHUNKS + half] = pair_ref[part, rows, columns]
-
-    @pl.when(pl.program_id(0) == 0)
-    def _():
-        head = lax.axis_index("seq")
-        listed = list_ref[...]
-        first = lax.axis_index("tm") * listed.shape[1]
-        tiles = first + lax.broadcasted_iota(jnp.int32, listed.shape, 1)
-        live = None
-        for axis, (low, mask) in enumerate(((5, 15), (3, 3), (0, 7))):
-            gap = jnp.abs(((listed >> low) & mask) - ((tiles >> low) & mask))
-            near = gap <= extents[axis, head]
-            live = near if live is None else live & near
-        shift = first - FRAME
-        id_ref[0] = jnp.where(live, listed, tiles) - shift
-        id_ref[1] = jnp.where(live, listed - shift, NO_TILE)
+def split_pairs_kernel(extents, list_ref, pair_hbm, block_hbm, id_ref, rows_in, rows_out, sems):
+    pieces = TILE // PIECE
+    reads, writes = [], []
+    for part in range(2):
+        for piece in range(CHUNKS * pieces):
+            place = len(reads)
+            rows = pl.ds(piece * PIECE, PIECE)
+            reads.append(
+                pltpu.make_async_copy(pair_hbm.at[part, rows], rows_in.at[place], sems.at[0, place])
+            )
+            block = part * CHUNKS + piece // pieces
+            rows = pl.ds(piece % pieces * PIECE, PIECE)
+            writes.append(
+                pltpu.make_async_copy(
+                    rows_out.at[place], block_hbm.at[:, block, rows], sems.at[1, place]
+                )
+            )
+    for copy in reads:
+        copy.start()
+
+    here = lax.axis_index("seq")
+    listed = list_ref[...]
+    first = lax.axis_index("tm") * listed.shape[1]
+    tiles = first + lax.broadcasted_iota(jnp.int32, listed.shape, 1)
+    live = None
+    for axis, (low, mask) in enumerate(((5, 15), (3, 3), (0, 7))):
+        gap = jnp.abs(((listed >> low) & mask) - ((tiles >> low) & mask))
+        near = gap <= extents[axis, here]
+        live = near if live is None else live & near
+    shift = first - FRAME
+    id_ref[0] = jnp.where(live, listed, tiles) - shift
+    id_ref[1] = jnp.where(live, listed - shift, NO_TILE)
+
+    for place, (read, write) in enumerate(zip(reads, writes)):
+        read.wait()
+        for head in range(rows_out.shape[1]):
+            rows_out[place, head] = rows_in[place, :, head * HEAD_DIM : (head + 1) * HEAD_DIM]
+        write.start()
+    for copy in writes:
+        copy.wait()
 
 
 def split_pairs(keys_values, extents, tile_lists):
     _, tok_dev, width_all = keys_values.shape
     heads = width_all // HEAD_DIM
-    parts = 2 * CHUNKS
+    places = 2 * tok_dev // PIECE
     rows, slots = tile_lists.shape
+    whole = pl.BlockSpec(memory_space=pl.ANY)
+    local = pl.BlockSpec(memory_space=pltpu.VMEM)
     return pl.pallas_call(
         split_pairs_kernel,
-        grid=(heads // HEADS_STEP,),
-        in_specs=[
-            pl.BlockSpec(memory_space=pltpu.SMEM),
-            pl.BlockSpec((slots, rows), lambda i: (0, 0)),
-            pl.BlockSpec((2, tok_dev, HEADS_STEP * HEAD_DIM), lambda i: (0, 0, i)),
+        in_specs=[pl.BlockSpec(memory_space=pltpu.SMEM), local, whole],
+        out_specs=[whole, local],
+        out_shape=[
+            jax.ShapeDtypeStruct((heads, 2 * CHUNKS, TILE, HEAD_DIM), jnp.bfloat16),
+            jax.ShapeDtypeStruct((2, slots, rows), jnp.int32),
         ],
-        out_specs=[
-            pl.BlockSpec((HEADS_STEP, parts, TILE, HEAD_DIM), lambda i: (i, 0, 0, 0)),
-            pl.BlockSpec((2, slots, rows), lambda i: (0, 0, 0)),
-        ],
-        out_shape=[
-            jax.ShapeDtypeStruct((heads, parts, TILE, HEAD_DIM), jnp.bfloat16),
-            jax.ShapeDtypeStruct((2, slots, rows), jnp.int32),
+        scratch_shapes=[
+            pltpu.VMEM((places, PIECE, width_all), jnp.bfloat16),
+            pltpu.VMEM((places, heads, PIECE, HEAD_DIM), jnp.bfloat16),
+            pltpu.SemaphoreType.DMA((2, places)),
         ],
         compiler_params=pltpu.CompilerParams(vmem_limit_bytes=60 * MIB),
     )(extents, tile_lists.T, keys_values)
@@ -96,7 +114,10 @@
     reads = []
     for by, source_hbm in enumerate(sources):
         for place in range(source_hbm.shape[0]):
-            head = place if count == 1 else ((here_x + by) & 3) * ALONG_Z + place
+            if count == 1:
+                head = ((here_x - (place & 3)) & 3) * ALONG_Z + (place >> 2)
+            else:
+                head = ((here_x + by) & 3) * ALONG_Z + place
             columns = pl.ds(pl.multiple_of(head * HEAD_DIM, HEAD_DIM), HEAD_DIM)
             reads.append(
                 pltpu.make_async_copy(
@@ -139,15 +160,9 @@
     left_hbm,
     own_hbm,
     right_hbm,
-    out_ref,
-    keys,
-    values,
-    query,
-    marks,
-    scores,
-    tops,
-    sems,
+    *refs,
 ):
+    out_refs, (keys, values, query, marks, scores, tops, sems) = refs[:-7], refs[-7:]
     pairs = own_hbm.shape[0]
     rim = left_hbm.shape[0]
     places = ((own_hbm, rim), (left_hbm, 0), (right_hbm, rim + pairs))
@@ -168,11 +183,10 @@
     values[NO_TILE // CHUNKS] = jnp.zeros((CHUNKS, TILE, HEAD_DIM), jnp.bfloat16)
     for copy in copies[:4]:
         copy.wait()
-    count = query.shape[0]
     here_x = lax.axis_index("seq") >> 3
 
-    def pair_of(tile):
-        return (((here_x - (tile & 3)) & 3) << 3) + (tile >> 2)
+    def pair_of(turn, by):
+        return (((here_x + by) & 3) << 3) + turn
 
     def score_pair(row, tile_query, slot):
         ids = [slot_ids[0, slot + i, row] for i in range(2)]
@@ -195,7 +209,7 @@
         tops[place] = jnp.broadcast_to(jnp.max(best, axis=1, keepdims=True), (TILE, TILE))
 
     best = None
-    first_row = pair_of(0) * CHUNKS + chunk
+    first_row = pair_of(0, 0) * CHUNKS + chunk
     for slot in range(0, KSEL, 2):
         score = score_pair(first_row, query[0], slot)
         scores[0, slot // 2] = score
@@ -205,11 +219,14 @@
         copy.wait()
 
     def step(turn, carry):
-        for now in range(2):
-            tile = turn * 2 + now
-            later = jnp.minimum(tile + 1, count - 1)
-            pair = pair_of(tile)
-            row, later_row = pair * CHUNKS + chunk, pair_of(later) * CHUNKS + chunk
+        for by in range(ALONG_X):
+            now = by % 2
+            later_by = (by + 1) % ALONG_X
+            later_turn = turn if later_by else jnp.minimum(turn + 1, ALONG_Z - 1)
+            tile = turn * ALONG_X + -by % ALONG_X
+            later = later_turn * ALONG_X + -later_by % ALONG_X
+            row = pair_of(turn, by) * CHUNKS + chunk
+            later_row = pair_of(later_turn, later_by) * CHUNKS + chunk
             top = tops[now]
             top = jnp.concatenate([top, top], axis=1)
             later_query = query[later]
@@ -227,22 +244,27 @@
                 )
                 mixed = part if mixed is None else mixed + part
             put_top(1 - now, best)
-            out_ref[tile if chunk == 0 else pair] = (mixed[:, :HEAD_DIM] / mixed[:, HEAD_DIM:]).astype(jnp.bfloat16)
+            tile_out = (mixed[:, :HEAD_DIM] / mixed[:, HEAD_DIM:]).astype(jnp.bfloat16)
+            if len(out_refs) == 1:
+                out_refs[0][tile] = tile_out
+            else:
+                out_refs[by][turn, 0] = tile_out
         return carry
 
-    lax.fori_loop(0, count // 2, step, 0)
-
-
-def attend(chunk, ids, query_tiles, left, own, right):
+    lax.fori_loop(0, ALONG_Z, step, 0)
+
+
+def attend(chunk, outs, ids, query_tiles, left, own, right):
     count = query_tiles.shape[0]
+    shape = (count, TILE, HEAD_DIM) if outs == 1 else (count // outs, 1, TILE, HEAD_DIM)
     held = own.shape[0] + 2 * left.shape[0]
     whole = pl.BlockSpec(memory_space=pl.ANY)
     scalar = pl.BlockSpec(memory_space=pltpu.SMEM)
     return pl.pallas_call(
         functools.partial(attend_kernel, chunk),
         in_specs=[scalar, whole, whole, whole, whole],
-        out_specs=pl.BlockSpec(memory_space=pltpu.VMEM),
-        out_shape=jax.ShapeDtypeStruct((count, TILE, HEAD_DIM), jnp.bfloat16),
+        out_specs=[pl.BlockSpec(memory_space=pltpu.VMEM)] * outs,
+        out_shape=[jax.ShapeDtypeStruct(shape, jnp.bfloat16)] * outs,
         scratch_shapes=[
             pltpu.VMEM((held, CHUNKS, TILE, HEAD_DIM), jnp.bfloat16),
             pltpu.VMEM((held + 1, CHUNKS, TILE, HEAD_DIM), jnp.bfloat16),
@@ -314,9 +336,11 @@
     right = lax.ppermute(own[:half], "tm", [(i + 1, i) for i in range(ends)])
     first = exchange_z(first)
     second = exchange_z(second)
-    first_out = exchange_z(attend(0, ids, first, left, own, right))
-    first_out = outputs_by_x(first_out)
-    second_out = exchange(attend(1, ids, second, left, own, right))
+    (first_out,) = attend(0, 1, ids, first, left, own, right)
+    first_out = outputs_by_x(exchange_z(first_out))
+    second_out = attend(1, ALONG_X, ids, second, left, own, right)
+    second_out = [shift_x(part, by) if by else part for by, part in enumerate(second_out)]
+    second_out = exchange_z(jnp.concatenate(second_out, axis=1).reshape(-1, TILE, HEAD_DIM))
     return join_heads(1, [second_out], join_heads(0, first_out))
 
 

time: 245 us -> 252 us (1.029)
  starting transfers between devices: 42.5 us -> 50.1 us
  Pallas kernels: 50.1 us -> 44.1 us
  waiting for transfers between devices: 140 us -> 144 us
    pallas_call x2, Pallas kernels: 40.1 us -> 33 us  [attend(): pl.pallas_call(functools.partial(attend_kernel, chunk), in_specs=[scalar,...]
    all_to_all x3 -> x4, starting transfers between devices: 10.7 us -> 17.5 us  [exchange_z(): lax.all_to_all(blocks, 'seq', split_axis=0, concat_axis=0, tiled=True, ax...]
    ppermute x6 -> x9, starting transfers between devices: 11.3 us -> 16.9 us  [shift_x(): return lax.ppermute(blocks, 'seq', pairs)]
    all_to_all x2 -> x1, starting transfers between devices: 16.2 us -> 11.5 us  [exchange(): lax.all_to_all(blocks, 'seq', split_axis=0, concat_axis=0, tiled=True)]
    all_to_all x3 -> x4, waiting for transfers between devices: 32.4 us -> 36.8 us  [exchange_z(): lax.all_to_all(blocks, 'seq', split_axis=0, concat_axis=0, tiled=True, ax...]
    all_to_all x2 -> x1, waiting for transfers between devices: 41.8 us -> 40.4 us  [exchange(): lax.all_to_all(blocks, 'seq', split_axis=0, concat_axis=0, tiled=True)]
    ppermute x6 -> x9, waiting for transfers between devices: 63.1 us -> 63.3 us  [shift_x(): return lax.ppermute(blocks, 'seq', pairs)]
  transfers between devices with their start and end apart: 13 -> 16, of which waited for: 10 -> 12; matrix products, arithmetic and copies ran while one was open for 4% -> 5% of each run, Pallas kernels for 18% -> 15%
where the time goes in v7:
time: 252 us; the launch traced here: 250 us
  waiting for transfers between devices  144 us (57%)
  starting transfers between devices  50.1 us (20%)
  Pallas kernels  44.1 us (18%)
  local copies, waits for them, and re-layouts  8.64 us (3%)
  other arithmetic  3.37 us (1%)
    ppermute x9, waiting for transfers between devices, shift_x(): return lax.ppermute(blocks, 'seq', pairs)  63.3 us
    all_to_all x1, waiting for transfers between devices, exchange(): lax.all_to_all(blocks, 'seq', split_axis=0, concat_axis=0, tiled=True)  40.4 us
    all_to_all x4, waiting for transfers between devices, exchange_z(): lax.all_to_all(blocks, 'seq', split_axis=0, concat_axis=0, tiled=True, ax...  36.8 us
    pallas_call x2, Pallas kernels, attend(): pl.pallas_call(functools.partial(attend_kernel, chunk), in_specs=[scalar,...  33 us
    all_to_all x4, starting transfers between devices, exchange_z(): lax.all_to_all(blocks, 'seq', split_axis=0, concat_axis=0, tiled=True, ax...  17.5 us
    ppermute x9, starting transfers between devices, shift_x(): return lax.ppermute(blocks, 'seq', pairs)  16.9 us
    all_to_all x1, starting transfers between devices, exchange(): lax.all_to_all(blocks, 'seq', split_axis=0, concat_axis=0, tiled=True)  11.5 us
    pallas_call x1, Pallas kernels, split_pairs(): pl.pallas_call(split_pairs_kernel, in_specs=[pl.BlockSpec(memory_space=pl...  5.11 us
  transfers between devices with their start and end apart: 16, of which 12 were waited for; matrix products, arithmetic and copies ran while one was open for 5% of the time, Pallas kernels for 15%

profile of v7, /device:TPU:8, one launch (start us, length us, event | category | flops | bytes accessed | tf_op | source)
XLA Modules:
  0.0 250.2 jit_solution(16431641436884297214)
XLA Ops:
  0.0 5.1 %shard_map.46 = (bf16[32,4,128,128]{3,2,1,0:T(8,128)(2,1)}, s32[2,16,64]{2,1,0:T(8,128)}) custom-call(s32[3,32]{1,0:T(4,128)} %extents.1, s32[16,64]{1,0:T(8,128)} %bitcast.22, bf16[2,256,4096]{2,1,0:T(8,128)(2,1)} %pair_hbm.1), custom_call_target="tpu_custom_call" | custom-call | tf_op jit(solution)/shard_map/pallas_call | solution.py:94
  5.1 11.5 %all-to-all-start.1 = ((bf16[32,4,128,128]{3,2,1,0:T(8,128)(2,1)}), bf16[32,4,128,128]{3,2,1,0:T(8,128)(2,1)}, u32[]{:S(2)}, u32[]{:S(2)}) async-start(bf16[32,4,128,128]{3,2,1,0:T(8,128)(2,1)} %get-tuple-element.12), calls=%async_computation.1 | async-start | bytes 8388608 | tf_op jit(solution)/shard_map/all_to_all | solution.py:287
  16.7 2.7 %shard_map.47 = bf16[32,2,128,128]{3,2,1,0:T(8,128)(2,1)} custom-call(bf16[256,4096]{1,0:T(8,128)(2,1)} %query_ref.1), custom_call_target="tpu_custom_call" | custom-call | bytes 4194304 | tf_op jit(solution)/shard_map/pallas_call | solution.py:34
  20.9 1.8 collective-permute-start
  24.2 2.0 collective-permute-start.1
  27.3 23.8 %collective-permute-done = bf16[8,2,128,128]{3,2,1,0:T(8,128)(2,1)} collective-permute-done((bf16[8,2,128,128]{3,2,1,0:T(8,128)(2,1)S(1)}, bf16[8,2,128,128]{3,2,1,0:T(8,128)(2,1)}, u32[]{:S(2)}, u32[]{:S(2)}) %collective-permute-start) | collective-permute-done | bytes 524320 | tf_op jit(solution)/shard_map/ppermute | solution.py:303
  52.2 19.6 %collective-permute-done.1 = bf16[8,2,128,128]{3,2,1,0:T(8,128)(2,1)S(1)} collective-permute-done((bf16[8,2,128,128]{3,2,1,0:T(8,128)(2,1)S(1)}, bf16[8,2,128,128]{3,2,1,0:T(8,128)(2,1)S(1)}, u32[]{:S(2)}, u32[]{:S(2)}) %collective-permute-start.1) | collective-permute-done | bytes 524320 | tf_op jit(solution)/shard_map/ppermute | solution.py:303
  72.9 40.4 %all-to-all-done.1.own_hbm = bf16[32,4,128,128]{3,2,1,0:T(8,128)(2,1)} async-done(((bf16[32,4,128,128]{3,2,1,0:T(8,128)(2,1)}), bf16[32,4,128,128]{3,2,1,0:T(8,128)(2,1)}, u32[]{:S(2)}, u32[]{:S(2)}) %all-to-all-start.1) | async-done | bytes 4194336 | tf_op jit(solution)/shard_map/all_to_all | solution.py:287
  113.3 3.6 %all-to-all-start.3 = ((bf16[32,128,128]{2,1,0:T(8,128)(2,1)}), bf16[32,128,128]{2,1,0:T(8,128)(2,1)S(1)}, u32[]{:S(2)}, u32[]{:S(2)}) async-start(bf16[32,128,128]{2,1,0:T(8,128)(2,1)} %bitcast.3), calls=%async_computation.3 | async-start | bytes 2097152 | tf_op jit(solution)/shard_map/all_to_all | solution.py:292
  116.9 4.9 %fusion = (bf16[16,4,128,128]{3,2,1,0:T(8,128)(2,1)}, bf16[16,4,128,128]{3,2,1,0:T(8,128)(2,1)}) fusion(bf16[32,4,128,128]{3,2,1,0:T(8,128)(2,1)} %all-to-all-done.1.own_hbm), kind=kLoop, calls=%fused_computation.12 | loop fusion | bytes 8388608 | tf_op jit(solution)/shard_map/slice | solution.py:336
  121.8 1.9 collective-permute-start.4
  123.7 2.4 collective-permute-start.3
  127.3 17.4 %all-to-all-done.3.query_hbm = bf16[32,128,128]{2,1,0:T(8,128)(2,1)S(1)} async-done(((bf16[32,128,128]{2,1,0:T(8,128)(2,1)}), bf16[32,128,128]{2,1,0:T(8,128)(2,1)S(1)}, u32[]{:S(2)}, u32[]{:S(2)}) %all-to-all-start.3) | async-done | bytes 1048608 | tf_op jit(solution)/shard_map/all_to_all | solution.py:292
  144.7 3.6 %all-to-all-start = ((bf16[32,128,128]{2,1,0:T(8,128)(2,1)}), bf16[32,128,128]{2,1,0:T(8,128)(2,1)S(1)}, u32[]{:S(2)}, u32[]{:S(2)}) async-start(bf16[32,128,128]{2,1,0:T(8,128)(2,1)} %bitcast.1), calls=%async_computation | async-start | bytes 2097152 | tf_op jit(solution)/shard_map/all_to_all | solution.py:292
  148.2 3.1 %collective-permute-done.3.left_hbm = bf16[16,4,128,128]{3,2,1,0:T(8,128)(2,1)} collective-permute-done((bf16[16,4,128,128]{3,2,1,0:T(8,128)(2,1)}, bf16[16,4,128,128]{3,2,1,0:T(8,128)(2,1)}, u32[]{:S(2)}, u32[]{:S(2)}) %collective-permute-start.3) | collective-permute-done | bytes 2097184 | tf_op jit(solution)/shard_map/ppermute | solution.py:335
  151.4 17.0 %shard_map.49 = bf16[32,128,128]{2,1,0:T(8,128)(2,1)} custom-call(s32[2,16,64]{2,1,0:T(8,128)S(1)} %copy-done, bf16[32,128,128]{2,1,0:T(8,128)(2,1)S(1)} %all-to-all-done.3.query_hbm, bf16[16,4,128,128]{3,2,1,0:T(8,128)(2,1)} %collective-permute-done.3.left_hbm, bf16[32,4,128,128]{3,2,1,0:T(8,128)(2,1)} %all-to-all-done.1.own_hbm, ...), custom_call_target="tpu_custom_call" | custom-call | flops 4294967296 | bytes 12582912 | tf_op jit(solution)/shard_map/pallas_call | solution.py:263
  168.4 9.0 %all-to-all-done.query_hbm = bf16[32,128,128]{2,1,0:T(8,128)(2,1)S(1)} async-done(((bf16[32,128,128]{2,1,0:T(8,128)(2,1)}), bf16[32,128,128]{2,1,0:T(8,128)(2,1)S(1)}, u32[]{:S(2)}, u32[]{:S(2)}) %all-to-all-start) | async-done | bytes 1048608 | tf_op jit(solution)/shard_map/all_to_all | solution.py:292
  177.4 3.6 %all-to-all-start.4 = ((bf16[32,128,128]{2,1,0:T(8,128)(2,1)}), bf16[32,128,128]{2,1,0:T(8,128)(2,1)S(1)}, u32[]{:S(2)}, u32[]{:S(2)}) async-start(bf16[32,128,128]{2,1,0:T(8,128)(2,1)} %shard_map.49), calls=%async_computation.4 | async-start | bytes 2097152 | tf_op jit(solution)/shard_map/all_to_all | solution.py:292
  181.0 16.0 %shard_map.48 = (bf16[8,1,128,128]{3,2,1,0:T(8,128)(2,1)S(1)}, bf16[8,1,128,128]{3,2,1,0:T(8,128)(2,1)S(1)}, bf16[8,1,128,128]{3,2,1,0:T(8,128)(2,1)S(1)}, bf16[8,1,128,128]{3,2,1,0:T(8,128)(2,1)S(1)}) custom-call(s32[2,16,64]{2,1,0:T(8,128)S(1)} %copy-done, bf16[32,128,128]{2,1,0:T(8,128)(2,1)S(1)} %all-to-all-done.query_hbm, ...), custom_call_target="tpu_custom_call" | custom-call | flops 4294967296 | bytes 12582912 | tf_op jit(solution)/shard_map/pallas_call | solution.py:263
  196.9 1.7 collective-permute-start.5
  198.6 1.6 collective-permute-start.6
  200.2 2.5 collective-permute-start.7
  202.7 4.4 %collective-permute-done.5 = bf16[8,1,128,128]{3,2,1,0:T(8,128)(2,1)S(1)} collective-permute-done((bf16[8,1,128,128]{3,2,1,0:T(8,128)(2,1)S(1)}, bf16[8,1,128,128]{3,2,1,0:T(8,128)(2,1)S(1)}, u32[]{:S(2)}, u32[]{:S(2)}) %collective-permute-start.5) | collective-permute-done | bytes 262176 | tf_op jit(solution)/shard_map/ppermute | solution.py:303
  207.2 5.0 %collective-permute-done.6 = bf16[8,1,128,128]{3,2,1,0:T(8,128)(2,1)S(1)} collective-permute-done((bf16[8,1,128,128]{3,2,1,0:T(8,128)(2,1)S(1)}, bf16[8,1,128,128]{3,2,1,0:T(8,128)(2,1)S(1)}, u32[]{:S(2)}, u32[]{:S(2)}) %collective-permute-start.6) | collective-permute-done | bytes 262176 | tf_op jit(solution)/shard_map/ppermute | solution.py:303
  213.8 6.8 %all-to-all-start.2 = ((bf16[32,128,128]{2,1,0:T(8,128)(2,1)}), bf16[32,128,128]{2,1,0:T(8,128)(2,1)S(1)}, u32[]{:S(2)}, u32[]{:S(2)}) async-start(bf16[32,128,128]{2,1,0:T(8,128)(2,1)} %bitcast.2), calls=%async_computation.2 | async-start | bytes 2097152 | tf_op jit(solution)/shard_map/all_to_all | solution.py:292
  220.8 1.8 collective-permute-start.10
  222.5 2.4 collective-permute-start.9
  226.5 3.2 %collective-permute-done.10.refs_3_ = bf16[8,128,128]{2,1,0:T(8,128)(2,1)S(1)} collective-permute-done((bf16[8,128,128]{2,1,0:T(8,128)(2,1)S(1)}, bf16[8,128,128]{2,1,0:T(8,128)(2,1)S(1)}, u32[]{:S(2)}, u32[]{:S(2)}) %collective-permute-start.10) | collective-permute-done | bytes 262176 | tf_op jit(solution)/shard_map/ppermute | solution.py:303
  229.7 6.7 %collective-permute-done.9.refs_2_ = bf16[8,128,128]{2,1,0:T(8,128)(2,1)S(1)} collective-permute-done((bf16[8,128,128]{2,1,0:T(8,128)(2,1)S(1)}, bf16[8,128,128]{2,1,0:T(8,128)(2,1)S(1)}, u32[]{:S(2)}, u32[]{:S(2)}) %collective-permute-start.9) | collective-permute-done | bytes 262176 | tf_op jit(solution)/shard_map/ppermute | solution.py:303
  236.5 1.6 shard_map.50.refs_1_
  238.1 10.4 %all-to-all-done.2.refs_0_ = bf16[32,128,128]{2,1,0:T(8,128)(2,1)S(1)} async-done(((bf16[32,128,128]{2,1,0:T(8,128)(2,1)}), bf16[32,128,128]{2,1,0:T(8,128)(2,1)S(1)}, u32[]{:S(2)}, u32[]{:S(2)}) %all-to-all-start.2) | async-done | bytes 1048608 | tf_op jit(solution)/shard_map/all_to_all | solution.py:292
  248.5 1.6 shard_map.51
  (18 shorter events, 10.8 us)
Async XLA Ops:
  5.1 108.2 %all-to-all-start.1 = ((bf16[32,4,128,128]{3,2,1,0:T(8,128)(2,1)}), bf16[32,4,128,128]{3,2,1,0:T(8,128)(2,1)}, u32[]{:S(2)}, u32[]{:S(2)}) async-start(bf16[32,4,128,128]{3,2,1,0:T(8,128)(2,1)} %get-tuple-element.12), calls=%async_computation.1 | async-start | bytes 8388608 | tf_op jit(solution)/shard_map/all_to_all | solution.py:287
  20.9 30.2 %collective-permute-start = (bf16[8,2,128,128]{3,2,1,0:T(8,128)(2,1)S(1)}, bf16[8,2,128,128]{3,2,1,0:T(8,128)(2,1)}, u32[]{:S(2)}, u32[]{:S(2)}) collective-permute-start(bf16[8,2,128,128]{3,2,1,0:T(8,128)(2,1)S(1)} %get-tuple-element.21), channel_id=1, source_target_pairs={{0,8},{1,9},{2,10},{3,11},{4,12},{5,13},{6,14},{7,15},{8,16},{9,17... | collective-permute-start | bytes 1572872 | tf_op jit(solution)/shard_map/ppermute | solution.py:303
  22.7 29.5 %collective-permute-start.2 = (bf16[8,2,128,128]{3,2,1,0:T(8,128)(2,1)S(1)}, bf16[8,2,128,128]{3,2,1,0:T(8,128)(2,1)S(1)}, u32[]{:S(2)}, u32[]{:S(2)}) collective-permute-start(bf16[8,2,128,128]{3,2,1,0:T(8,128)(2,1)S(1)} %get-tuple-element.22), channel_id=1, source_target_pairs={{0,24},{1,25},{2,26},{3,27},{4,28},{5,29},{6,30},{7,31},{8,0},{9,1... | collective-permute-start | bytes 1572872 | tf_op jit(solution)/shard_map/ppermute | solution.py:303
  24.2 47.6 %collective-permute-start.1 = (bf16[8,2,128,128]{3,2,1,0:T(8,128)(2,1)S(1)}, bf16[8,2,128,128]{3,2,1,0:T(8,128)(2,1)S(1)}, u32[]{:S(2)}, u32[]{:S(2)}) collective-permute-start(bf16[8,2,128,128]{3,2,1,0:T(8,128)(2,1)S(1)} %get-tuple-element.23), channel_id=1, source_target_pairs={{0,16},{1,17},{2,18},{3,19},{4,20},{5,21},{6,22},{7,23},{8,24},{9,... | collective-permute-start | bytes 1572872 | tf_op jit(solution)/shard_map/ppermute | solution.py:303
  113.3 31.3 %all-to-all-start.3 = ((bf16[32,128,128]{2,1,0:T(8,128)(2,1)}), bf16[32,128,128]{2,1,0:T(8,128)(2,1)S(1)}, u32[]{:S(2)}, u32[]{:S(2)}) async-start(bf16[32,128,128]{2,1,0:T(8,128)(2,1)} %bitcast.3), calls=%async_computation.3 | async-start | bytes 2097152 | tf_op jit(solution)/shard_map/all_to_all | solution.py:292
  121.8 26.5 %collective-permute-start.4 = (bf16[16,4,128,128]{3,2,1,0:T(8,128)(2,1)}, bf16[16,4,128,128]{3,2,1,0:T(8,128)(2,1)}, u32[]{:S(2)}, u32[]{:S(2)}) collective-permute-start(bf16[16,4,128,128]{3,2,1,0:T(8,128)(2,1)} %get-tuple-element.17), channel_id=1, source_target_pairs={{32,0},{64,32},{96,64},{128,96},{160,128},{192,160},{224,192},{33,... | collective-permute-start | bytes 6291464 | tf_op jit(solution)/shard_map/ppermute | solution.py:336
  123.7 27.7 %collective-permute-start.3 = (bf16[16,4,128,128]{3,2,1,0:T(8,128)(2,1)}, bf16[16,4,128,128]{3,2,1,0:T(8,128)(2,1)}, u32[]{:S(2)}, u32[]{:S(2)}) collective-permute-start(bf16[16,4,128,128]{3,2,1,0:T(8,128)(2,1)} %get-tuple-element.18), channel_id=1, source_target_pairs={{0,32},{32,64},{64,96},{96,128},{128,160},{160,192},{192,224},{1,3... | collective-permute-start | bytes 6291464 | tf_op jit(solution)/shard_map/ppermute | solution.py:335
  126.1 25.3 %copy-start = (s32[2,16,64]{2,1,0:T(8,128)S(1)}, s32[2,16,64]{2,1,0:T(8,128)}, u32[]{:S(2)}) copy-start(s32[2,16,64]{2,1,0:T(8,128)} %get-tuple-element.11.slot_ids) | copy-start | bytes 24580
  144.7 32.7 %all-to-all-start = ((bf16[32,128,128]{2,1,0:T(8,128)(2,1)}), bf16[32,128,128]{2,1,0:T(8,128)(2,1)S(1)}, u32[]{:S(2)}, u32[]{:S(2)}) async-start(bf16[32,128,128]{2,1,0:T(8,128)(2,1)} %bitcast.1), calls=%async_computation | async-start | bytes 2097152 | tf_op jit(solution)/shard_map/all_to_all | solution.py:292
  177.4 36.4 %all-to-all-start.4 = ((bf16[32,128,128]{2,1,0:T(8,128)(2,1)}), bf16[32,128,128]{2,1,0:T(8,128)(2,1)S(1)}, u32[]{:S(2)}, u32[]{:S(2)}) async-start(bf16[32,128,128]{2,1,0:T(8,128)(2,1)} %shard_map.49), calls=%async_computation.4 | async-start | bytes 2097152 | tf_op jit(solution)/shard_map/all_to_all | solution.py:292
  196.9 10.2 %collective-permute-start.5 = (bf16[8,1,128,128]{3,2,1,0:T(8,128)(2,1)S(1)}, bf16[8,1,128,128]{3,2,1,0:T(8,128)(2,1)S(1)}, u32[]{:S(2)}, u32[]{:S(2)}) collective-permute-start(bf16[8,1,128,128]{3,2,1,0:T(8,128)(2,1)S(1)} %get-tuple-element.14), channel_id=1, source_target_pairs={{0,8},{1,9},{2,10},{3,11},{4,12},{5,13},{6,14},{7,15},{8,16},{9,17... | collective-permute-start | bytes 786440 | tf_op jit(solution)/shard_map/ppermute | solution.py:303
  198.6 13.6 %collective-permute-start.6 = (bf16[8,1,128,128]{3,2,1,0:T(8,128)(2,1)S(1)}, bf16[8,1,128,128]{3,2,1,0:T(8,128)(2,1)S(1)}, u32[]{:S(2)}, u32[]{:S(2)}) collective-permute-start(bf16[8,1,128,128]{3,2,1,0:T(8,128)(2,1)S(1)} %get-tuple-element.15), channel_id=1, source_target_pairs={{0,16},{1,17},{2,18},{3,19},{4,20},{5,21},{6,22},{7,23},{8,24},{9,... | collective-permute-start | bytes 786440 | tf_op jit(solution)/shard_map/ppermute | solution.py:303
  200.2 12.5 %collective-permute-start.7 = (bf16[8,1,128,128]{3,2,1,0:T(8,128)(2,1)S(1)}, bf16[8,1,128,128]{3,2,1,0:T(8,128)(2,1)S(1)}, u32[]{:S(2)}, u32[]{:S(2)}) collective-permute-start(bf16[8,1,128,128]{3,2,1,0:T(8,128)(2,1)S(1)} %get-tuple-element.16), channel_id=1, source_target_pairs={{0,24},{1,25},{2,26},{3,27},{4,28},{5,29},{6,30},{7,31},{8,0},{9,1... | collective-permute-start | bytes 786440 | tf_op jit(solution)/shard_map/ppermute | solution.py:303
  213.8 34.7 %all-to-all-start.2 = ((bf16[32,128,128]{2,1,0:T(8,128)(2,1)}), bf16[32,128,128]{2,1,0:T(8,128)(2,1)S(1)}, u32[]{:S(2)}, u32[]{:S(2)}) async-start(bf16[32,128,128]{2,1,0:T(8,128)(2,1)} %bitcast.2), calls=%async_computation.2 | async-start | bytes 2097152 | tf_op jit(solution)/shard_map/all_to_all | solution.py:292
  220.8 9.0 %collective-permute-start.10 = (bf16[8,128,128]{2,1,0:T(8,128)(2,1)S(1)}, bf16[8,128,128]{2,1,0:T(8,128)(2,1)S(1)}, u32[]{:S(2)}, u32[]{:S(2)}) collective-permute-start(bf16[8,128,128]{2,1,0:T(8,128)(2,1)S(1)} %get-tuple-element.24), channel_id=1, source_target_pairs={{0,8},{1,9},{2,10},{3,11},{4,12},{5,13},{6,14},{7,15},{8,16},{9,17... | collective-permute-start | bytes 786440 | tf_op jit(solution)/shard_map/ppermute | solution.py:303
  222.5 13.9 %collective-permute-start.9 = (bf16[8,128,128]{2,1,0:T(8,128)(2,1)S(1)}, bf16[8,128,128]{2,1,0:T(8,128)(2,1)S(1)}, u32[]{:S(2)}, u32[]{:S(2)}) collective-permute-start(bf16[8,128,128]{2,1,0:T(8,128)(2,1)S(1)} %get-tuple-element.25), channel_id=1, source_target_pairs={{0,16},{1,17},{2,18},{3,19},{4,20},{5,21},{6,22},{7,23},{8,24},{9,... | collective-permute-start | bytes 786440 | tf_op jit(solution)/shard_map/ppermute | solution.py:303
  224.9 11.5 %collective-permute-start.8 = (bf16[8,128,128]{2,1,0:T(8,128)(2,1)S(1)}, bf16[8,128,128]{2,1,0:T(8,128)(2,1)S(1)}, u32[]{:S(2)}, u32[]{:S(2)}) collective-permute-start(bf16[8,128,128]{2,1,0:T(8,128)(2,1)S(1)} %get-tuple-element.26), channel_id=1, source_target_pairs={{0,24},{1,25},{2,26},{3,27},{4,28},{5,29},{6,30},{7,31},{8,0},{9,1... | collective-permute-start | bytes 786440 | tf_op jit(solution)/shard_map/ppermute | solution.py:303

commit v8 on v6

--- a/solution.py
+++ b/solution.py
@@ -168,11 +168,10 @@
     values[NO_TILE // CHUNKS] = jnp.zeros((CHUNKS, TILE, HEAD_DIM), jnp.bfloat16)
     for copy in copies[:4]:
         copy.wait()
-    count = query.shape[0]
     here_x = lax.axis_index("seq") >> 3
 
-    def pair_of(tile):
-        return (((here_x - (tile & 3)) & 3) << 3) + (tile >> 2)
+    def pair_of(turn, by):
+        return (((here_x + by) & 3) << 3) + turn
 
     def score_pair(row, tile_query, slot):
         ids = [slot_ids[0, slot + i, row] for i in range(2)]
@@ -195,7 +194,7 @@
         tops[place] = jnp.broadcast_to(jnp.max(best, axis=1, keepdims=True), (TILE, TILE))
 
     best = None
-    first_row = pair_of(0) * CHUNKS + chunk
+    first_row = pair_of(0, 0) * CHUNKS + chunk
     for slot in range(0, KSEL, 2):
         score = score_pair(first_row, query[0], slot)
         scores[0, slot // 2] = score
@@ -205,11 +204,15 @@
         copy.wait()
 
     def step(turn, carry):
-        for now in range(2):
-            tile = turn * 2 + now
-            later = jnp.minimum(tile + 1, count - 1)
-            pair = pair_of(tile)
-            row, later_row = pair * CHUNKS + chunk, pair_of(later) * CHUNKS + chunk
+        for by in range(ALONG_X):
+            now = by % 2
+            later_by = (by + 1) % ALONG_X
+            later_turn = turn if later_by else jnp.minimum(turn + 1, ALONG_Z - 1)
+            tile = turn * ALONG_X + -by % ALONG_X
+            later = later_turn * ALONG_X + -later_by % ALONG_X
+            pair = pair_of(turn, by)
+            row = pair * CHUNKS + chunk
+            later_row = pair_of(later_turn, later_by) * CHUNKS + chunk
             top = tops[now]
             top = jnp.concatenate([top, top], axis=1)
             later_query = query[later]
@@ -230,7 +233,7 @@
             out_ref[tile if chunk == 0 else pair] = (mixed[:, :HEAD_DIM] / mixed[:, HEAD_DIM:]).astype(jnp.bfloat16)
         return carry
 
-    lax.fori_loop(0, count // 2, step, 0)
+    lax.fori_loop(0, ALONG_Z, step, 0)
 
 
 def attend(chunk, ids, query_tiles, left, own, right):

time: 245 us -> 245 us (level)
  Pallas kernels: 50.1 us -> 44.1 us
  waiting for transfers between devices: 140 us -> 146 us
    all_to_all x3, waiting for transfers between devices: 32.4 us -> 38.4 us  [exchange_z(): lax.all_to_all(blocks, 'seq', split_axis=0, concat_axis=0, tiled=True, ax...]
    pallas_call x2, Pallas kernels: 40.1 us -> 34.2 us  [attend(): pl.pallas_call(functools.partial(attend_kernel, chunk), in_specs=[scalar,...]
  transfers between devices with their start and end apart: 13 -> 13, of which waited for: 10 -> 10; matrix products, arithmetic and copies ran while one was open for 4% -> 4% of each run, Pallas kernels for 18% -> 16%
where the time goes in v8:
time: 245 us; the launch traced here: 244 us
  waiting for transfers between devices  146 us (60%)
  Pallas kernels  44.1 us (18%)
  starting transfers between devices  42.5 us (17%)
  local copies, waits for them, and re-layouts  8.67 us (4%)
    ppermute x6, waiting for transfers between devices, shift_x(): return lax.ppermute(blocks, 'seq', pairs)  63.1 us
    all_to_all x2, waiting for transfers between devices, exchange(): lax.all_to_all(blocks, 'seq', split_axis=0, concat_axis=0, tiled=True)  41.8 us
    all_to_all x3, waiting for transfers between devices, exchange_z(): lax.all_to_all(blocks, 'seq', split_axis=0, concat_axis=0, tiled=True, ax...  38.4 us
    pallas_call x2, Pallas kernels, attend(): pl.pallas_call(functools.partial(attend_kernel, chunk), in_specs=[scalar,...  34.2 us
    all_to_all x2, starting transfers between devices, exchange(): lax.all_to_all(blocks, 'seq', split_axis=0, concat_axis=0, tiled=True)  16.2 us
    ppermute x6, starting transfers between devices, shift_x(): return lax.ppermute(blocks, 'seq', pairs)  11.3 us
    all_to_all x3, starting transfers between devices, exchange_z(): lax.all_to_all(blocks, 'seq', split_axis=0, concat_axis=0, tiled=True, ax...  10.7 us
    slice x1, local copies, waits for them, and re-layouts, per_device(): right = lax.ppermute(own[:half], 'tm', [(i + 1, i) for i in range(ends)])  4.9 us
  transfers between devices with their start and end apart: 13, of which 10 were waited for; matrix products, arithmetic and copies ran while one was open for 4% of the time, Pallas kernels for 16%

profile of v8, /device:TPU:8, one launch (start us, length us, event | category | flops | bytes accessed | tf_op | source)
XLA Modules:
  0.0 244.1 jit_solution(4644711464413145313)
XLA Ops:
  0.0 4.0 %shard_map.46 = (bf16[32,4,128,128]{3,2,1,0:T(8,128)(2,1)}, s32[2,16,64]{2,1,0:T(8,128)}) custom-call(s32[3,32]{1,0:T(4,128)} %extents.1, s32[16,64]{1,0:T(8,128)} %bitcast.21, bf16[2,256,4096]{2,1,0:T(8,128)(2,1)} %pair_ref.1), custom_call_target="tpu_custom_call" | custom-call | tf_op jit(solution)/shard_map/pallas_call | solution.py:73
  4.0 11.4 %all-to-all-start.1 = ((bf16[32,4,128,128]{3,2,1,0:T(8,128)(2,1)}), bf16[32,4,128,128]{3,2,1,0:T(8,128)(2,1)}, u32[]{:S(2)}, u32[]{:S(2)}) async-start(bf16[32,4,128,128]{3,2,1,0:T(8,128)(2,1)} %get-tuple-element.8), calls=%async_computation.1 | async-start | bytes 8388608 | tf_op jit(solution)/shard_map/all_to_all | solution.py:268
  15.5 2.7 %shard_map.47 = bf16[32,2,128,128]{3,2,1,0:T(8,128)(2,1)} custom-call(bf16[256,4096]{1,0:T(8,128)(2,1)} %query_ref.1), custom_call_target="tpu_custom_call" | custom-call | bytes 4194304 | tf_op jit(solution)/shard_map/pallas_call | solution.py:33
  18.3 1.5 constant_dynamic-slice_fusion.3
  19.8 1.8 collective-permute-start
  21.6 1.5 collective-permute-start.2
  23.1 2.0 collective-permute-start.1
  26.2 23.8 %collective-permute-done = bf16[8,2,128,128]{3,2,1,0:T(8,128)(2,1)} collective-permute-done((bf16[8,2,128,128]{3,2,1,0:T(8,128)(2,1)S(1)}, bf16[8,2,128,128]{3,2,1,0:T(8,128)(2,1)}, u32[]{:S(2)}, u32[]{:S(2)}) %collective-permute-start) | collective-permute-done | bytes 524320 | tf_op jit(solution)/shard_map/ppermute | solution.py:284
  51.1 19.6 %collective-permute-done.1 = bf16[8,2,128,128]{3,2,1,0:T(8,128)(2,1)S(1)} collective-permute-done((bf16[8,2,128,128]{3,2,1,0:T(8,128)(2,1)S(1)}, bf16[8,2,128,128]{3,2,1,0:T(8,128)(2,1)S(1)}, u32[]{:S(2)}, u32[]{:S(2)}) %collective-permute-start.1) | collective-permute-done | bytes 524320 | tf_op jit(solution)/shard_map/ppermute | solution.py:284
  71.8 40.4 %all-to-all-done.1.own_hbm = bf16[32,4,128,128]{3,2,1,0:T(8,128)(2,1)} async-done(((bf16[32,4,128,128]{3,2,1,0:T(8,128)(2,1)}), bf16[32,4,128,128]{3,2,1,0:T(8,128)(2,1)}, u32[]{:S(2)}, u32[]{:S(2)}) %all-to-all-start.1) | async-done | bytes 4194336 | tf_op jit(solution)/shard_map/all_to_all | solution.py:268
  112.2 3.6 %all-to-all-start.3 = ((bf16[32,128,128]{2,1,0:T(8,128)(2,1)}), bf16[32,128,128]{2,1,0:T(8,128)(2,1)S(1)}, u32[]{:S(2)}, u32[]{:S(2)}) async-start(bf16[32,128,128]{2,1,0:T(8,128)(2,1)} %bitcast.2), calls=%async_computation.3 | async-start | bytes 2097152 | tf_op jit(solution)/shard_map/all_to_all | solution.py:273
  115.8 4.9 %fusion = (bf16[16,4,128,128]{3,2,1,0:T(8,128)(2,1)}, bf16[16,4,128,128]{3,2,1,0:T(8,128)(2,1)}) fusion(bf16[32,4,128,128]{3,2,1,0:T(8,128)(2,1)} %all-to-all-done.1.own_hbm), kind=kLoop, calls=%fused_computation.11 | loop fusion | bytes 8388608 | tf_op jit(solution)/shard_map/slice | solution.py:317
  120.7 1.9 collective-permute-start.4
  122.6 2.4 collective-permute-start.3
  125.0 1.1 pad_maximum_fusion
  126.2 17.4 %all-to-all-done.3.query_hbm = bf16[32,128,128]{2,1,0:T(8,128)(2,1)S(1)} async-done(((bf16[32,128,128]{2,1,0:T(8,128)(2,1)}), bf16[32,128,128]{2,1,0:T(8,128)(2,1)S(1)}, u32[]{:S(2)}, u32[]{:S(2)}) %all-to-all-start.3) | async-done | bytes 1048608 | tf_op jit(solution)/shard_map/all_to_all | solution.py:273
  143.6 3.6 %all-to-all-start = ((bf16[32,128,128]{2,1,0:T(8,128)(2,1)}), bf16[32,128,128]{2,1,0:T(8,128)(2,1)S(1)}, u32[]{:S(2)}, u32[]{:S(2)}) async-start(bf16[32,128,128]{2,1,0:T(8,128)(2,1)} %bitcast.1), calls=%async_computation | async-start | bytes 2097152 | tf_op jit(solution)/shard_map/all_to_all | solution.py:273
  147.1 3.1 %collective-permute-done.3.left_hbm = bf16[16,4,128,128]{3,2,1,0:T(8,128)(2,1)} collective-permute-done((bf16[16,4,128,128]{3,2,1,0:T(8,128)(2,1)}, bf16[16,4,128,128]{3,2,1,0:T(8,128)(2,1)}, u32[]{:S(2)}, u32[]{:S(2)}) %collective-permute-start.3) | collective-permute-done | bytes 2097184 | tf_op jit(solution)/shard_map/ppermute | solution.py:316
  150.3 17.0 %shard_map.49 = bf16[32,128,128]{2,1,0:T(8,128)(2,1)} custom-call(s32[2,16,64]{2,1,0:T(8,128)S(1)} %copy-done, bf16[32,128,128]{2,1,0:T(8,128)(2,1)S(1)} %all-to-all-done.3.query_hbm, bf16[16,4,128,128]{3,2,1,0:T(8,128)(2,1)} %collective-permute-done.3.left_hbm, bf16[32,4,128,128]{3,2,1,0:T(8,128)(2,1)} %all-to-all-done.1.own_hbm, ...), custom_call_target="tpu_custom_call" | custom-call | flops 4294967296 | bytes 12582912 | tf_op jit(solution)/shard_map/pallas_call | solution.py:244
  167.3 8.9 %all-to-all-done.query_hbm = bf16[32,128,128]{2,1,0:T(8,128)(2,1)S(1)} async-done(((bf16[32,128,128]{2,1,0:T(8,128)(2,1)}), bf16[32,128,128]{2,1,0:T(8,128)(2,1)S(1)}, u32[]{:S(2)}, u32[]{:S(2)}) %all-to-all-start) | async-done | bytes 1048608 | tf_op jit(solution)/shard_map/all_to_all | solution.py:273
  176.3 3.6 %all-to-all-start.4 = ((bf16[32,128,128]{2,1,0:T(8,128)(2,1)}), bf16[32,128,128]{2,1,0:T(8,128)(2,1)S(1)}, u32[]{:S(2)}, u32[]{:S(2)}) async-start(bf16[32,128,128]{2,1,0:T(8,128)(2,1)} %shard_map.49), calls=%async_computation.4 | async-start | bytes 2097152 | tf_op jit(solution)/shard_map/all_to_all | solution.py:273
  179.8 17.1 %shard_map.48 = bf16[32,128,128]{2,1,0:T(8,128)(2,1)} custom-call(s32[2,16,64]{2,1,0:T(8,128)S(1)} %copy-done, bf16[32,128,128]{2,1,0:T(8,128)(2,1)S(1)} %all-to-all-done.query_hbm, bf16[16,4,128,128]{3,2,1,0:T(8,128)(2,1)} %collective-permute-done.3.left_hbm, bf16[32,4,128,128]{3,2,1,0:T(8,128)(2,1)} %all-to-all-done.1.own_hbm, ...), custom_call_target="tpu_custom_call" | custom-call | flops 4294967296 | bytes 12582912 | tf_op jit(solution)/shard_map/pallas_call | solution.py:244
  197.0 12.0 %all-to-all-done.4 = bf16[32,128,128]{2,1,0:T(8,128)(2,1)S(1)} async-done(((bf16[32,128,128]{2,1,0:T(8,128)(2,1)}), bf16[32,128,128]{2,1,0:T(8,128)(2,1)S(1)}, u32[]{:S(2)}, u32[]{:S(2)}) %all-to-all-start.4) | async-done | bytes 1048608 | tf_op jit(solution)/shard_map/all_to_all | solution.py:273
  209.0 4.7 %all-to-all-start.2 = ((bf16[32,128,128]{2,1,0:T(8,128)(2,1)}), bf16[32,128,128]{2,1,0:T(8,128)(2,1)S(1)}, u32[]{:S(2)}, u32[]{:S(2)}) async-start(bf16[32,128,128]{2,1,0:T(8,128)(2,1)} %shard_map.48), calls=%async_computation.2 | async-start | bytes 2097152 | tf_op jit(solution)/shard_map/all_to_all | solution.py:268
  213.8 1.9 collective-permute-start.7
  215.7 2.7 %collective-permute-start.6 = (bf16[8,128,128]{2,1,0:T(8,128)(2,1)S(1)}, bf16[8,128,128]{2,1,0:T(8,128)(2,1)S(1)}, u32[]{:S(2)}, u32[]{:S(2)}) collective-permute-start(bf16[8,128,128]{2,1,0:T(8,128)(2,1)S(1)} %get-tuple-element.17), channel_id=1, source_target_pairs={{0,16},{1,17},{2,18},{3,19},{4,20},{5,21},{6,22},{7,23},{8,24},{9,... | collective-permute-start | bytes 786440 | tf_op jit(solution)/shard_map/ppermute | solution.py:284
  218.4 1.4 collective-permute-start.5
  219.8 8.8 %collective-permute-done.7.refs_3_ = bf16[8,128,128]{2,1,0:T(8,128)(2,1)S(1)} collective-permute-done((bf16[8,128,128]{2,1,0:T(8,128)(2,1)S(1)}, bf16[8,128,128]{2,1,0:T(8,128)(2,1)S(1)}, u32[]{:S(2)}, u32[]{:S(2)}) %collective-permute-start.7) | collective-permute-done | bytes 262176 | tf_op jit(solution)/shard_map/ppermute | solution.py:284
  228.6 10.9 %collective-permute-done.6.refs_2_ = bf16[8,128,128]{2,1,0:T(8,128)(2,1)S(1)} collective-permute-done((bf16[8,128,128]{2,1,0:T(8,128)(2,1)S(1)}, bf16[8,128,128]{2,1,0:T(8,128)(2,1)S(1)}, u32[]{:S(2)}, u32[]{:S(2)}) %collective-permute-start.6) | collective-permute-done | bytes 262176 | tf_op jit(solution)/shard_map/ppermute | solution.py:284
  239.6 1.6 shard_map.50.refs_1_
  241.2 1.3 all-to-all-done.2.refs_0_
  242.5 1.6 shard_map.51
  (11 shorter events, 3.4 us)
Async XLA Ops:
  4.0 108.2 %all-to-all-start.1 = ((bf16[32,4,128,128]{3,2,1,0:T(8,128)(2,1)}), bf16[32,4,128,128]{3,2,1,0:T(8,128)(2,1)}, u32[]{:S(2)}, u32[]{:S(2)}) async-start(bf16[32,4,128,128]{3,2,1,0:T(8,128)(2,1)} %get-tuple-element.8), calls=%async_computation.1 | async-start | bytes 8388608 | tf_op jit(solution)/shard_map/all_to_all | solution.py:268
  19.8 30.2 %collective-permute-start = (bf16[8,2,128,128]{3,2,1,0:T(8,128)(2,1)S(1)}, bf16[8,2,128,128]{3,2,1,0:T(8,128)(2,1)}, u32[]{:S(2)}, u32[]{:S(2)}) collective-permute-start(bf16[8,2,128,128]{3,2,1,0:T(8,128)(2,1)S(1)} %get-tuple-element.13), channel_id=1, source_target_pairs={{0,8},{1,9},{2,10},{3,11},{4,12},{5,13},{6,14},{7,15},{8,16},{9,17... | collective-permute-start | bytes 1572872 | tf_op jit(solution)/shard_map/ppermute | solution.py:284
  21.6 29.5 %collective-permute-start.2 = (bf16[8,2,128,128]{3,2,1,0:T(8,128)(2,1)S(1)}, bf16[8,2,128,128]{3,2,1,0:T(8,128)(2,1)S(1)}, u32[]{:S(2)}, u32[]{:S(2)}) collective-permute-start(bf16[8,2,128,128]{3,2,1,0:T(8,128)(2,1)S(1)} %get-tuple-element.14), channel_id=1, source_target_pairs={{0,24},{1,25},{2,26},{3,27},{4,28},{5,29},{6,30},{7,31},{8,0},{9,1... | collective-permute-start | bytes 1572872 | tf_op jit(solution)/shard_map/ppermute | solution.py:284
  23.1 47.6 %collective-permute-start.1 = (bf16[8,2,128,128]{3,2,1,0:T(8,128)(2,1)S(1)}, bf16[8,2,128,128]{3,2,1,0:T(8,128)(2,1)S(1)}, u32[]{:S(2)}, u32[]{:S(2)}) collective-permute-start(bf16[8,2,128,128]{3,2,1,0:T(8,128)(2,1)S(1)} %get-tuple-element.15), channel_id=1, source_target_pairs={{0,16},{1,17},{2,18},{3,19},{4,20},{5,21},{6,22},{7,23},{8,24},{9,... | collective-permute-start | bytes 1572872 | tf_op jit(solution)/shard_map/ppermute | solution.py:284
  112.2 31.3 %all-to-all-start.3 = ((bf16[32,128,128]{2,1,0:T(8,128)(2,1)}), bf16[32,128,128]{2,1,0:T(8,128)(2,1)S(1)}, u32[]{:S(2)}, u32[]{:S(2)}) async-start(bf16[32,128,128]{2,1,0:T(8,128)(2,1)} %bitcast.2), calls=%async_computation.3 | async-start | bytes 2097152 | tf_op jit(solution)/shard_map/all_to_all | solution.py:273
  120.7 26.4 %collective-permute-start.4 = (bf16[16,4,128,128]{3,2,1,0:T(8,128)(2,1)}, bf16[16,4,128,128]{3,2,1,0:T(8,128)(2,1)}, u32[]{:S(2)}, u32[]{:S(2)}) collective-permute-start(bf16[16,4,128,128]{3,2,1,0:T(8,128)(2,1)} %get-tuple-element.9), channel_id=1, source_target_pairs={{32,0},{64,32},{96,64},{128,96},{160,128},{192,160},{224,192},{33,... | collective-permute-start | bytes 6291464 | tf_op jit(solution)/shard_map/ppermute | solution.py:317
  122.6 27.7 %collective-permute-start.3 = (bf16[16,4,128,128]{3,2,1,0:T(8,128)(2,1)}, bf16[16,4,128,128]{3,2,1,0:T(8,128)(2,1)}, u32[]{:S(2)}, u32[]{:S(2)}) collective-permute-start(bf16[16,4,128,128]{3,2,1,0:T(8,128)(2,1)} %get-tuple-element.10), channel_id=1, source_target_pairs={{0,32},{32,64},{64,96},{96,128},{128,160},{160,192},{192,224},{1,3... | collective-permute-start | bytes 6291464 | tf_op jit(solution)/shard_map/ppermute | solution.py:316
  125.0 25.3 %copy-start = (s32[2,16,64]{2,1,0:T(8,128)S(1)}, s32[2,16,64]{2,1,0:T(8,128)}, u32[]{:S(2)}) copy-start(s32[2,16,64]{2,1,0:T(8,128)} %get-tuple-element.7.slot_ids) | copy-start | bytes 24580
  143.6 32.7 %all-to-all-start = ((bf16[32,128,128]{2,1,0:T(8,128)(2,1)}), bf16[32,128,128]{2,1,0:T(8,128)(2,1)S(1)}, u32[]{:S(2)}, u32[]{:S(2)}) async-start(bf16[32,128,128]{2,1,0:T(8,128)(2,1)} %bitcast.1), calls=%async_computation | async-start | bytes 2097152 | tf_op jit(solution)/shard_map/all_to_all | solution.py:273
  176.3 32.7 %all-to-all-start.4 = ((bf16[32,128,128]{2,1,0:T(8,128)(2,1)}), bf16[32,128,128]{2,1,0:T(8,128)(2,1)S(1)}, u32[]{:S(2)}, u32[]{:S(2)}) async-start(bf16[32,128,128]{2,1,0:T(8,128)(2,1)} %shard_map.49), calls=%async_computation.4 | async-start | bytes 2097152 | tf_op jit(solution)/shard_map/all_to_all | solution.py:273
  209.0 33.5 %all-to-all-start.2 = ((bf16[32,128,128]{2,1,0:T(8,128)(2,1)}), bf16[32,128,128]{2,1,0:T(8,128)(2,1)S(1)}, u32[]{:S(2)}, u32[]{:S(2)}) async-start(bf16[32,128,128]{2,1,0:T(8,128)(2,1)} %shard_map.48), calls=%async_computation.2 | async-start | bytes 2097152 | tf_op jit(solution)/shard_map/all_to_all | solution.py:268
  213.8 14.8 %collective-permute-start.7 = (bf16[8,128,128]{2,1,0:T(8,128)(2,1)S(1)}, bf16[8,128,128]{2,1,0:T(8,128)(2,1)S(1)}, u32[]{:S(2)}, u32[]{:S(2)}) collective-permute-start(bf16[8,128,128]{2,1,0:T(8,128)(2,1)S(1)} %get-tuple-element.16), channel_id=1, source_target_pairs={{0,8},{1,9},{2,10},{3,11},{4,12},{5,13},{6,14},{7,15},{8,16},{9,17... | collective-permute-start | bytes 786440 | tf_op jit(solution)/shard_map/ppermute | solution.py:284
  215.7 23.9 %collective-permute-start.6 = (bf16[8,128,128]{2,1,0:T(8,128)(2,1)S(1)}, bf16[8,128,128]{2,1,0:T(8,128)(2,1)S(1)}, u32[]{:S(2)}, u32[]{:S(2)}) collective-permute-start(bf16[8,128,128]{2,1,0:T(8,128)(2,1)S(1)} %get-tuple-element.17), channel_id=1, source_target_pairs={{0,16},{1,17},{2,18},{3,19},{4,20},{5,21},{6,22},{7,23},{8,24},{9,... | collective-permute-start | bytes 786440 | tf_op jit(solution)/shard_map/ppermute | solution.py:284
  218.4 21.2 %collective-permute-start.5 = (bf16[8,128,128]{2,1,0:T(8,128)(2,1)S(1)}, bf16[8,128,128]{2,1,0:T(8,128)(2,1)S(1)}, u32[]{:S(2)}, u32[]{:S(2)}) collective-permute-start(bf16[8,128,128]{2,1,0:T(8,128)(2,1)S(1)} %get-tuple-element.18), channel_id=1, source_target_pairs={{0,24},{1,25},{2,26},{3,27},{4,28},{5,29},{6,30},{7,31},{8,0},{9,1... | collective-permute-start | bytes 786440 | tf_op jit(solution)/shard_map/ppermute | solution.py:284

commit v9 on v8

--- a/solution.py
+++ b/solution.py
@@ -173,6 +173,12 @@
     def pair_of(turn, by):
         return (((here_x + by) & 3) << 3) + turn
 
+    here_z = lax.axis_index("seq") & 7
+
+    def query_of(turn, by):
+        place = (here_z - turn) & 7 if chunk == 0 else turn
+        return place * ALONG_X + -by % ALONG_X
+
     def score_pair(row, tile_query, slot):
         ids = [slot_ids[0, slot + i, row] for i in range(2)]
         both = jnp.concatenate([keys[k >> 1, k & 1] for k in ids], axis=0)
@@ -196,7 +202,7 @@
     best = None
     first_row = pair_of(0, 0) * CHUNKS + chunk
     for slot in range(0, KSEL, 2):
-        score = score_pair(first_row, query[0], slot)
+        score = score_pair(first_row, query[query_of(0, 0)], slot)
         scores[0, slot // 2] = score
         best = fold(best, score)
     put_top(0, best)
@@ -209,7 +215,7 @@
             later_by = (by + 1) % ALONG_X
             later_turn = turn if later_by else jnp.minimum(turn + 1, ALONG_Z - 1)
             tile = turn * ALONG_X + -by % ALONG_X
-            later = later_turn * ALONG_X + -later_by % ALONG_X
+            later = query_of(later_turn, later_by)
             pair = pair_of(turn, by)
             row = pair * CHUNKS + chunk
             later_row = pair_of(later_turn, later_by) * CHUNKS + chunk
@@ -298,6 +304,25 @@
     ]
 
 
+def shift_z(blocks, by):
+    pairs = [
+        (x * ALONG_Z + z, x * ALONG_Z + (z + by) % ALONG_Z)
+        for x in range(ALONG_X)
+        for z in range(ALONG_Z)
+    ]
+    return lax.ppermute(blocks, "seq", pairs)
+
+
+def queries_by_z(blocks):
+    blocks = blocks.reshape(ALONG_Z, ALONG_X, TILE, HEAD_DIM)
+    z = lax.axis_index("seq") % ALONG_Z
+    parts = [None] * ALONG_Z
+    for by in (0, 4, 3, 5, 2, 6, 1, 7):
+        part = lax.dynamic_slice_in_dim(blocks, (z + by) % ALONG_Z, 1, axis=0)
+        parts[by] = shift_z(part, by) if by else part
+    return jnp.concatenate(parts, axis=0).reshape(-1, TILE, HEAD_DIM)
+
+
 def outputs_by_x(blocks):
     blocks = blocks.reshape(ALONG_Z, ALONG_X, TILE, HEAD_DIM)
     return [
@@ -311,11 +336,12 @@
     blocks, ids = split_pairs(keys_values, extents, tile_lists)
     first, second = queries_by_x(queries)
     own = exchange(blocks)
+    first = queries_by_z(first)
+    own, first = lax.optimization_barrier((own, first))
     half = seq_size // 2
     ends = tm_size - 1
     left = lax.ppermute(own[half:], "tm", [(i, i + 1) for i in range(ends)])
     right = lax.ppermute(own[:half], "tm", [(i + 1, i) for i in range(ends)])
-    first = exchange_z(first)
     second = exchange_z(second)
     first_out = exchange_z(attend(0, ids, first, left, own, right))
     first_out = outputs_by_x(first_out)

time: 245 us -> 253 us (1.033)
  starting transfers between devices: 42.5 us -> 64.4 us
  waiting for transfers between devices: 146 us -> 133 us
    all_to_all x2, waiting for transfers between devices: 41.8 us -> 1.34 us  [exchange(): lax.all_to_all(blocks, 'seq', split_axis=0, concat_axis=0, tiled=True)]
    ppermute x0 -> x7, waiting for transfers between devices: none -> 40 us  [shift_z(): return lax.ppermute(blocks, 'seq', pairs)]
    all_to_all x3 -> x2, waiting for transfers between devices: 38.4 us -> 11.1 us  [exchange_z(): lax.all_to_all(blocks, 'seq', split_axis=0, concat_axis=0, tiled=True, ax...]
    ppermute x0 -> x7, starting transfers between devices: none -> 20 us  [shift_z(): return lax.ppermute(blocks, 'seq', pairs)]
    ppermute x1, waiting for transfers between devices: 0.01 us -> 14 us  [per_device(): right = lax.ppermute(own[:half], 'tm', [(i + 1, i) for i in range(ends)])]
    all_to_all x3 -> x2, starting transfers between devices: 10.7 us -> 12.8 us  [exchange_z(): lax.all_to_all(blocks, 'seq', split_axis=0, concat_axis=0, tiled=True, ax...]
  transfers between devices with their start and end apart: 13 -> 19, of which waited for: 10 -> 12; matrix products, arithmetic and copies ran while one was open for 4% -> 2% of each run, Pallas kernels for 16% -> 15%
where the time goes in v9:
time: 253 us; the launch traced here: 252 us
  waiting for transfers between devices  133 us (53%)
  starting transfers between devices  64.4 us (25%)
  Pallas kernels  44 us (17%)
  local copies, waits for them, and re-layouts  8.88 us (4%)
    ppermute x6, waiting for transfers between devices, shift_x(): return lax.ppermute(blocks, 'seq', pairs)  62.9 us
    ppermute x7, waiting for transfers between devices, shift_z(): return lax.ppermute(blocks, 'seq', pairs)  40 us
    pallas_call x2, Pallas kernels, attend(): pl.pallas_call(functools.partial(attend_kernel, chunk), in_specs=[scalar,...  34 us
    ppermute x7, starting transfers between devices, shift_z(): return lax.ppermute(blocks, 'seq', pairs)  20 us
    all_to_all x2, starting transfers between devices, exchange(): lax.all_to_all(blocks, 'seq', split_axis=0, concat_axis=0, tiled=True)  15.9 us
    ppermute x1, waiting for transfers between devices, per_device(): right = lax.ppermute(own[:half], 'tm', [(i + 1, i) for i in range(ends)])  14 us
    all_to_all x2, starting transfers between devices, exchange_z(): lax.all_to_all(blocks, 'seq', split_axis=0, concat_axis=0, tiled=True, ax...  12.8 us
    ppermute x6, starting transfers between devices, shift_x(): return lax.ppermute(blocks, 'seq', pairs)  11.3 us
  transfers between devices with their start and end apart: 19, of which 12 were waited for; matrix products, arithmetic and copies ran while one was open for 2% of the time, Pallas kernels for 15%

profile of v9, /device:TPU:8, one launch (start us, length us, event | category | flops | bytes accessed | tf_op | source)
XLA Modules:
  0.0 252.2 jit_solution(9602313544645895573)
XLA Ops:
  0.0 4.0 %shard_map.46 = (bf16[32,4,128,128]{3,2,1,0:T(8,128)(2,1)}, s32[2,16,64]{2,1,0:T(8,128)}) custom-call(s32[3,32]{1,0:T(4,128)} %extents.1, s32[16,64]{1,0:T(8,128)} %bitcast.22, bf16[2,256,4096]{2,1,0:T(8,128)(2,1)} %pair_ref.1), custom_call_target="tpu_custom_call" | custom-call | tf_op jit(solution)/shard_map/pallas_call | solution.py:73
  4.0 11.4 %all-to-all-start.1 = ((bf16[32,4,128,128]{3,2,1,0:T(8,128)(2,1)}), bf16[32,4,128,128]{3,2,1,0:T(8,128)(2,1)}, u32[]{:S(2)}, u32[]{:S(2)}) async-start(bf16[32,4,128,128]{3,2,1,0:T(8,128)(2,1)} %get-tuple-element.10), calls=%async_computation.1 | async-start | bytes 8388608 | tf_op jit(solution)/shard_map/all_to_all | solution.py:274
  15.6 2.7 %shard_map.47 = bf16[32,2,128,128]{3,2,1,0:T(8,128)(2,1)} custom-call(bf16[256,4096]{1,0:T(8,128)(2,1)} %query_ref.1), custom_call_target="tpu_custom_call" | custom-call | bytes 4194304 | tf_op jit(solution)/shard_map/pallas_call | solution.py:33
  19.8 1.8 collective-permute-start
  23.1 2.0 collective-permute-start.1
  26.4 23.5 %collective-permute-done = bf16[8,2,128,128]{3,2,1,0:T(8,128)(2,1)} collective-permute-done((bf16[8,2,128,128]{3,2,1,0:T(8,128)(2,1)S(1)}, bf16[8,2,128,128]{3,2,1,0:T(8,128)(2,1)}, u32[]{:S(2)}, u32[]{:S(2)}) %collective-permute-start) | collective-permute-done | bytes 524320 | tf_op jit(solution)/shard_map/ppermute | solution.py:290
  51.0 19.7 %collective-permute-done.1 = bf16[8,2,128,128]{3,2,1,0:T(8,128)(2,1)S(1)} collective-permute-done((bf16[8,2,128,128]{3,2,1,0:T(8,128)(2,1)S(1)}, bf16[8,2,128,128]{3,2,1,0:T(8,128)(2,1)S(1)}, u32[]{:S(2)}, u32[]{:S(2)}) %collective-permute-start.1) | collective-permute-done | bytes 524320 | tf_op jit(solution)/shard_map/ppermute | solution.py:290
  70.9 8.5 %collective-permute-start.3 = (bf16[1,4,128,128]{3,2,1,0:T(8,128)(2,1)S(1)}, bf16[1,4,128,128]{3,2,1,0:T(8,128)(2,1)S(1)}, u32[]{:S(2)}, u32[]{:S(2)}) collective-permute-start(bf16[1,4,128,128]{3,2,1,0:T(8,128)(2,1)S(1)} %get-tuple-element.30), channel_id=1, source_target_pairs={{0,1},{1,2},{2,3},{3,4},{4,5},{5,6},{6,7},{7,0},{8,9},{9,10},{10,1... | collective-permute-start | bytes 393224 | tf_op jit(solution)/shard_map/ppermute | solution.py:313
  79.4 2.6 %collective-permute-start.4 = (bf16[1,4,128,128]{3,2,1,0:T(8,128)(2,1)S(1)}, bf16[1,4,128,128]{3,2,1,0:T(8,128)(2,1)S(1)}, u32[]{:S(2)}, u32[]{:S(2)}) collective-permute-start(bf16[1,4,128,128]{3,2,1,0:T(8,128)(2,1)S(1)} %get-tuple-element.29), channel_id=1, source_target_pairs={{0,2},{1,3},{2,4},{3,5},{4,6},{5,7},{6,0},{7,1},{8,10},{9,11},{10,... | collective-permute-start | bytes 393224 | tf_op jit(solution)/shard_map/ppermute | solution.py:313
  83.6 3.9 %collective-permute-start.7 = (bf16[1,4,128,128]{3,2,1,0:T(8,128)(2,1)S(1)}, bf16[1,4,128,128]{3,2,1,0:T(8,128)(2,1)S(1)}, u32[]{:S(2)}, u32[]{:S(2)}) collective-permute-start(bf16[1,4,128,128]{3,2,1,0:T(8,128)(2,1)S(1)} %get-tuple-element.26), channel_id=1, source_target_pairs={{0,5},{1,6},{2,7},{3,0},{4,1},{5,2},{6,3},{7,4},{8,13},{9,14},{10,... | collective-permute-start | bytes 393224 | tf_op jit(solution)/shard_map/ppermute | solution.py:313
  87.5 25.5 %collective-permute-done.3 = bf16[1,4,128,128]{3,2,1,0:T(8,128)(2,1)S(1)} collective-permute-done((bf16[1,4,128,128]{3,2,1,0:T(8,128)(2,1)S(1)}, bf16[1,4,128,128]{3,2,1,0:T(8,128)(2,1)S(1)}, u32[]{:S(2)}, u32[]{:S(2)}) %collective-permute-start.3) | collective-permute-done | bytes 131104 | tf_op jit(solution)/shard_map/ppermute | solution.py:313
  113.1 6.5 %collective-permute-done.4 = bf16[1,4,128,128]{3,2,1,0:T(8,128)(2,1)S(1)} collective-permute-done((bf16[1,4,128,128]{3,2,1,0:T(8,128)(2,1)S(1)}, bf16[1,4,128,128]{3,2,1,0:T(8,128)(2,1)S(1)}, u32[]{:S(2)}, u32[]{:S(2)}) %collective-permute-start.4) | collective-permute-done | bytes 131104 | tf_op jit(solution)/shard_map/ppermute | solution.py:313
  119.6 3.4 %collective-permute-start.6 = (bf16[1,4,128,128]{3,2,1,0:T(8,128)(2,1)S(1)}, bf16[1,4,128,128]{3,2,1,0:T(8,128)(2,1)S(1)}, u32[]{:S(2)}, u32[]{:S(2)}) collective-permute-start(bf16[1,4,128,128]{3,2,1,0:T(8,128)(2,1)S(1)} %get-tuple-element.27), channel_id=1, source_target_pairs={{0,4},{1,5},{2,6},{3,7},{4,0},{5,1},{6,2},{7,3},{8,12},{9,13},{10,... | collective-permute-start | bytes 393224 | tf_op jit(solution)/shard_map/ppermute | solution.py:313
  123.0 5.6 %collective-permute-done.5 = bf16[1,4,128,128]{3,2,1,0:T(8,128)(2,1)S(1)} collective-permute-done((bf16[1,4,128,128]{3,2,1,0:T(8,128)(2,1)S(1)}, bf16[1,4,128,128]{3,2,1,0:T(8,128)(2,1)S(1)}, u32[]{:S(2)}, u32[]{:S(2)}) %collective-permute-start.5) | collective-permute-done | bytes 131104 | tf_op jit(solution)/shard_map/ppermute | solution.py:313
  128.6 2.4 collective-permute-done.6
  131.2 4.9 %fusion = (bf16[16,4,128,128]{3,2,1,0:T(8,128)(2,1)}, bf16[16,4,128,128]{3,2,1,0:T(8,128)(2,1)}) fusion(bf16[32,4,128,128]{3,2,1,0:T(8,128)(2,1)} %all-to-all-done.1.own_hbm), kind=kLoop, calls=%fused_computation.26 | loop fusion | bytes 8388608 | tf_op jit(solution)/shard_map/slice | solution.py:344
  136.1 1.9 collective-permute-start.11
  138.0 2.4 collective-permute-start.10
  141.5 6.3 %all-to-all-start = ((bf16[32,128,128]{2,1,0:T(8,128)(2,1)}), bf16[32,128,128]{2,1,0:T(8,128)(2,1)S(1)}, u32[]{:S(2)}, u32[]{:S(2)}) async-start(bf16[32,128,128]{2,1,0:T(8,128)(2,1)} %bitcast.1), calls=%async_computation | async-start | bytes 2097152 | tf_op jit(solution)/shard_map/all_to_all | solution.py:279
  147.9 14.0 %collective-permute-done.11.right_hbm = bf16[16,4,128,128]{3,2,1,0:T(8,128)(2,1)} collective-permute-done((bf16[16,4,128,128]{3,2,1,0:T(8,128)(2,1)}, bf16[16,4,128,128]{3,2,1,0:T(8,128)(2,1)}, u32[]{:S(2)}, u32[]{:S(2)}) %collective-permute-start.11) | collective-permute-done | bytes 2097184 | tf_op jit(solution)/shard_map/ppermute | solution.py:344
  161.8 3.8 %collective-permute-done.10.left_hbm = bf16[16,4,128,128]{3,2,1,0:T(8,128)(2,1)} collective-permute-done((bf16[16,4,128,128]{3,2,1,0:T(8,128)(2,1)}, bf16[16,4,128,128]{3,2,1,0:T(8,128)(2,1)}, u32[]{:S(2)}, u32[]{:S(2)}) %collective-permute-start.10) | collective-permute-done | bytes 2097184 | tf_op jit(solution)/shard_map/ppermute | solution.py:343
  165.6 17.0 %shard_map.49 = bf16[32,128,128]{2,1,0:T(8,128)(2,1)} custom-call(s32[2,16,64]{2,1,0:T(8,128)S(1)} %copy-done, bf16[32,128,128]{2,1,0:T(8,128)(2,1)S(1)} %bitcast.20, bf16[16,4,128,128]{3,2,1,0:T(8,128)(2,1)} %collective-permute-done.10.left_hbm, bf16[32,4,128,128]{3,2,1,0:T(8,128)(2,1)} %all-to-all-done.1.own_hbm, ...), custom_call_target="tpu_custom_call" | custom-call | flops 4294967296 | bytes 12582912 | tf_op jit(solution)/shard_map/pallas_call | solution.py:250
  182.6 6.4 %all-to-all-start.3 = ((bf16[32,128,128]{2,1,0:T(8,128)(2,1)}), bf16[32,128,128]{2,1,0:T(8,128)(2,1)S(1)}, u32[]{:S(2)}, u32[]{:S(2)}) async-start(bf16[32,128,128]{2,1,0:T(8,128)(2,1)} %shard_map.49), calls=%async_computation.3 | async-start | bytes 2097152 | tf_op jit(solution)/shard_map/all_to_all | solution.py:279
  189.1 17.1 %shard_map.48 = bf16[32,128,128]{2,1,0:T(8,128)(2,1)} custom-call(s32[2,16,64]{2,1,0:T(8,128)S(1)} %copy-done, bf16[32,128,128]{2,1,0:T(8,128)(2,1)S(1)} %all-to-all-done.query_hbm, bf16[16,4,128,128]{3,2,1,0:T(8,128)(2,1)} %collective-permute-done.10.left_hbm, bf16[32,4,128,128]{3,2,1,0:T(8,128)(2,1)} %all-to-all-done.1.own_hbm, ...), custom_call_target="tpu_custom_call" | custom-call | flops 4294967296 | bytes 12582912 | tf_op jit(solution)/shard_map/pallas_call | solution.py:250
  206.1 11.1 %all-to-all-done.3 = bf16[32,128,128]{2,1,0:T(8,128)(2,1)S(1)} async-done(((bf16[32,128,128]{2,1,0:T(8,128)(2,1)}), bf16[32,128,128]{2,1,0:T(8,128)(2,1)S(1)}, u32[]{:S(2)}, u32[]{:S(2)}) %all-to-all-start.3) | async-done | bytes 1048608 | tf_op jit(solution)/shard_map/all_to_all | solution.py:279
  217.2 4.5 %all-to-all-start.2 = ((bf16[32,128,128]{2,1,0:T(8,128)(2,1)}), bf16[32,128,128]{2,1,0:T(8,128)(2,1)S(1)}, u32[]{:S(2)}, u32[]{:S(2)}) async-start(bf16[32,128,128]{2,1,0:T(8,128)(2,1)} %shard_map.48), calls=%async_computation.2 | async-start | bytes 2097152 | tf_op jit(solution)/shard_map/all_to_all | solution.py:274
  221.7 1.9 collective-permute-start.14
  223.6 2.7 %collective-permute-start.13 = (bf16[8,128,128]{2,1,0:T(8,128)(2,1)S(1)}, bf16[8,128,128]{2,1,0:T(8,128)(2,1)S(1)}, u32[]{:S(2)}, u32[]{:S(2)}) collective-permute-start(bf16[8,128,128]{2,1,0:T(8,128)(2,1)S(1)} %get-tuple-element.21), channel_id=1, source_target_pairs={{0,16},{1,17},{2,18},{3,19},{4,20},{5,21},{6,22},{7,23},{8,24},{9,... | collective-permute-start | bytes 786440 | tf_op jit(solution)/shard_map/ppermute | solution.py:290
  227.7 8.8 %collective-permute-done.14.refs_3_ = bf16[8,128,128]{2,1,0:T(8,128)(2,1)S(1)} collective-permute-done((bf16[8,128,128]{2,1,0:T(8,128)(2,1)S(1)}, bf16[8,128,128]{2,1,0:T(8,128)(2,1)S(1)}, u32[]{:S(2)}, u32[]{:S(2)}) %collective-permute-start.14) | collective-permute-done | bytes 262176 | tf_op jit(solution)/shard_map/ppermute | solution.py:290
  236.6 10.9 %collective-permute-done.13.refs_2_ = bf16[8,128,128]{2,1,0:T(8,128)(2,1)S(1)} collective-permute-done((bf16[8,128,128]{2,1,0:T(8,128)(2,1)S(1)}, bf16[8,128,128]{2,1,0:T(8,128)(2,1)S(1)}, u32[]{:S(2)}, u32[]{:S(2)}) %collective-permute-start.13) | collective-permute-done | bytes 262176 | tf_op jit(solution)/shard_map/ppermute | solution.py:290
  247.5 1.6 shard_map.50.refs_1_
  250.4 1.6 shard_map.51
  (31 shorter events, 11.1 us)
Async XLA Ops:
  4.0 127.1 %all-to-all-start.1 = ((bf16[32,4,128,128]{3,2,1,0:T(8,128)(2,1)}), bf16[32,4,128,128]{3,2,1,0:T(8,128)(2,1)}, u32[]{:S(2)}, u32[]{:S(2)}) async-start(bf16[32,4,128,128]{3,2,1,0:T(8,128)(2,1)} %get-tuple-element.10), calls=%async_computation.1 | async-start | bytes 8388608 | tf_op jit(solution)/shard_map/all_to_all | solution.py:274
  19.8 30.0 %collective-permute-start = (bf16[8,2,128,128]{3,2,1,0:T(8,128)(2,1)S(1)}, bf16[8,2,128,128]{3,2,1,0:T(8,128)(2,1)}, u32[]{:S(2)}, u32[]{:S(2)}) collective-permute-start(bf16[8,2,128,128]{3,2,1,0:T(8,128)(2,1)S(1)} %get-tuple-element.17), channel_id=1, source_target_pairs={{0,8},{1,9},{2,10},{3,11},{4,12},{5,13},{6,14},{7,15},{8,16},{9,17... | collective-permute-start | bytes 1572872 | tf_op jit(solution)/shard_map/ppermute | solution.py:290
  21.6 29.3 %collective-permute-start.2 = (bf16[8,2,128,128]{3,2,1,0:T(8,128)(2,1)S(1)}, bf16[8,2,128,128]{3,2,1,0:T(8,128)(2,1)S(1)}, u32[]{:S(2)}, u32[]{:S(2)}) collective-permute-start(bf16[8,2,128,128]{3,2,1,0:T(8,128)(2,1)S(1)} %get-tuple-element.18), channel_id=1, source_target_pairs={{0,24},{1,25},{2,26},{3,27},{4,28},{5,29},{6,30},{7,31},{8,0},{9,1... | collective-permute-start | bytes 1572872 | tf_op jit(solution)/shard_map/ppermute | solution.py:290
  23.1 47.6 %collective-permute-start.1 = (bf16[8,2,128,128]{3,2,1,0:T(8,128)(2,1)S(1)}, bf16[8,2,128,128]{3,2,1,0:T(8,128)(2,1)S(1)}, u32[]{:S(2)}, u32[]{:S(2)}) collective-permute-start(bf16[8,2,128,128]{3,2,1,0:T(8,128)(2,1)S(1)} %get-tuple-element.19), channel_id=1, source_target_pairs={{0,16},{1,17},{2,18},{3,19},{4,20},{5,21},{6,22},{7,23},{8,24},{9,... | collective-permute-start | bytes 1572872 | tf_op jit(solution)/shard_map/ppermute | solution.py:290
  70.9 42.0 %collective-permute-start.3 = (bf16[1,4,128,128]{3,2,1,0:T(8,128)(2,1)S(1)}, bf16[1,4,128,128]{3,2,1,0:T(8,128)(2,1)S(1)}, u32[]{:S(2)}, u32[]{:S(2)}) collective-permute-start(bf16[1,4,128,128]{3,2,1,0:T(8,128)(2,1)S(1)} %get-tuple-element.30), channel_id=1, source_target_pairs={{0,1},{1,2},{2,3},{3,4},{4,5},{5,6},{6,7},{7,0},{8,9},{9,10},{10,1... | collective-permute-start | bytes 393224 | tf_op jit(solution)/shard_map/ppermute | solution.py:313
  79.4 40.1 %collective-permute-start.4 = (bf16[1,4,128,128]{3,2,1,0:T(8,128)(2,1)S(1)}, bf16[1,4,128,128]{3,2,1,0:T(8,128)(2,1)S(1)}, u32[]{:S(2)}, u32[]{:S(2)}) collective-permute-start(bf16[1,4,128,128]{3,2,1,0:T(8,128)(2,1)S(1)} %get-tuple-element.29), channel_id=1, source_target_pairs={{0,2},{1,3},{2,4},{3,5},{4,6},{5,7},{6,0},{7,1},{8,10},{9,11},{10,... | collective-permute-start | bytes 393224 | tf_op jit(solution)/shard_map/ppermute | solution.py:313
  82.1 49.1 %collective-permute-start.9 = (bf16[1,4,128,128]{3,2,1,0:T(8,128)(2,1)S(1)}, bf16[1,4,128,128]{3,2,1,0:T(8,128)(2,1)S(1)}, u32[]{:S(2)}, u32[]{:S(2)}) collective-permute-start(bf16[1,4,128,128]{3,2,1,0:T(8,128)(2,1)S(1)} %get-tuple-element.24), channel_id=1, source_target_pairs={{0,7},{1,0},{2,1},{3,2},{4,3},{5,4},{6,5},{7,6},{8,15},{9,8},{10,9... | collective-permute-start | bytes 393224 | tf_op jit(solution)/shard_map/ppermute | solution.py:313
  82.2 48.9 %collective-permute-start.8 = (bf16[1,4,128,128]{3,2,1,0:T(8,128)(2,1)S(1)}, bf16[1,4,128,128]{3,2,1,0:T(8,128)(2,1)S(1)}, u32[]{:S(2)}, u32[]{:S(2)}) collective-permute-start(bf16[1,4,128,128]{3,2,1,0:T(8,128)(2,1)S(1)} %get-tuple-element.25), channel_id=1, source_target_pairs={{0,6},{1,7},{2,0},{3,1},{4,2},{5,3},{6,4},{7,5},{8,14},{9,15},{10,... | collective-permute-start | bytes 393224 | tf_op jit(solution)/shard_map/ppermute | solution.py:313
  83.6 47.5 %collective-permute-start.7 = (bf16[1,4,128,128]{3,2,1,0:T(8,128)(2,1)S(1)}, bf16[1,4,128,128]{3,2,1,0:T(8,128)(2,1)S(1)}, u32[]{:S(2)}, u32[]{:S(2)}) collective-permute-start(bf16[1,4,128,128]{3,2,1,0:T(8,128)(2,1)S(1)} %get-tuple-element.26), channel_id=1, source_target_pairs={{0,5},{1,6},{2,7},{3,0},{4,1},{5,2},{6,3},{7,4},{8,13},{9,14},{10,... | collective-permute-start | bytes 393224 | tf_op jit(solution)/shard_map/ppermute | solution.py:313
  113.0 15.6 %collective-permute-start.5 = (bf16[1,4,128,128]{3,2,1,0:T(8,128)(2,1)S(1)}, bf16[1,4,128,128]{3,2,1,0:T(8,128)(2,1)S(1)}, u32[]{:S(2)}, u32[]{:S(2)}) collective-permute-start(bf16[1,4,128,128]{3,2,1,0:T(8,128)(2,1)S(1)} %get-tuple-element.28), channel_id=1, source_target_pairs={{0,3},{1,4},{2,5},{3,6},{4,7},{5,0},{6,1},{7,2},{8,11},{9,12},{10,... | collective-permute-start | bytes 393224 | tf_op jit(solution)/shard_map/ppermute | solution.py:313
  119.6 11.5 %collective-permute-start.6 = (bf16[1,4,128,128]{3,2,1,0:T(8,128)(2,1)S(1)}, bf16[1,4,128,128]{3,2,1,0:T(8,128)(2,1)S(1)}, u32[]{:S(2)}, u32[]{:S(2)}) collective-permute-start(bf16[1,4,128,128]{3,2,1,0:T(8,128)(2,1)S(1)} %get-tuple-element.27), channel_id=1, source_target_pairs={{0,4},{1,5},{2,6},{3,7},{4,0},{5,1},{6,2},{7,3},{8,12},{9,13},{10,... | collective-permute-start | bytes 393224 | tf_op jit(solution)/shard_map/ppermute | solution.py:313
  136.1 25.8 %collective-permute-start.11 = (bf16[16,4,128,128]{3,2,1,0:T(8,128)(2,1)}, bf16[16,4,128,128]{3,2,1,0:T(8,128)(2,1)}, u32[]{:S(2)}, u32[]{:S(2)}) collective-permute-start(bf16[16,4,128,128]{3,2,1,0:T(8,128)(2,1)} %get-tuple-element.13), channel_id=1, source_target_pairs={{32,0},{64,32},{96,64},{128,96},{160,128},{192,160},{224,192},{33,... | collective-permute-start | bytes 6291464 | tf_op jit(solution)/shard_map/ppermute | solution.py:344
  138.0 27.7 %collective-permute-start.10 = (bf16[16,4,128,128]{3,2,1,0:T(8,128)(2,1)}, bf16[16,4,128,128]{3,2,1,0:T(8,128)(2,1)}, u32[]{:S(2)}, u32[]{:S(2)}) collective-permute-start(bf16[16,4,128,128]{3,2,1,0:T(8,128)(2,1)} %get-tuple-element.14), channel_id=1, source_target_pairs={{0,32},{32,64},{64,96},{96,128},{128,160},{160,192},{192,224},{1,3... | collective-permute-start | bytes 6291464 | tf_op jit(solution)/shard_map/ppermute | solution.py:343
  140.4 25.3 %copy-start = (s32[2,16,64]{2,1,0:T(8,128)S(1)}, s32[2,16,64]{2,1,0:T(8,128)}, u32[]{:S(2)}) copy-start(s32[2,16,64]{2,1,0:T(8,128)} %get-tuple-element.9.slot_ids) | copy-start | bytes 24580
  141.5 41.1 %all-to-all-start = ((bf16[32,128,128]{2,1,0:T(8,128)(2,1)}), bf16[32,128,128]{2,1,0:T(8,128)(2,1)S(1)}, u32[]{:S(2)}, u32[]{:S(2)}) async-start(bf16[32,128,128]{2,1,0:T(8,128)(2,1)} %bitcast.1), calls=%async_computation | async-start | bytes 2097152 | tf_op jit(solution)/shard_map/all_to_all | solution.py:279
  182.6 34.6 %all-to-all-start.3 = ((bf16[32,128,128]{2,1,0:T(8,128)(2,1)}), bf16[32,128,128]{2,1,0:T(8,128)(2,1)S(1)}, u32[]{:S(2)}, u32[]{:S(2)}) async-start(bf16[32,128,128]{2,1,0:T(8,128)(2,1)} %shard_map.49), calls=%async_computation.3 | async-start | bytes 2097152 | tf_op jit(solution)/shard_map/all_to_all | solution.py:279
  217.2 33.3 %all-to-all-start.2 = ((bf16[32,128,128]{2,1,0:T(8,128)(2,1)}), bf16[32,128,128]{2,1,0:T(8,128)(2,1)S(1)}, u32[]{:S(2)}, u32[]{:S(2)}) async-start(bf16[32,128,128]{2,1,0:T(8,128)(2,1)} %shard_map.48), calls=%async_computation.2 | async-start | bytes 2097152 | tf_op jit(solution)/shard_map/all_to_all | solution.py:274
  221.7 14.8 %collective-permute-start.14 = (bf16[8,128,128]{2,1,0:T(8,128)(2,1)S(1)}, bf16[8,128,128]{2,1,0:T(8,128)(2,1)S(1)}, u32[]{:S(2)}, u32[]{:S(2)}) collective-permute-start(bf16[8,128,128]{2,1,0:T(8,128)(2,1)S(1)} %get-tuple-element.20), channel_id=1, source_target_pairs={{0,8},{1,9},{2,10},{3,11},{4,12},{5,13},{6,14},{7,15},{8,16},{9,17... | collective-permute-start | bytes 786440 | tf_op jit(solution)/shard_map/ppermute | solution.py:290
  223.6 23.9 %collective-permute-start.13 = (bf16[8,128,128]{2,1,0:T(8,128)(2,1)S(1)}, bf16[8,128,128]{2,1,0:T(8,128)(2,1)S(1)}, u32[]{:S(2)}, u32[]{:S(2)}) collective-permute-start(bf16[8,128,128]{2,1,0:T(8,128)(2,1)S(1)} %get-tuple-element.21), channel_id=1, source_target_pairs={{0,16},{1,17},{2,18},{3,19},{4,20},{5,21},{6,22},{7,23},{8,24},{9,... | collective-permute-start | bytes 786440 | tf_op jit(solution)/shard_map/ppermute | solution.py:290
  226.3 21.2 %collective-permute-start.12 = (bf16[8,128,128]{2,1,0:T(8,128)(2,1)S(1)}, bf16[8,128,128]{2,1,0:T(8,128)(2,1)S(1)}, u32[]{:S(2)}, u32[]{:S(2)}) collective-permute-start(bf16[8,128,128]{2,1,0:T(8,128)(2,1)S(1)} %get-tuple-element.22), channel_id=1, source_target_pairs={{0,24},{1,25},{2,26},{3,27},{4,28},{5,29},{6,30},{7,31},{8,0},{9,1... | collective-permute-start | bytes 786440 | tf_op jit(solution)/shard_map/ppermute | solution.py:290

commit v10 on v8

--- a/solution.py
+++ b/solution.py
@@ -92,11 +92,26 @@
 
 def join_kernel(chunk, count, *refs):
     sources, (out_hbm, held, in_sems, out_sem) = refs[:count], refs[-4:]
+    if count == 1:
+        rows = pl.ds(chunk * TILE, TILE)
+        writes = [
+            pltpu.make_async_copy(
+                sources[0].at[head],
+                out_hbm.at[rows, pl.ds(head * HEAD_DIM, HEAD_DIM)],
+                in_sems.at[head],
+            )
+            for head in range(sources[0].shape[0])
+        ]
+        for copy in writes:
+            copy.start()
+        for copy in writes:
+            copy.wait()
+        return
     here_x = lax.axis_index("seq") >> 3
     reads = []
     for by, source_hbm in enumerate(sources):
         for place in range(source_hbm.shape[0]):
-            head = place if count == 1 else ((here_x + by) & 3) * ALONG_Z + place
+            head = ((here_x + by) & 3) * ALONG_Z + place
             columns = pl.ds(pl.multiple_of(head * HEAD_DIM, HEAD_DIM), HEAD_DIM)
             reads.append(
                 pltpu.make_async_copy(
@@ -116,9 +131,10 @@
     heads = sum(source.shape[0] for source in sources)
     width = heads * HEAD_DIM
     whole = pl.BlockSpec(memory_space=pl.ANY)
+    local = pl.BlockSpec(memory_space=pltpu.VMEM)
     return pl.pallas_call(
         functools.partial(join_kernel, chunk, len(sources)),
-        in_specs=[whole] * (len(sources) + len(joined)),
+        in_specs=[local if joined else whole] * len(sources) + [whole] * len(joined),
         out_specs=whole,
         out_shape=jax.ShapeDtypeStruct((CHUNKS * TILE, width), jnp.bfloat16),
         input_output_aliases={len(sources): 0} if joined else {},

time: 245 us -> 244 us (level)
  no operation moved by 1% of the time
where the time goes in v10:
time: 244 us
  waiting for transfers between devices  146 us (60%)
  Pallas kernels  43.8 us (18%)
  starting transfers between devices  42.5 us (17%)
  local copies, waits for them, and re-layouts  8.67 us (4%)
    ppermute x6, waiting for transfers between devices, shift_x(): return lax.ppermute(blocks, 'seq', pairs)  63.1 us
    all_to_all x2, waiting for transfers between devices, exchange(): lax.all_to_all(blocks, 'seq', split_axis=0, concat_axis=0, tiled=True)  41.8 us
    all_to_all x3, waiting for transfers between devices, exchange_z(): lax.all_to_all(blocks, 'seq', split_axis=0, concat_axis=0, tiled=True, ax...  38.4 us
    pallas_call x2, Pallas kernels, attend(): pl.pallas_call(functools.partial(attend_kernel, chunk), in_specs=[scalar,...  34.2 us
    all_to_all x2, starting transfers between devices, exchange(): lax.all_to_all(blocks, 'seq', split_axis=0, concat_axis=0, tiled=True)  16.2 us
    ppermute x6, starting transfers between devices, shift_x(): return lax.ppermute(blocks, 'seq', pairs)  11.3 us
    all_to_all x3, starting transfers between devices, exchange_z(): lax.all_to_all(blocks, 'seq', split_axis=0, concat_axis=0, tiled=True, ax...  10.7 us
    slice x1, local copies, waits for them, and re-layouts, per_device(): right = lax.ppermute(own[:half], 'tm', [(i + 1, i) for i in range(ends)])  4.9 us
  transfers between devices with their start and end apart: 13, of which 10 were waited for; matrix products, arithmetic and copies ran while one was open for 4% of the time, Pallas kernels for 16%

profile of v10, /device:TPU:8, one launch (start us, length us, event | category | flops | bytes accessed | tf_op | source)
XLA Modules:
  0.0 243.8 jit_solution(15929248552110393991)
XLA Ops:
  0.0 4.0 %shard_map.46 = (bf16[32,4,128,128]{3,2,1,0:T(8,128)(2,1)}, s32[2,16,64]{2,1,0:T(8,128)}) custom-call(s32[3,32]{1,0:T(4,128)} %extents.1, s32[16,64]{1,0:T(8,128)} %bitcast.21, bf16[2,256,4096]{2,1,0:T(8,128)(2,1)} %pair_ref.1), custom_call_target="tpu_custom_call" | custom-call | tf_op jit(solution)/shard_map/pallas_call | solution.py:73
  4.0 11.4 %all-to-all-start.1 = ((bf16[32,4,128,128]{3,2,1,0:T(8,128)(2,1)}), bf16[32,4,128,128]{3,2,1,0:T(8,128)(2,1)}, u32[]{:S(2)}, u32[]{:S(2)}) async-start(bf16[32,4,128,128]{3,2,1,0:T(8,128)(2,1)} %get-tuple-element.8), calls=%async_computation.1 | async-start | bytes 8388608 | tf_op jit(solution)/shard_map/all_to_all | solution.py:284
  15.5 2.7 %shard_map.47 = bf16[32,2,128,128]{3,2,1,0:T(8,128)(2,1)} custom-call(bf16[256,4096]{1,0:T(8,128)(2,1)} %query_ref.1), custom_call_target="tpu_custom_call" | custom-call | bytes 4194304 | tf_op jit(solution)/shard_map/pallas_call | solution.py:33
  18.3 1.5 constant_dynamic-slice_fusion.3
  19.8 1.8 collective-permute-start
  21.6 1.5 collective-permute-start.2
  23.1 2.0 collective-permute-start.1
  26.2 23.8 %collective-permute-done = bf16[8,2,128,128]{3,2,1,0:T(8,128)(2,1)} collective-permute-done((bf16[8,2,128,128]{3,2,1,0:T(8,128)(2,1)S(1)}, bf16[8,2,128,128]{3,2,1,0:T(8,128)(2,1)}, u32[]{:S(2)}, u32[]{:S(2)}) %collective-permute-start) | collective-permute-done | bytes 524320 | tf_op jit(solution)/shard_map/ppermute | solution.py:300
  51.1 19.6 %collective-permute-done.1 = bf16[8,2,128,128]{3,2,1,0:T(8,128)(2,1)S(1)} collective-permute-done((bf16[8,2,128,128]{3,2,1,0:T(8,128)(2,1)S(1)}, bf16[8,2,128,128]{3,2,1,0:T(8,128)(2,1)S(1)}, u32[]{:S(2)}, u32[]{:S(2)}) %collective-permute-start.1) | collective-permute-done | bytes 524320 | tf_op jit(solution)/shard_map/ppermute | solution.py:300
  71.8 40.4 %all-to-all-done.1.own_hbm = bf16[32,4,128,128]{3,2,1,0:T(8,128)(2,1)} async-done(((bf16[32,4,128,128]{3,2,1,0:T(8,128)(2,1)}), bf16[32,4,128,128]{3,2,1,0:T(8,128)(2,1)}, u32[]{:S(2)}, u32[]{:S(2)}) %all-to-all-start.1) | async-done | bytes 4194336 | tf_op jit(solution)/shard_map/all_to_all | solution.py:284
  112.2 3.6 %all-to-all-start.3 = ((bf16[32,128,128]{2,1,0:T(8,128)(2,1)}), bf16[32,128,128]{2,1,0:T(8,128)(2,1)S(1)}, u32[]{:S(2)}, u32[]{:S(2)}) async-start(bf16[32,128,128]{2,1,0:T(8,128)(2,1)} %bitcast.2), calls=%async_computation.3 | async-start | bytes 2097152 | tf_op jit(solution)/shard_map/all_to_all | solution.py:289
  115.8 4.9 %fusion = (bf16[16,4,128,128]{3,2,1,0:T(8,128)(2,1)}, bf16[16,4,128,128]{3,2,1,0:T(8,128)(2,1)}) fusion(bf16[32,4,128,128]{3,2,1,0:T(8,128)(2,1)} %all-to-all-done.1.own_hbm), kind=kLoop, calls=%fused_computation.11 | loop fusion | bytes 8388608 | tf_op jit(solution)/shard_map/slice | solution.py:333
  120.7 1.9 collective-permute-start.4
  122.6 2.4 collective-permute-start.3
  125.0 1.1 pad_maximum_fusion
  126.2 17.4 %all-to-all-done.3.query_hbm = bf16[32,128,128]{2,1,0:T(8,128)(2,1)S(1)} async-done(((bf16[32,128,128]{2,1,0:T(8,128)(2,1)}), bf16[32,128,128]{2,1,0:T(8,128)(2,1)S(1)}, u32[]{:S(2)}, u32[]{:S(2)}) %all-to-all-start.3) | async-done | bytes 1048608 | tf_op jit(solution)/shard_map/all_to_all | solution.py:289
  143.6 3.6 %all-to-all-start = ((bf16[32,128,128]{2,1,0:T(8,128)(2,1)}), bf16[32,128,128]{2,1,0:T(8,128)(2,1)S(1)}, u32[]{:S(2)}, u32[]{:S(2)}) async-start(bf16[32,128,128]{2,1,0:T(8,128)(2,1)} %bitcast.1), calls=%async_computation | async-start | bytes 2097152 | tf_op jit(solution)/shard_map/all_to_all | solution.py:289
  147.1 3.1 %collective-permute-done.3.left_hbm = bf16[16,4,128,128]{3,2,1,0:T(8,128)(2,1)} collective-permute-done((bf16[16,4,128,128]{3,2,1,0:T(8,128)(2,1)}, bf16[16,4,128,128]{3,2,1,0:T(8,128)(2,1)}, u32[]{:S(2)}, u32[]{:S(2)}) %collective-permute-start.3) | collective-permute-done | bytes 2097184 | tf_op jit(solution)/shard_map/ppermute | solution.py:332
  150.3 17.0 %shard_map.49 = bf16[32,128,128]{2,1,0:T(8,128)(2,1)} custom-call(s32[2,16,64]{2,1,0:T(8,128)S(1)} %copy-done, bf16[32,128,128]{2,1,0:T(8,128)(2,1)S(1)} %all-to-all-done.3.query_hbm, bf16[16,4,128,128]{3,2,1,0:T(8,128)(2,1)} %collective-permute-done.3.left_hbm, bf16[32,4,128,128]{3,2,1,0:T(8,128)(2,1)} %all-to-all-done.1.own_hbm, ...), custom_call_target="tpu_custom_call" | custom-call | flops 4294967296 | bytes 12582912 | tf_op jit(solution)/shard_map/pallas_call | solution.py:260
  167.3 8.9 %all-to-all-done.query_hbm = bf16[32,128,128]{2,1,0:T(8,128)(2,1)S(1)} async-done(((bf16[32,128,128]{2,1,0:T(8,128)(2,1)}), bf16[32,128,128]{2,1,0:T(8,128)(2,1)S(1)}, u32[]{:S(2)}, u32[]{:S(2)}) %all-to-all-start) | async-done | bytes 1048608 | tf_op jit(solution)/shard_map/all_to_all | solution.py:289
  176.3 3.6 %all-to-all-start.4 = ((bf16[32,128,128]{2,1,0:T(8,128)(2,1)}), bf16[32,128,128]{2,1,0:T(8,128)(2,1)S(1)}, u32[]{:S(2)}, u32[]{:S(2)}) async-start(bf16[32,128,128]{2,1,0:T(8,128)(2,1)} %shard_map.49), calls=%async_computation.4 | async-start | bytes 2097152 | tf_op jit(solution)/shard_map/all_to_all | solution.py:289
  179.8 17.1 %shard_map.48 = bf16[32,128,128]{2,1,0:T(8,128)(2,1)} custom-call(s32[2,16,64]{2,1,0:T(8,128)S(1)} %copy-done, bf16[32,128,128]{2,1,0:T(8,128)(2,1)S(1)} %all-to-all-done.query_hbm, bf16[16,4,128,128]{3,2,1,0:T(8,128)(2,1)} %collective-permute-done.3.left_hbm, bf16[32,4,128,128]{3,2,1,0:T(8,128)(2,1)} %all-to-all-done.1.own_hbm, ...), custom_call_target="tpu_custom_call" | custom-call | flops 4294967296 | bytes 12582912 | tf_op jit(solution)/shard_map/pallas_call | solution.py:260
  197.0 12.0 %all-to-all-done.4 = bf16[32,128,128]{2,1,0:T(8,128)(2,1)S(1)} async-done(((bf16[32,128,128]{2,1,0:T(8,128)(2,1)}), bf16[32,128,128]{2,1,0:T(8,128)(2,1)S(1)}, u32[]{:S(2)}, u32[]{:S(2)}) %all-to-all-start.4) | async-done | bytes 1048608 | tf_op jit(solution)/shard_map/all_to_all | solution.py:289
  209.0 4.7 %all-to-all-start.2 = ((bf16[32,128,128]{2,1,0:T(8,128)(2,1)}), bf16[32,128,128]{2,1,0:T(8,128)(2,1)S(1)}, u32[]{:S(2)}, u32[]{:S(2)}) async-start(bf16[32,128,128]{2,1,0:T(8,128)(2,1)} %shard_map.48), calls=%async_computation.2 | async-start | bytes 2097152 | tf_op jit(solution)/shard_map/all_to_all | solution.py:284
  213.8 1.9 collective-permute-start.7
  215.7 2.7 %collective-permute-start.6 = (bf16[8,128,128]{2,1,0:T(8,128)(2,1)S(1)}, bf16[8,128,128]{2,1,0:T(8,128)(2,1)S(1)}, u32[]{:S(2)}, u32[]{:S(2)}) collective-permute-start(bf16[8,128,128]{2,1,0:T(8,128)(2,1)S(1)} %get-tuple-element.17), channel_id=1, source_target_pairs={{0,16},{1,17},{2,18},{3,19},{4,20},{5,21},{6,22},{7,23},{8,24},{9,... | collective-permute-start | bytes 786440 | tf_op jit(solution)/shard_map/ppermute | solution.py:300
  218.4 1.4 collective-permute-start.5
  219.8 8.8 %collective-permute-done.7.refs_3_ = bf16[8,128,128]{2,1,0:T(8,128)(2,1)S(1)} collective-permute-done((bf16[8,128,128]{2,1,0:T(8,128)(2,1)S(1)}, bf16[8,128,128]{2,1,0:T(8,128)(2,1)S(1)}, u32[]{:S(2)}, u32[]{:S(2)}) %collective-permute-start.7) | collective-permute-done | bytes 262176 | tf_op jit(solution)/shard_map/ppermute | solution.py:300
  228.6 10.9 %collective-permute-done.6.refs_2_ = bf16[8,128,128]{2,1,0:T(8,128)(2,1)S(1)} collective-permute-done((bf16[8,128,128]{2,1,0:T(8,128)(2,1)S(1)}, bf16[8,128,128]{2,1,0:T(8,128)(2,1)S(1)}, u32[]{:S(2)}, u32[]{:S(2)}) %collective-permute-start.6) | collective-permute-done | bytes 262176 | tf_op jit(solution)/shard_map/ppermute | solution.py:300
  239.6 1.6 shard_map.50.refs_1_
  241.2 1.3 all-to-all-done.2.refs_0_
  242.5 1.2 shard_map.51
  (11 shorter events, 3.4 us)
Async XLA Ops:
  4.0 108.2 %all-to-all-start.1 = ((bf16[32,4,128,128]{3,2,1,0:T(8,128)(2,1)}), bf16[32,4,128,128]{3,2,1,0:T(8,128)(2,1)}, u32[]{:S(2)}, u32[]{:S(2)}) async-start(bf16[32,4,128,128]{3,2,1,0:T(8,128)(2,1)} %get-tuple-element.8), calls=%async_computation.1 | async-start | bytes 8388608 | tf_op jit(solution)/shard_map/all_to_all | solution.py:284
  19.8 30.2 %collective-permute-start = (bf16[8,2,128,128]{3,2,1,0:T(8,128)(2,1)S(1)}, bf16[8,2,128,128]{3,2,1,0:T(8,128)(2,1)}, u32[]{:S(2)}, u32[]{:S(2)}) collective-permute-start(bf16[8,2,128,128]{3,2,1,0:T(8,128)(2,1)S(1)} %get-tuple-element.13), channel_id=1, source_target_pairs={{0,8},{1,9},{2,10},{3,11},{4,12},{5,13},{6,14},{7,15},{8,16},{9,17... | collective-permute-start | bytes 1572872 | tf_op jit(solution)/shard_map/ppermute | solution.py:300
  21.6 29.5 %collective-permute-start.2 = (bf16[8,2,128,128]{3,2,1,0:T(8,128)(2,1)S(1)}, bf16[8,2,128,128]{3,2,1,0:T(8,128)(2,1)S(1)}, u32[]{:S(2)}, u32[]{:S(2)}) collective-permute-start(bf16[8,2,128,128]{3,2,1,0:T(8,128)(2,1)S(1)} %get-tuple-element.14), channel_id=1, source_target_pairs={{0,24},{1,25},{2,26},{3,27},{4,28},{5,29},{6,30},{7,31},{8,0},{9,1... | collective-permute-start | bytes 1572872 | tf_op jit(solution)/shard_map/ppermute | solution.py:300
  23.1 47.6 %collective-permute-start.1 = (bf16[8,2,128,128]{3,2,1,0:T(8,128)(2,1)S(1)}, bf16[8,2,128,128]{3,2,1,0:T(8,128)(2,1)S(1)}, u32[]{:S(2)}, u32[]{:S(2)}) collective-permute-start(bf16[8,2,128,128]{3,2,1,0:T(8,128)(2,1)S(1)} %get-tuple-element.15), channel_id=1, source_target_pairs={{0,16},{1,17},{2,18},{3,19},{4,20},{5,21},{6,22},{7,23},{8,24},{9,... | collective-permute-start | bytes 1572872 | tf_op jit(solution)/shard_map/ppermute | solution.py:300
  112.2 31.3 %all-to-all-start.3 = ((bf16[32,128,128]{2,1,0:T(8,128)(2,1)}), bf16[32,128,128]{2,1,0:T(8,128)(2,1)S(1)}, u32[]{:S(2)}, u32[]{:S(2)}) async-start(bf16[32,128,128]{2,1,0:T(8,128)(2,1)} %bitcast.2), calls=%async_computation.3 | async-start | bytes 2097152 | tf_op jit(solution)/shard_map/all_to_all | solution.py:289
  120.7 26.4 %collective-permute-start.4 = (bf16[16,4,128,128]{3,2,1,0:T(8,128)(2,1)}, bf16[16,4,128,128]{3,2,1,0:T(8,128)(2,1)}, u32[]{:S(2)}, u32[]{:S(2)}) collective-permute-start(bf16[16,4,128,128]{3,2,1,0:T(8,128)(2,1)} %get-tuple-element.9), channel_id=1, source_target_pairs={{32,0},{64,32},{96,64},{128,96},{160,128},{192,160},{224,192},{33,... | collective-permute-start | bytes 6291464 | tf_op jit(solution)/shard_map/ppermute | solution.py:333
  122.6 27.7 %collective-permute-start.3 = (bf16[16,4,128,128]{3,2,1,0:T(8,128)(2,1)}, bf16[16,4,128,128]{3,2,1,0:T(8,128)(2,1)}, u32[]{:S(2)}, u32[]{:S(2)}) collective-permute-start(bf16[16,4,128,128]{3,2,1,0:T(8,128)(2,1)} %get-tuple-element.10), channel_id=1, source_target_pairs={{0,32},{32,64},{64,96},{96,128},{128,160},{160,192},{192,224},{1,3... | collective-permute-start | bytes 6291464 | tf_op jit(solution)/shard_map/ppermute | solution.py:332
  125.0 25.3 %copy-start = (s32[2,16,64]{2,1,0:T(8,128)S(1)}, s32[2,16,64]{2,1,0:T(8,128)}, u32[]{:S(2)}) copy-start(s32[2,16,64]{2,1,0:T(8,128)} %get-tuple-element.7.slot_ids) | copy-start | bytes 24580
  143.6 32.7 %all-to-all-start = ((bf16[32,128,128]{2,1,0:T(8,128)(2,1)}), bf16[32,128,128]{2,1,0:T(8,128)(2,1)S(1)}, u32[]{:S(2)}, u32[]{:S(2)}) async-start(bf16[32,128,128]{2,1,0:T(8,128)(2,1)} %bitcast.1), calls=%async_computation | async-start | bytes 2097152 | tf_op jit(solution)/shard_map/all_to_all | solution.py:289
  176.3 32.7 %all-to-all-start.4 = ((bf16[32,128,128]{2,1,0:T(8,128)(2,1)}), bf16[32,128,128]{2,1,0:T(8,128)(2,1)S(1)}, u32[]{:S(2)}, u32[]{:S(2)}) async-start(bf16[32,128,128]{2,1,0:T(8,128)(2,1)} %shard_map.49), calls=%async_computation.4 | async-start | bytes 2097152 | tf_op jit(solution)/shard_map/all_to_all | solution.py:289
  209.0 33.5 %all-to-all-start.2 = ((bf16[32,128,128]{2,1,0:T(8,128)(2,1)}), bf16[32,128,128]{2,1,0:T(8,128)(2,1)S(1)}, u32[]{:S(2)}, u32[]{:S(2)}) async-start(bf16[32,128,128]{2,1,0:T(8,128)(2,1)} %shard_map.48), calls=%async_computation.2 | async-start | bytes 2097152 | tf_op jit(solution)/shard_map/all_to_all | solution.py:284
  213.8 14.8 %collective-permute-start.7 = (bf16[8,128,128]{2,1,0:T(8,128)(2,1)S(1)}, bf16[8,128,128]{2,1,0:T(8,128)(2,1)S(1)}, u32[]{:S(2)}, u32[]{:S(2)}) collective-permute-start(bf16[8,128,128]{2,1,0:T(8,128)(2,1)S(1)} %get-tuple-element.16), channel_id=1, source_target_pairs={{0,8},{1,9},{2,10},{3,11},{4,12},{5,13},{6,14},{7,15},{8,16},{9,17... | collective-permute-start | bytes 786440 | tf_op jit(solution)/shard_map/ppermute | solution.py:300
  215.7 23.9 %collective-permute-start.6 = (bf16[8,128,128]{2,1,0:T(8,128)(2,1)S(1)}, bf16[8,128,128]{2,1,0:T(8,128)(2,1)S(1)}, u32[]{:S(2)}, u32[]{:S(2)}) collective-permute-start(bf16[8,128,128]{2,1,0:T(8,128)(2,1)S(1)} %get-tuple-element.17), channel_id=1, source_target_pairs={{0,16},{1,17},{2,18},{3,19},{4,20},{5,21},{6,22},{7,23},{8,24},{9,... | collective-permute-start | bytes 786440 | tf_op jit(solution)/shard_map/ppermute | solution.py:300
  218.4 21.2 %collective-permute-start.5 = (bf16[8,128,128]{2,1,0:T(8,128)(2,1)S(1)}, bf16[8,128,128]{2,1,0:T(8,128)(2,1)S(1)}, u32[]{:S(2)}, u32[]{:S(2)}) collective-permute-start(bf16[8,128,128]{2,1,0:T(8,128)(2,1)S(1)} %get-tuple-element.18), channel_id=1, source_target_pairs={{0,24},{1,25},{2,26},{3,27},{4,28},{5,29},{6,30},{7,31},{8,0},{9,1... | collective-permute-start | bytes 786440 | tf_op jit(solution)/shard_map/ppermute | solution.py:300
